TPU v7x, 32 devices: a whole 2x2x4 slice. The times are simulated.
32 devices in a mesh: ctx: 4 (over y, core), tp: 4 (over z), fsdp: 2 (over x).
Axes of the slice: x: 2, y: 2, z: 4, core: 2. Of those that a mesh axis runs over, the one named last changes fastest.
Arguments:
- tokens: bfloat16 [2, 512, 2048], P('fsdp', 'ctx'), may hold values from -6 to 6
- out_grad: bfloat16 [2, 512, 2048], P('fsdp', 'ctx'), may hold values from -6 to 6
- segment_start: int32 [2, 512], P('fsdp'), may hold values from 0 to 511, as said below
- norm_attn: bfloat16 [2048], P('fsdp'), may hold values from 0.5 to 1.5
- norm_mlp: bfloat16 [2048], P('fsdp'), may hold values from 0.5 to 1.5
- w_query: bfloat16 [2048, 2048], P('fsdp', 'tp'), may hold values from -0.125 to 0.125
- w_key: bfloat16 [2048, 2048], P('fsdp', 'tp'), may hold values from -0.125 to 0.125
- w_value: bfloat16 [2048, 2048], P('fsdp', 'tp'), may hold values from -0.125 to 0.125
- w_out: bfloat16 [2048, 2048], P('tp', 'fsdp'), may hold values from -1 to 1
- w_gate: bfloat16 [2048, 8192], P('fsdp', 'tp'), may hold values from -0.125 to 0.125
- w_up: bfloat16 [2048, 8192], P('fsdp', 'tp'), may hold values from -0.125 to 0.125
- w_down: bfloat16 [8192, 2048], P('tp', 'fsdp'), may hold values from -0.0625 to 0.0625
- mom_query: float32 [2048, 2048], P('fsdp', 'tp'), may hold values from -160 to 160
- mom_key: float32 [2048, 2048], P('fsdp', 'tp'), may hold values from -160 to 160
- mom_value: float32 [2048, 2048], P('fsdp', 'tp'), may hold values from -160 to 160
- mom_out: float32 [2048, 2048], P('tp', 'fsdp'), may hold values from -160 to 160
- mom_gate: float32 [2048, 8192], P('fsdp', 'tp'), may hold values from -160 to 160
- mom_up: float32 [2048, 8192], P('fsdp', 'tp'), may hold values from -160 to 160
- mom_down: float32 [8192, 2048], P('tp', 'fsdp'), may hold values from -160 to 160
Outputs:
- output: bfloat16 [2, 512, 2048], P('fsdp', 'ctx')
- input_grad: float32 [2, 512, 2048], P('fsdp', 'ctx')
- grad_norm_attn: float32 [2048], P('fsdp')
- grad_norm_mlp: float32 [2048], P('fsdp')
- grad_query: float32 [2048, 2048], P('fsdp', 'tp')
- grad_key: float32 [2048, 2048], P('fsdp', 'tp')
- grad_value: float32 [2048, 2048], P('fsdp', 'tp')
- grad_out: float32 [2048, 2048], P('tp', 'fsdp')
- grad_gate: float32 [2048, 8192], P('fsdp', 'tp')
- grad_up: float32 [2048, 8192], P('fsdp', 'tp')
- grad_down: float32 [8192, 2048], P('tp', 'fsdp')
- new_mom_query: float32 [2048, 2048], P('fsdp', 'tp')
- new_mom_key: float32 [2048, 2048], P('fsdp', 'tp')
- new_mom_value: float32 [2048, 2048], P('fsdp', 'tp')
- new_mom_out: float32 [2048, 2048], P('tp', 'fsdp')
- new_mom_gate: float32 [2048, 8192], P('fsdp', 'tp')
- new_mom_up: float32 [2048, 8192], P('fsdp', 'tp')
- new_mom_down: float32 [8192, 2048], P('tp', 'fsdp')
- new_query: float32 [2048, 2048], P('fsdp', 'tp')
- new_key: float32 [2048, 2048], P('fsdp', 'tp')
- new_value: float32 [2048, 2048], P('fsdp', 'tp')
- new_out: float32 [2048, 2048], P('tp', 'fsdp')
- new_gate: float32 [2048, 8192], P('fsdp', 'tp')
- new_up: float32 [2048, 8192], P('fsdp', 'tp')
- new_down: float32 [8192, 2048], P('tp', 'fsdp')
Inputs may be any that keep to these rules, and one draw needn't show every extreme that they name: segment_start[g, i] is the first index in group g of the sequence that holds token i; a group's sequences are consecutive runs of 1 to 256 tokens, each group has one of exactly 256, and the last token of each group is a sequence of its own.
All inputs are finite; a program needn't handle non-finite values.
Results may differ from a plain program's by a relative error of at most 0.013.
Values may be sent and summed in bfloat16 or wider, within the bound.
No kernel may reach another device: no remote copies, remote signals or barrier semaphores. Data moves between devices by JAX's collectives and lax.ppermute only.
A program may use at most 448 MiB of HBM per device.

v0:
```python
import math

import jax
import jax.numpy as jnp
from jax import lax
from jax.sharding import PartitionSpec as P

HEAD_DIM = 64
NS_STEPS = 5
UNITS = 16


EPS = 1e-05
THETA = 130000.0
MOMENTUM = 0.95
COEF_A = 3.4445
COEF_B = -4.775
COEF_C = 2.0315
RATE = 0.5
HIGH = lax.Precision.HIGHEST


def as_sent(x):

    def short(part):
        return part.astype(jnp.bfloat16) if part.dtype == jnp.float32 else part

    return jax.tree.map(short, x)


def product(left, right):
    return jnp.dot(left, right, preferred_element_type=jnp.float32)


def product_left(left, right):
    return lax.dot_general(
        left, right, (((0,), (0,)), ((), ())), preferred_element_type=jnp.float32
    )


def product_right(left, right):
    return lax.dot_general(
        left, right, (((1,), (1,)), ((), ())), preferred_element_type=jnp.float32
    )


def rope_tables(position, head_size):
    half = head_size // 2
    freq = THETA ** (-(jnp.arange(half, dtype=jnp.float32) * 2.0 / head_size))
    angle = position[:, None] * freq[None, :]
    cosine = jnp.concatenate([jnp.cos(angle), jnp.cos(angle)], axis=1)
    sine = jnp.concatenate([jnp.sin(angle), jnp.sin(angle)], axis=1)
    return (cosine, sine)


def rotate(values, cosine, sine):
    half = values.shape[-1] // 2
    turned = jnp.concatenate([-values[..., half:], values[..., :half]], axis=-1)
    return values * cosine[:, None, :] + turned * sine[:, None, :]


def unrotate(grads, cosine, sine):
    half = grads.shape[-1] // 2
    scaled = grads * sine[:, None, :]
    back = jnp.concatenate([scaled[..., half:], -scaled[..., :half]], axis=-1)
    return grads * cosine[:, None, :] + back


def regroup(array, dim, fsdp_size, ctx_size):
    moved = jnp.moveaxis(array, dim, 0)
    shape = moved.shape
    parts = moved.reshape((fsdp_size, ctx_size, shape[0] // (fsdp_size * ctx_size)) + shape[1:])
    parts = jnp.swapaxes(parts, 0, 1).reshape(shape)
    return jnp.moveaxis(parts, 0, dim)


def orthogonal(block):
    shape = block.shape
    units = block.reshape((-1,) + shape[2:])
    norms = jnp.sqrt(jnp.sum(units * units, axis=(1, 2), keepdims=True)) + 1e-07
    state = units / norms
    for step in range(NS_STEPS):
        gram = jnp.einsum(
            "ubd,ucd->ubc", state, state, precision=HIGH, preferred_element_type=jnp.float32
        )
        square = jnp.einsum(
            "ubc,uce->ube", gram, gram, precision=HIGH, preferred_element_type=jnp.float32
        )
        mixed = COEF_B * gram + COEF_C * square
        state = COEF_A * state + jnp.einsum(
            "ubc,ucd->ubd", mixed, state, precision=HIGH, preferred_element_type=jnp.float32
        )
    return state.reshape(shape)


def body(
    tokens,
    out_grad,
    segment_start,
    norm_attn,
    norm_mlp,
    w_query,
    w_key,
    w_value,
    w_out,
    w_gate,
    w_up,
    w_down,
    mom_query,
    mom_key,
    mom_value,
    mom_out,
    mom_gate,
    mom_up,
    mom_down,
):
    rows = tokens.shape[1]
    head_size = HEAD_DIM
    scale = 1.0 / math.sqrt(head_size)
    inputs = tokens[0].astype(jnp.float32)
    starts = segment_start[0]
    group_rows = starts.shape[0]
    offset = lax.axis_index("ctx") * rows
    key_index = jnp.arange(group_rows, dtype=jnp.int32)
    query_index = offset + jnp.arange(rows, dtype=jnp.int32)
    query_start = lax.dynamic_slice_in_dim(starts, offset, rows)
    cosine, sine = rope_tables((query_index - query_start).astype(jnp.float32), head_size)
    allowed = (starts[None, :] == query_start[:, None]) & (
        key_index[None, :] <= query_index[:, None]
    )
    wquery, wkey, wvalue, wout, gain_attn = (
        lax.all_gather(w_query, "fsdp", axis=0, tiled=True),
        lax.all_gather(w_key, "fsdp", axis=0, tiled=True),
        lax.all_gather(w_value, "fsdp", axis=0, tiled=True),
        lax.all_gather(w_out, "fsdp", axis=1, tiled=True),
        lax.all_gather(norm_attn, "fsdp", axis=0, tiled=True),
    )
    gain_one = gain_attn.astype(jnp.float32)
    inv_one = lax.rsqrt(jnp.mean(inputs * inputs, axis=1, keepdims=True) + EPS)
    normed = (inputs * inv_one * gain_one).astype(jnp.bfloat16)
    local_width = wquery.shape[1]
    heads = local_width // head_size
    query = rotate(product(normed, wquery).reshape(rows, heads, head_size), cosine, sine).astype(
        jnp.bfloat16
    )
    keys_own = rotate(product(normed, wkey).reshape(rows, heads, head_size), cosine, sine).astype(
        jnp.bfloat16
    )
    values_own = product(normed, wvalue).astype(jnp.bfloat16)
    keys_all, values_all = (
        lax.all_gather(keys_own.reshape(rows, local_width), "ctx", axis=0, tiled=True),
        lax.all_gather(values_own, "ctx", axis=0, tiled=True),
    )
    query_heads = jnp.transpose(query, (1, 0, 2))
    key_heads = jnp.transpose(keys_all.reshape(group_rows, heads, head_size), (1, 0, 2))
    value_heads = jnp.transpose(values_all.reshape(group_rows, heads, head_size), (1, 0, 2))

    def head_forward(pack):
        query_one, key_one, value_one = pack
        scores = jnp.where(allowed, product_right(query_one, key_one) * scale, -1e30)
        top = jnp.max(scores, axis=1, keepdims=True)
        total = jnp.sum(jnp.exp(scores - top), axis=1, keepdims=True)
        log_total = top + jnp.log(total)
        weights = jnp.exp(scores - log_total).astype(jnp.bfloat16)
        return (product(weights, value_one), log_total)

    attn_heads, log_totals = lax.map(head_forward, (query_heads, key_heads, value_heads))
    attn = jnp.transpose(attn_heads, (1, 0, 2)).reshape(rows, local_width).astype(jnp.bfloat16)
    middle = inputs + lax.psum(product(attn, wout), "tp")
    wgate, wup, wdown, gain_mlp = (
        lax.all_gather(w_gate, "fsdp", axis=0, tiled=True),
        lax.all_gather(w_up, "fsdp", axis=0, tiled=True),
        lax.all_gather(w_down, "fsdp", axis=1, tiled=True),
        lax.all_gather(norm_mlp, "fsdp", axis=0, tiled=True),
    )
    gain_two = gain_mlp.astype(jnp.float32)
    inv_two = lax.rsqrt(jnp.mean(middle * middle, axis=1, keepdims=True) + EPS)
    normed_two = (middle * inv_two * gain_two).astype(jnp.bfloat16)
    gate = product(normed_two, wgate)
    upper = product(normed_two, wup)
    sigma = jax.nn.sigmoid(gate)
    hidden = (gate * sigma * upper).astype(jnp.bfloat16)
    result = middle + lax.psum(product(hidden, wdown).astype(jnp.bfloat16), "tp").astype(
        jnp.float32
    )
    grad_in = out_grad[0].astype(jnp.float32)
    grad_low = grad_in.astype(jnp.bfloat16)
    local_down = product_left(hidden, grad_low)
    grad_hidden = product_right(grad_low, wdown)
    grad_gate_pre = (grad_hidden * upper * sigma * (1.0 + gate * (1.0 - sigma))).astype(
        jnp.bfloat16
    )
    grad_up_pre = (grad_hidden * gate * sigma).astype(jnp.bfloat16)
    local_gate = product_left(normed_two, grad_gate_pre)
    local_up = product_left(normed_two, grad_up_pre)
    grad_normed_two = lax.psum(
        product_right(grad_gate_pre, wgate) + product_right(grad_up_pre, wup), "tp"
    )
    scaled_two = middle * inv_two
    local_gain_two = jnp.sum(grad_normed_two * scaled_two, axis=0)
    weighted_two = grad_normed_two * gain_two
    grad_middle = grad_in + inv_two * (
        weighted_two - scaled_two * jnp.mean(weighted_two * scaled_two, axis=1, keepdims=True)
    )
    middle_low = grad_middle.astype(jnp.bfloat16)
    local_out = product_left(attn, middle_low)
    grad_attn = product_right(middle_low, wout).astype(jnp.bfloat16)
    grad_attn_heads = jnp.transpose(grad_attn.reshape(rows, heads, head_size), (1, 0, 2))

    def head_backward(pack):
        query_one, key_one, value_one, grad_one, log_total = pack
        scores = jnp.where(allowed, product_right(query_one, key_one) * scale, -1e30)
        prob = jnp.exp(scores - log_total)
        grad_prob = product_right(grad_one, value_one)
        delta = jnp.sum(prob * grad_prob, axis=1, keepdims=True)
        grad_score = (prob * (grad_prob - delta)).astype(jnp.bfloat16)
        return (product(grad_score, key_one) * scale, grad_score, prob.astype(jnp.bfloat16))

    grad_query_heads, grad_scores, probs = lax.map(
        head_backward, (query_heads, key_heads, value_heads, grad_attn_heads, log_totals)
    )
    grad_query_pre = (
        unrotate(jnp.transpose(grad_query_heads, (1, 0, 2)), cosine, sine)
        .reshape(rows, local_width)
        .astype(jnp.bfloat16)
    )
    grad_keys = (
        jnp.einsum("hqk,hqd->khd", grad_scores, query_heads, preferred_element_type=jnp.float32)
        * scale
    )
    grad_values = jnp.einsum(
        "hqk,hqd->khd", probs, grad_attn_heads, preferred_element_type=jnp.float32
    )
    kv_total = lax.psum_scatter(
        jnp.concatenate(
            [
                grad_keys.reshape(rows * lax.axis_size("ctx"), local_width),
                grad_values.reshape(rows * lax.axis_size("ctx"), local_width),
            ],
            axis=1,
        ),
        "ctx",
        scatter_dimension=0,
        tiled=True,
    )
    grad_key_pre = (
        unrotate(kv_total[:, :local_width].reshape(rows, heads, head_size), cosine, sine)
        .reshape(rows, local_width)
        .astype(jnp.bfloat16)
    )
    grad_value_pre = kv_total[:, local_width:].astype(jnp.bfloat16)
    local_query = product_left(normed, grad_query_pre)
    local_key = product_left(normed, grad_key_pre)
    local_value = product_left(normed, grad_value_pre)
    grad_normed = lax.psum(
        product_right(grad_query_pre, wquery)
        + product_right(grad_key_pre, wkey)
        + product_right(grad_value_pre, wvalue),
        "tp",
    )
    scaled_one = inputs * inv_one
    local_gain_one = jnp.sum(grad_normed * scaled_one, axis=0)
    weighted_one = grad_normed * gain_one
    input_grad = grad_middle + inv_one * (
        weighted_one - scaled_one * jnp.mean(weighted_one * scaled_one, axis=1, keepdims=True)
    )
    ctx_size = lax.axis_size("ctx")
    fsdp_size = lax.axis_size("fsdp")
    pieces = (
        lax.psum_scatter(
            regroup(local_query, 0, fsdp_size, ctx_size),
            ("ctx", "fsdp"),
            scatter_dimension=0,
            tiled=True,
        ),
        lax.psum_scatter(
            regroup(local_key, 0, fsdp_size, ctx_size),
            ("ctx", "fsdp"),
            scatter_dimension=0,
            tiled=True,
        ),
        lax.psum_scatter(
            regroup(local_value, 0, fsdp_size, ctx_size),
            ("ctx", "fsdp"),
            scatter_dimension=0,
            tiled=True,
        ),
        lax.psum_scatter(
            regroup(local_out, 1, fsdp_size, ctx_size),
            ("ctx", "fsdp"),
            scatter_dimension=1,
            tiled=True,
        ),
        lax.psum_scatter(
            regroup(local_gate, 0, fsdp_size, ctx_size),
            ("ctx", "fsdp"),
            scatter_dimension=0,
            tiled=True,
        ),
        lax.psum_scatter(
            regroup(local_up, 0, fsdp_size, ctx_size),
            ("ctx", "fsdp"),
            scatter_dimension=0,
            tiled=True,
        ),
        lax.psum_scatter(
            regroup(local_down, 1, fsdp_size, ctx_size),
            ("ctx", "fsdp"),
            scatter_dimension=1,
            tiled=True,
        ),
        lax.psum_scatter(
            regroup(local_gain_one, 0, fsdp_size, ctx_size),
            ("ctx", "fsdp"),
            scatter_dimension=0,
            tiled=True,
        ),
        lax.psum_scatter(
            regroup(local_gain_two, 0, fsdp_size, ctx_size),
            ("ctx", "fsdp"),
            scatter_dimension=0,
            tiled=True,
        ),
    )
    shards = (
        lax.all_gather(pieces[0], "ctx", axis=0, tiled=True),
        lax.all_gather(pieces[1], "ctx", axis=0, tiled=True),
        lax.all_gather(pieces[2], "ctx", axis=0, tiled=True),
        lax.all_gather(pieces[3], "ctx", axis=1, tiled=True),
        lax.all_gather(pieces[4], "ctx", axis=0, tiled=True),
        lax.all_gather(pieces[5], "ctx", axis=0, tiled=True),
        lax.all_gather(pieces[6], "ctx", axis=1, tiled=True),
        lax.all_gather(pieces[7], "ctx", axis=0, tiled=True),
        lax.all_gather(pieces[8], "ctx", axis=0, tiled=True),
    )
    (
        grad_query,
        grad_key,
        grad_value,
        grad_out,
        grad_gate,
        grad_up,
        grad_down,
        grad_gain_one,
        grad_gain_two,
    ) = shards
    moments = (mom_query, mom_key, mom_value, mom_out, mom_gate, mom_up, mom_down)
    matrix_grads = (grad_query, grad_key, grad_value, grad_out, grad_gate, grad_up, grad_down)
    new_moms = tuple((MOMENTUM * m + g for m, g in zip(moments, matrix_grads)))
    looks = tuple((g + MOMENTUM * m for m, g in zip(new_moms, matrix_grads)))
    block_rows = w_query.shape[1]
    shard_rows = w_query.shape[0]
    mult = w_gate.shape[1] // block_rows

    def wide_columns(matrix):
        return jnp.transpose(matrix.reshape(shard_rows, mult, block_rows), (1, 2, 0))

    stacked = jnp.concatenate(
        [
            looks[0].T[None],
            looks[1].T[None],
            looks[2].T[None],
            looks[3][None],
            wide_columns(looks[4]),
            wide_columns(looks[5]),
            looks[6].reshape(mult, block_rows, shard_rows),
        ],
        axis=0,
    )
    fsdp_size = lax.axis_size("fsdp")
    per_owner = UNITS // fsdp_size
    arranged = jnp.swapaxes(stacked.reshape(per_owner, fsdp_size, block_rows, shard_rows), 0, 1)
    ortho = orthogonal(
        lax.all_to_all(
            arranged.astype(jnp.bfloat16), "fsdp", split_axis=0, concat_axis=3, tiled=True
        ).astype(arranged.dtype)
    )
    returned = lax.all_to_all(
        as_sent(ortho), "fsdp", split_axis=3, concat_axis=0, tiled=True
    ).astype(ortho.dtype)
    units = jnp.swapaxes(returned, 0, 1).reshape(UNITS, block_rows, shard_rows)

    def back_columns(part):
        return jnp.transpose(part, (2, 0, 1)).reshape(shard_rows, mult * block_rows)

    new_query = w_query.astype(jnp.float32) - RATE * units[0].T
    new_key = w_key.astype(jnp.float32) - RATE * units[1].T
    new_value = w_value.astype(jnp.float32) - RATE * units[2].T
    new_out = w_out.astype(jnp.float32) - RATE * units[3]
    new_gate = w_gate.astype(jnp.float32) - RATE * back_columns(units[4 : 4 + mult])
    new_up = w_up.astype(jnp.float32) - RATE * back_columns(units[4 + mult : 4 + 2 * mult])
    new_down = w_down.astype(jnp.float32) - RATE * units[4 + 2 * mult :].reshape(
        mult * block_rows, shard_rows
    )
    return (
        result.astype(jnp.bfloat16)[None],
        input_grad[None],
        grad_gain_one,
        grad_gain_two,
        grad_query,
        grad_key,
        grad_value,
        grad_out,
        grad_gate,
        grad_up,
        grad_down,
        new_moms[0],
        new_moms[1],
        new_moms[2],
        new_moms[3],
        new_moms[4],
        new_moms[5],
        new_moms[6],
        new_query,
        new_key,
        new_value,
        new_out,
        new_gate,
        new_up,
        new_down,
    )


def solution(mesh):
    in_specs = (
        P("fsdp", "ctx", None),
        P("fsdp", "ctx", None),
        P("fsdp", None),
        P("fsdp"),
        P("fsdp"),
        P("fsdp", "tp"),
        P("fsdp", "tp"),
        P("fsdp", "tp"),
        P("tp", "fsdp"),
        P("fsdp", "tp"),
        P("fsdp", "tp"),
        P("tp", "fsdp"),
        P("fsdp", "tp"),
        P("fsdp", "tp"),
        P("fsdp", "tp"),
        P("tp", "fsdp"),
        P("fsdp", "tp"),
        P("fsdp", "tp"),
        P("tp", "fsdp"),
    )
    out_specs = (
        P("fsdp", "ctx", None),
        P("fsdp", "ctx", None),
        P("fsdp"),
        P("fsdp"),
        P("fsdp", "tp"),
        P("fsdp", "tp"),
        P("fsdp", "tp"),
        P("tp", "fsdp"),
        P("fsdp", "tp"),
        P("fsdp", "tp"),
        P("tp", "fsdp"),
        P("fsdp", "tp"),
        P("fsdp", "tp"),
        P("fsdp", "tp"),
        P("tp", "fsdp"),
        P("fsdp", "tp"),
        P("fsdp", "tp"),
        P("tp", "fsdp"),
        P("fsdp", "tp"),
        P("fsdp", "tp"),
        P("fsdp", "tp"),
        P("tp", "fsdp"),
        P("fsdp", "tp"),
        P("fsdp", "tp"),
        P("tp", "fsdp"),
    )
    return jax.shard_map(body, mesh=mesh, in_specs=in_specs, out_specs=out_specs, check_vma=False)
```

profile of v0, /device:TPU:0, one launch (start us, length us, event | category | flops | bytes accessed | tf_op | source)
XLA Modules:
  0.0 3150.5 jit_solution(15104620711360597847)
XLA Ops:
  18.2 27.3 all-gather.19.cloned.1.call-done
  48.4 31.8 %all-gather.17.cloned.1.call-done = bf16[2048,512]{1,0:T(8,128)(2,1)} async-done(((bf16[1024,512]{1,0:T(8,128)(2,1)}), bf16[2048,512]{1,0:T(8,128)(2,1)}) %all-gather.17.cloned.1.call-update) | async-done | bytes 2097168 | tf_op jit(solution)/shard_map/all_gather | solution.py:132
  95.9 19.0 all-gather.21.cloned.1.call-done
  124.8 16.5 while.30
  159.2 45.3 %all-reduce.8.cloned.1.call-done = f32[128,2048]{1,0:T(8,128)} async-done(((f32[128,2048]{1,0:T(8,128)}), f32[128,2048]{1,0:T(8,128)}) %all-reduce.8.cloned.1.call-update) | async-done | bytes 1048592 | tf_op jit(solution)/shard_map/psum | solution.py:169
  206.1 103.3 %all-gather.25.cloned.1.call-done = bf16[2048,2048]{1,0:T(8,128)(2,1)} async-done(((bf16[1024,2048]{1,0:T(8,128)(2,1)}), bf16[2048,2048]{1,0:T(8,128)(2,1)}) %all-gather.25.cloned.1.call-update) | async-done | bytes 8388624 | tf_op jit(solution)/shard_map/all_gather | solution.py:171
  315.0 100.0 %all-gather.27.cloned.1.call-done = bf16[2048,2048]{1,0:T(8,128)(2,1)} async-done(((bf16[1024,2048]{1,0:T(8,128)(2,1)}), bf16[2048,2048]{1,0:T(8,128)(2,1)}) %all-gather.27.cloned.1.call-update) | async-done | bytes 8388624 | tf_op jit(solution)/shard_map/all_gather | solution.py:172
  420.6 100.0 %all-gather.29.cloned.1.call-done = bf16[2048,2048]{1,0:T(8,128)(2,1)} async-done(((bf16[2048,1024]{1,0:T(8,128)(2,1)}), bf16[2048,2048]{1,0:T(8,128)(2,1)}) %all-gather.29.cloned.1.call-update) | async-done | bytes 8388624 | tf_op jit(solution)/shard_map/all_gather | solution.py:173
  542.4 45.9 %all-reduce.12.cloned.1.call-done = f32[128,2048]{1,0:T(8,128)} async-done(((f32[128,2048]{1,0:T(8,128)}), f32[128,2048]{1,0:T(8,128)}) %all-reduce.12.cloned.1.call-update) | async-done | bytes 1048592 | tf_op jit(solution)/shard_map/psum | solution.py:196
  590.6 38.3 %all-reduce.10.cloned.1.call-done = bf16[128,2048]{1,0:T(8,128)(2,1)} async-done(((bf16[128,2048]{1,0:T(8,128)(2,1)}), bf16[128,2048]{1,0:T(8,128)(2,1)}) %all-reduce.10.cloned.1.call-update) | async-done | bytes 524304 | tf_op jit(solution)/shard_map/psum | solution.py:183
  635.2 36.9 %while.31 = (s32[]{:T(128)}, f32[8,128,64]{1,2,0:T(8,128)}, bf16[8,128,512]{2,1,0:T(8,128)(2,1)}, bf16[8,128,512]{2,1,0:T(8,128)(2,1)}, bf16[8,128,64]{2,1,0:T(8...) while((s32[]{:T(128)}, f32[8,128,64]{1,2,0:T(8,128)}, ...), condition=%wide.region_12.13_spmd.clone.clone, body=%wide.region_10.12_spmd.clone.sunk.clone | while | flops 25960320 | bytes 2318981 | solution.py:219
  689.8 22.8 reduce-scatter.9.cloned.1.call-done
  731.2 47.0 %all-reduce.14.cloned.1.call-done = f32[128,2048]{1,0:T(8,128)} async-done(((f32[128,2048]{1,0:T(8,128)}), f32[128,2048]{1,0:T(8,128)}) %all-reduce.14.cloned.1.call-update) | async-done | bytes 1048592 | tf_op jit(solution)/shard_map/psum | solution.py:255
  819.8 25.5 copy.315
  845.4 22.1 reshape.324
  868.1 20.4 reduce-scatter.11.cloned.1.call-done
  888.5 55.0 %reduce-scatter.13.cloned.1.call-done = f32[256,512]{1,0:T(8,128)} async-done(((f32[2048,512]{1,0:T(8,128)}), f32[256,512]{1,0:T(8,128)}) %reduce-scatter.13.cloned.1.call-update) | async-done | bytes 524304 | tf_op jit(solution)/shard_map/reduce_scatter | solution.py:276
  943.6 55.5 %reduce-scatter.15.cloned.1.call-done = f32[256,512]{1,0:T(8,128)} async-done(((f32[2048,512]{1,0:T(8,128)}), f32[256,512]{1,0:T(8,128)}) %reduce-scatter.15.cloned.1.call-update) | async-done | bytes 524304 | tf_op jit(solution)/shard_map/reduce_scatter | solution.py:282
  999.2 119.3 %reduce-scatter.19.cloned.1.call-done = f32[256,2048]{1,0:T(8,128)} async-done(((f32[2048,2048]{1,0:T(8,128)}), f32[256,2048]{1,0:T(8,128)}) %reduce-scatter.19.cloned.1.call-update) | async-done | bytes 2097168 | tf_op jit(solution)/shard_map/reduce_scatter | solution.py:294
  1118.6 119.3 %reduce-scatter.21.cloned.1.call-done = f32[256,2048]{1,0:T(8,128)} async-done(((f32[2048,2048]{1,0:T(8,128)}), f32[256,2048]{1,0:T(8,128)}) %reduce-scatter.21.cloned.1.call-update) | async-done | bytes 2097168 | tf_op jit(solution)/shard_map/reduce_scatter | solution.py:300
  1238.1 119.3 %reduce-scatter.23.cloned.1.call-done = f32[2048,256]{1,0:T(8,128)} async-done(((f32[2048,2048]{1,0:T(8,128)}), f32[2048,256]{1,0:T(8,128)}) %reduce-scatter.23.cloned.1.call-update) | async-done | bytes 2097168 | tf_op jit(solution)/shard_map/reduce_scatter | solution.py:306
  1359.4 22.1 all-gather.37.cloned.1.call-done
  1385.5 20.2 all-gather.31.cloned.1.call-done
  1410.3 19.6 all-gather.33.cloned.1.call-done
  1435.3 18.8 all-gather.35.cloned.1.call-done
  1466.4 47.4 %all-gather.39.cloned.1.call-done = f32[1024,2048]{1,0:T(8,128)} async-done(((f32[256,2048]{1,0:T(8,128)}), f32[1024,2048]{1,0:T(8,128)}) %all-gather.39.cloned.1.call-update) | async-done | bytes 8388624 | tf_op jit(solution)/shard_map/all_gather | solution.py:330
  1513.8 10.2 add_convert_fusion.3
  1530.5 43.1 %all-gather.41.cloned.1.call-done = f32[1024,2048]{1,0:T(8,128)} async-done(((f32[256,2048]{1,0:T(8,128)}), f32[1024,2048]{1,0:T(8,128)}) %all-gather.41.cloned.1.call-update) | async-done | bytes 8388624 | tf_op jit(solution)/shard_map/all_gather | solution.py:331
  1573.7 10.2 add_convert_fusion.2
  1597.8 35.6 %all-gather.43.cloned.1.call-done = f32[2048,1024]{1,0:T(8,128)} async-done(((f32[2048,256]{1,0:T(8,128)}), f32[2048,1024]{1,0:T(8,128)}) %all-gather.43.cloned.1.call-update) | async-done | bytes 8388624 | tf_op jit(solution)/shard_map/all_gather | solution.py:332
  1633.4 9.5 add_convert_fusion.1
  1653.5 186.9 %all_to_all.8 = bf16[2,8,512,1024]{3,2,1,0:T(8,128)(2,1)S(1)} all-to-all(bf16[2,8,512,1024]{3,2,1,0:T(8,128)(2,1)S(1)} %copy.324), channel_id=1, replica_groups=mesh['ctx'=4,'tp'=4,'fsdp'=2] {'fsdp'}, dimensions={0} | all-to-all | bytes 33554432 | tf_op jit(solution)/shard_map/all_to_all | solution.py:374
  1846.2 11.3 convert_bitcast_fusion
  1857.5 55.1 %copy.325 = f32[1,8,512,2,1024]{4,3,2,1,0:T(2,128)} copy(f32[1,8,512,2,1024]{4,2,1,3,0:T(8,128)} %convert_bitcast_fusion) | data formatting | bytes 67108864 | tf_op jit(solution)/shard_map/convert_element_type | solution.py:376
  1912.7 42.8 %reshape.330 = f32[8,512,2048]{2,1,0:T(8,128)} reshape(f32[1,8,512,2,1024]{4,3,2,1,0:T(2,128)} %copy.325) | data formatting | bytes 67108864 | tf_op jit(solution)/shard_map/convert_element_type | solution.py:376
  1955.5 10.9 fusion.37
  1966.4 62.6 %fusion.54 = f32[8,512,512]{2,1,0:T(8,128)S(1)} fusion(f32[8,512,2048]{2,1,0:T(8,128)} %reshape.330, f32[8]{0:T(128)S(1)} %sqrt_add_fusion), kind=kOutput, calls=%fused_computation.88 | convolution fusion | flops 51547996160 | bytes 41943072 | tf_op jit(solution)/shard_map/ubd,ucd->ubc/dot_general | solution.py:83
  2032.4 16.4 fusion.130
  2048.8 11.3 fusion.208
  2060.1 66.6 %multiply_add_fusion.3 = f32[8,512,2048]{2,1,0:T(8,128)} fusion(f32[8,512,2048]{2,1,0:T(8,128)} %reshape.330, f32[8]{0:T(128)S(1)} %sqrt_add_fusion, f32[8,512,512]{2,1,0:T(8,128)} %fusion.208), kind=kOutput, calls=%fused_computation.57 | convolution fusion | flops 51573161984 | bytes 75497504 | tf_op jit(solution)/shard_map/ubc,ucd->ubd/dot_general | solution.py:90
  2126.7 61.3 %fusion.131 = f32[8,512,512]{2,1,0:T(8,128)S(1)} fusion(f32[8,512,2048]{2,1,0:T(8,128)} %multiply_add_fusion.3), kind=kOutput, calls=%fused_computation.233 | convolution fusion | flops 51539607552 | bytes 41943040 | tf_op jit(solution)/shard_map/ubd,ucd->ubc/dot_general | solution.py:83
  2191.4 16.4 fusion.132
  2207.8 64.0 %multiply_add_fusion.2 = f32[8,512,2048]{2,1,0:T(8,128)} fusion(f32[8,512,2048]{2,1,0:T(8,128)} %multiply_add_fusion.3, f32[8,512,512]{2,1,0:T(8,128)} %fusion.132, f32[8,512,512]{2,1,0:T(8,128)} %copy-done.1), kind=kOutput, calls=%fused_computation.56 | convolution fusion | flops 51562676224 | bytes 83886080 | tf_op jit(solution)/shard_map/ubc,ucd->ubd/dot_general | solution.py:90
  2271.8 61.4 %fusion.133 = f32[8,512,512]{2,1,0:T(8,128)S(1)} fusion(f32[8,512,2048]{2,1,0:T(8,128)} %multiply_add_fusion.2), kind=kOutput, calls=%fused_computation.235 | convolution fusion | flops 51539607552 | bytes 41943040 | tf_op jit(solution)/shard_map/ubd,ucd->ubc/dot_general | solution.py:83
  2336.5 16.7 fusion.134
  2353.2 63.9 %multiply_add_fusion.1 = f32[8,512,2048]{2,1,0:T(8,128)} fusion(f32[8,512,2048]{2,1,0:T(8,128)} %multiply_add_fusion.2, f32[8,512,512]{2,1,0:T(8,128)} %fusion.134, f32[8,512,512]{2,1,0:T(8,128)} %copy-done.2), kind=kOutput, calls=%fused_computation.55 | convolution fusion | flops 51562676224 | bytes 83886080 | tf_op jit(solution)/shard_map/ubc,ucd->ubd/dot_general | solution.py:90
  2417.1 61.4 %fusion.135 = f32[8,512,512]{2,1,0:T(8,128)S(1)} fusion(f32[8,512,2048]{2,1,0:T(8,128)} %multiply_add_fusion.1), kind=kOutput, calls=%fused_computation.237 | convolution fusion | flops 51539607552 | bytes 41943040 | tf_op jit(solution)/shard_map/ubd,ucd->ubc/dot_general | solution.py:83
  2481.8 16.4 fusion.136
  2498.2 64.0 %multiply_add_fusion = f32[8,512,2048]{2,1,0:T(8,128)} fusion(f32[8,512,2048]{2,1,0:T(8,128)} %multiply_add_fusion.1, f32[8,512,512]{2,1,0:T(8,128)} %fusion.136, f32[8,512,512]{2,1,0:T(8,128)} %copy-done.3), kind=kOutput, calls=%fused_computation.54 | convolution fusion | flops 51562676224 | bytes 83886080 | tf_op jit(solution)/shard_map/ubc,ucd->ubd/dot_general | solution.py:90
  2562.3 61.6 %fusion.137 = f32[8,512,512]{2,1,0:T(8,128)S(1)} fusion(f32[8,512,2048]{2,1,0:T(8,128)} %multiply_add_fusion), kind=kOutput, calls=%fused_computation.239 | convolution fusion | flops 51539607552 | bytes 41943040 | tf_op jit(solution)/shard_map/ubd,ucd->ubc/dot_general | solution.py:83
  2627.3 16.3 fusion.138
  2643.6 64.0 %fusion.38 = bf16[1,8,512,2048]{3,2,1,0:T(8,128)(2,1)} fusion(f32[8,512,2048]{2,1,0:T(8,128)} %multiply_add_fusion, f32[8,512,512]{2,1,0:T(8,128)} %fusion.138, f32[8,512,512]{2,1,0:T(8,128)} %copy-done.4), kind=kOutput, calls=%fused_computation.59 | convolution fusion | flops 51571064832 | bytes 67108864 | tf_op jit(solution)/shard_map/ubc,ucd->ubd/dot_general | solution.py:90
  2707.6 23.9 copy.326
  2731.5 10.1 all-to-all-start.1
  2748.1 193.5 %all-reduce.2 = (f32[2048]{0:T(1024)S(1)}, f32[2048]{0:T(1024)S(1)}) all-reduce(f32[2048]{0:T(1024)S(1)} %bitcast.420, f32[2048]{0:T(1024)S(1)} %bitcast.419), channel_id=3, replica_groups=mesh['ctx'=4,'tp'=4,'fsdp'=2] {'ctx','fsdp'}, use_global_device_ids=true, to_apply=%region_17.18.clone | all-reduce | flops 4096 | bytes 32768
  2960.4 12.1 copy.327
  2972.5 12.0 convert.52
  2984.5 12.0 convert_bitcast_fusion.1
  3028.9 17.7 slice_multiply_fusion
  3055.3 9.1 copy.335
  3064.4 10.1 convert_subtract_fusion.1
  3083.2 9.4 copy.337
  3092.6 10.1 convert_subtract_fusion
  3111.3 10.3 bitcast_subtract_fusion
  (356 shorter events, 418.9 us)
Async XLA Ops:
  7.2 76.9 %copy-start.8 = (bf16[1,128,2048]{2,1,0:T(8,128)(2,1)S(1)}, bf16[1,128,2048]{2,1,0:T(8,128)(2,1)}, u32[]{:S(2)}) copy-start(bf16[1,128,2048]{2,1,0:T(8,128)(2,1)} %param.23) | copy-start | bytes 1572868
  7.2 38.2 %all-gather.19.cloned.1.call-start = ((), (), s32[]{:S(2)}) async-start(), calls=%async_computation.11 | async-start | bytes 3145728 | tf_op jit(solution)/shard_map/all_gather | solution.py:133
  7.9 72.2 %all-gather.17.cloned.1.call-start = ((), (), s32[]{:S(2)}) async-start(), calls=%async_computation.10 | async-start | bytes 3145728 | tf_op jit(solution)/shard_map/all_gather | solution.py:132
  8.7 106.2 %all-gather.21.cloned.1.call-start = ((), (), s32[]{:S(2)}) async-start(), calls=%async_computation.12 | async-start | bytes 3145728 | tf_op jit(solution)/shard_map/all_gather | solution.py:134
  9.4 140.0 %all-gather.23.cloned.1.call-start = ((), (), s32[]{:S(2)}) async-start(), calls=%async_computation.13 | async-start | bytes 3145728 | tf_op jit(solution)/shard_map/all_gather | solution.py:135
  10.0 194.5 %all-reduce.8.cloned.1.call-start = ((), (), s32[]{:S(2)}) async-start(), calls=%async_computation.14 | async-start | bytes 2097152 | tf_op jit(solution)/shard_map/psum | solution.py:169
  16.0 762.2 %copy-start.30 = (f32[2048]{0:T(1024)}, f32[2048]{0:T(1024)S(1)}, u32[]{:S(2)}) copy-start(f32[2048]{0:T(1024)S(1)} %convert_element_type.170) | copy-start | bytes 24580
  17.3 760.9 %copy-start.34 = (f32[128]{0:T(128)}, f32[128]{0:T(128)S(1)}, u32[]{:S(2)}) copy-start(f32[128]{0:T(128)S(1)} %add_rsqrt_fusion.1) | copy-start | bytes 1540
  18.1 70.1 %copy-start.27 = (f32[128,64]{0,1:T(8,128)}, f32[128,64]{0,1:T(8,128)S(1)}, u32[]{:S(2)}) copy-start(f32[128,64]{0,1:T(8,128)S(1)} %get-tuple-element.552) | copy-start | bytes 98308
  18.1 70.1 %copy-start.29 = (f32[128,64]{0,1:T(8,128)}, f32[128,64]{0,1:T(8,128)S(1)}, u32[]{:S(2)}) copy-start(f32[128,64]{0,1:T(8,128)S(1)} %get-tuple-element.551) | copy-start | bytes 98308
  141.3 13.2 copy-start.20
  149.4 5.2 copy-start.36
  152.5 156.9 %all-gather.25.cloned.1.call-start = ((), (), s32[]{:S(2)}) async-start(), calls=%async_computation.15 | async-start | bytes 12582912 | tf_op jit(solution)/shard_map/all_gather | solution.py:171
  153.1 262.0 %all-gather.27.cloned.1.call-start = ((), (), s32[]{:S(2)}) async-start(), calls=%async_computation.16 | async-start | bytes 12582912 | tf_op jit(solution)/shard_map/all_gather | solution.py:172
  153.8 366.9 %all-gather.29.cloned.1.call-start = ((), (), s32[]{:S(2)}) async-start(), calls=%async_computation.17 | async-start | bytes 12582912 | tf_op jit(solution)/shard_map/all_gather | solution.py:173
  154.6 433.8 %all-reduce.12.cloned.1.call-start = ((), (), s32[]{:S(2)}) async-start(), calls=%async_computation.19 | async-start | bytes 2097152 | tf_op jit(solution)/shard_map/psum | solution.py:196
  520.7 8.1 copy-start.6
  528.8 3.8 copy-start.7
  536.4 92.4 %all-reduce.10.cloned.1.call-start = ((), (), s32[]{:S(2)}) async-start(), calls=%async_computation.18 | async-start | bytes 1048576 | tf_op jit(solution)/shard_map/psum | solution.py:183
  542.1 170.5 %reduce-scatter.9.cloned.1.call-start = ((), (), s32[]{:S(2)}) async-start(), calls=%async_computation.20 | async-start | bytes 2621440 | tf_op jit(solution)/shard_map/reduce_scatter | solution.py:234
  676.5 39.6 %copy-start.28 = (f32[128,64]{0,1:T(8,128)S(1)}, f32[128,64]{0,1:T(8,128)}, u32[]{:S(2)}) copy-start(f32[128,64]{0,1:T(8,128)} %copy-done.27) | copy-start | bytes 98308
  677.8 42.9 %copy-start.16 = (bf16[2048,512]{1,0:T(8,128)(2,1)S(1)}, bf16[2048,512]{1,0:T(8,128)(2,1)}, u32[]{:S(2)}) copy-start(bf16[2048,512]{1,0:T(8,128)(2,1)} %all-gather.19.cloned.1.call-done) | copy-start | bytes 6291460
  681.0 97.2 %all-reduce.14.cloned.1.call-start = ((), (), s32[]{:S(2)}) async-start(), calls=%async_computation.21 | async-start | bytes 2097152 | tf_op jit(solution)/shard_map/psum | solution.py:255
  726.3 141.2 %reduce-scatter.17.cloned.1.call-start = ((), (), s32[]{:S(2)}) async-start(), calls=%async_computation.28 | async-start | bytes 4718592 | tf_op jit(solution)/shard_map/reduce_scatter | solution.py:288
  731.1 157.3 %reduce-scatter.11.cloned.1.call-start = ((), (), s32[]{:S(2)}) async-start(), calls=%async_computation.22 | async-start | bytes 4718592 | tf_op jit(solution)/shard_map/reduce_scatter | solution.py:270
  784.3 3.6 copy-start.24
  784.3 159.3 %reduce-scatter.13.cloned.1.call-start = ((), (), s32[]{:S(2)}) async-start(), calls=%async_computation.24 | async-start | bytes 4718592 | tf_op jit(solution)/shard_map/reduce_scatter | solution.py:276
  787.8 4.1 copy-start.23
  787.8 211.3 %reduce-scatter.15.cloned.1.call-start = ((), (), s32[]{:S(2)}) async-start(), calls=%async_computation.26 | async-start | bytes 4718592 | tf_op jit(solution)/shard_map/reduce_scatter | solution.py:282
  791.4 327.1 %reduce-scatter.19.cloned.1.call-start = ((), (), s32[]{:S(2)}) async-start(), calls=%async_computation.30 | async-start | bytes 18874368 | tf_op jit(solution)/shard_map/reduce_scatter | solution.py:294
  800.7 437.2 %reduce-scatter.21.cloned.1.call-start = ((), (), s32[]{:S(2)}) async-start(), calls=%async_computation.32 | async-start | bytes 18874368 | tf_op jit(solution)/shard_map/reduce_scatter | solution.py:300
  810.4 547.0 %reduce-scatter.23.cloned.1.call-start = ((), (), s32[]{:S(2)}) async-start(), calls=%async_computation.34 | async-start | bytes 18874368 | tf_op jit(solution)/shard_map/reduce_scatter | solution.py:306
  867.4 514.0 %all-gather.37.cloned.1.call-start = ((), (), s32[]{:S(2)}) async-start(), calls=%async_computation.29 | async-start | bytes 2621440 | tf_op jit(solution)/shard_map/all_gather | solution.py:329
  868.0 537.6 %all-gather.31.cloned.1.call-start = ((), (), s32[]{:S(2)}) async-start(), calls=%async_computation.23 | async-start | bytes 2621440 | tf_op jit(solution)/shard_map/all_gather | solution.py:326
  888.5 541.4 %all-gather.33.cloned.1.call-start = ((), (), s32[]{:S(2)}) async-start(), calls=%async_computation.25 | async-start | bytes 2621440 | tf_op jit(solution)/shard_map/all_gather | solution.py:327
  943.6 510.5 %all-gather.35.cloned.1.call-start = ((), (), s32[]{:S(2)}) async-start(), calls=%async_computation.27 | async-start | bytes 2621440 | tf_op jit(solution)/shard_map/all_gather | solution.py:328
  999.1 514.7 %all-gather.39.cloned.1.call-start = ((), (), s32[]{:S(2)}) async-start(), calls=%async_computation.31 | async-start | bytes 10485760 | tf_op jit(solution)/shard_map/all_gather | solution.py:330
  1118.5 455.2 %all-gather.41.cloned.1.call-start = ((), (), s32[]{:S(2)}) async-start(), calls=%async_computation.33 | async-start | bytes 10485760 | tf_op jit(solution)/shard_map/all_gather | solution.py:331
  1237.9 395.5 %all-gather.43.cloned.1.call-start = ((), (), s32[]{:S(2)}) async-start(), calls=%async_computation.35 | async-start | bytes 10485760 | tf_op jit(solution)/shard_map/all_gather | solution.py:332
  1590.4 4.8 copy-start.10
  1840.3 5.9 copy-start
  2029.0 3.4 copy-start.5
  2188.0 3.4 copy-start.1
  2333.1 3.4 copy-start.2
  2478.4 3.4 copy-start.3
  2623.9 3.4 copy-start.4
  2731.5 10.2 copy-start.19
  2731.5 15.3 copy-start.38
  2731.5 16.5 copy-start.32
  2731.5 16.6 copy-start.33
  2731.5 220.3 %copy-start.37 = (f32[128]{0:T(128)S(1)}, f32[128]{0:T(128)}, u32[]{:S(2)}) copy-start(f32[128]{0:T(128)} %get-tuple-element.453) | copy-start | bytes 1540
  2731.5 220.3 %copy-start.9 = (bf16[1,128,2048]{2,1,0:T(8,128)(2,1)S(1)}, bf16[1,128,2048]{2,1,0:T(8,128)(2,1)}, u32[]{:S(2)}) copy-start(bf16[1,128,2048]{2,1,0:T(8,128)(2,1)} %param.23) | copy-start | bytes 1572868
  2731.5 220.3 %copy-start.12 = (f32[128,2048]{1,0:T(8,128)S(1)}, f32[128,2048]{1,0:T(8,128)}, u32[]{:S(2)}) copy-start(f32[128,2048]{1,0:T(8,128)} %copy-done.11) | copy-start | bytes 3145732
  2731.5 220.3 %copy-start.31 = (f32[2048]{0:T(1024)S(1)}, f32[2048]{0:T(1024)}, u32[]{:S(2)}) copy-start(f32[2048]{0:T(1024)} %copy-done.30) | copy-start | bytes 24580
  2731.5 220.3 %copy-start.35 = (f32[128]{0:T(128)S(1)}, f32[128]{0:T(128)}, u32[]{:S(2)}) copy-start(f32[128]{0:T(128)} %copy-done.34) | copy-start | bytes 1540
  2731.5 228.9 %all-to-all-start.1 = ((bf16[1,8,512,2048]{2,1,0,3:T(8,128)(2,1)}), bf16[1,8,512,2048]{2,1,0,3:T(8,128)(2,1)}, u32[]{:S(2)}, u32[]{:S(2)}) async-start(bf16[1,8,512,2048]{2,1,0,3:T(8,128)(2,1)} %copy.326), calls=%async_computation.9 | async-start | bytes 33554432 | tf_op jit(solution)/shard_map/all_to_all | solution.py:378
  3017.6 9.7 copy-start.18
  3111.3 11.5 copy-start.13
  3111.3 12.8 copy-start.14
  3121.6 3.8 copy-start.15
  3124.2 10.7 slice-start
  3126.8 8.0 slice-start.1
  3126.8 12.3 slice-start.2
  3134.9 5.2 slice-start.3
  (6 other events, 10.0 us)
Sparse Core Ops, SparseCore 0:
  9.6 35.7 all-gather.18
  47.0 33.1 all-gather.16
  81.7 33.1 all-gather.20
  116.3 33.1 all-gather.22
  152.6 51.8 all-reduce.7
  205.9 103.3 all-gather.24
  311.0 103.9 all-gather.26
  416.6 103.9 all-gather.28
  536.5 51.8 all-reduce.11
  591.2 37.6 all-reduce.9
  681.2 31.3 reduce-scatter.8
  726.4 51.7 all-reduce.13
  782.2 50.6 reduce-scatter.16
  837.1 51.3 reduce-scatter.10
  892.2 51.2 reduce-scatter.12
  947.7 51.3 reduce-scatter.14
  1002.5 115.9 reduce-scatter.18
  1121.9 115.9 reduce-scatter.20
  1241.4 115.9 reduce-scatter.22
  1358.9 22.5 all-gather.36
  1383.1 22.5 all-gather.30
  1407.2 22.5 all-gather.32
  1431.4 22.5 all-gather.34
  1455.5 58.2 all-gather.38
  1515.3 58.2 all-gather.40
  1575.1 58.2 all-gather.42
where the time goes:
time: 3160 us; the launch traced here: 3150 us
  waiting for transfers between devices  1290 us (41%)
  matrix products  819 us (26%)
  blocking collectives  415 us (13%)
  local copies, waits for them, and re-layouts  404 us (13%)
  other arithmetic  194 us (6%)
    dot_general x5, matrix products, orthogonal(): jnp.einsum('ubc,ucd->ubd', mixed, state, precision=HIGH, preferred_elemen...  322 us
    dot_general x5, matrix products, orthogonal(): jnp.einsum('ubd,ucd->ubc', state, state, precision=HIGH, preferred_elemen...  308 us
    unnamed x1, blocking collectives  193 us
    all_to_all x1, blocking collectives, body(): lax.all_to_all(arranged.astype(jnp.bfloat16), 'fsdp', split_axis=0, conca...  187 us
    reduce_scatter x1, waiting for transfers between devices, body(): lax.psum_scatter(regroup(local_up, 0, fsdp_size, ctx_size), ('ctx', 'fsdp...  119 us
    reduce_scatter x1, waiting for transfers between devices, body(): lax.psum_scatter(regroup(local_down, 1, fsdp_size, ctx_size), ('ctx', 'fs...  119 us
    reduce_scatter x1, waiting for transfers between devices, body(): lax.psum_scatter(regroup(local_gate, 0, fsdp_size, ctx_size), ('ctx', 'fs...  119 us
    all_gather x1, waiting for transfers between devices, body(): lax.all_gather(w_gate, 'fsdp', axis=0, tiled=True)  103 us
  transfers between devices with their start and end apart: 27, of which 25 were waited for; matrix products, arithmetic and copies ran while one was open for 8% of the time, Pallas kernels for 0%

commit v1 on v0

v1 whole, which is shorter than its diff:
```python
import functools
import math

import jax
import jax.numpy as jnp
from jax import lax
from jax.experimental import pallas as pl
from jax.experimental.pallas import tpu as pltpu
from jax.sharding import PartitionSpec as P

HEAD_DIM = 64
NS_STEPS = 5
EPS = 1e-05
THETA = 130000.0
MOMENTUM = 0.95
COEF_A = 3.4445
COEF_B = -4.775
COEF_C = 2.0315
RATE = 0.5
BF = jnp.bfloat16
F32 = jnp.float32
VMEM_LIMIT = 56 * 1024 * 1024


def dot(left, right, ldim=1, rdim=0):
    return lax.dot_general(
        left, right, (((ldim,), (rdim,)), ((), ())), preferred_element_type=F32
    )


def params():
    return pltpu.CompilerParams(vmem_limit_bytes=VMEM_LIMIT)


def cost(flops, nbytes):
    return pl.CostEstimate(flops=int(flops), bytes_accessed=int(nbytes), transcendentals=0)


def swap(value, axis, bit):
    size = lax.axis_size(axis)
    return lax.ppermute(value, axis, [(i, i ^ bit) for i in range(size)])


def ctx_parts(value):
    two = swap(value, "ctx", 2)
    return [value, swap(value, "ctx", 1), two, swap(two, "ctx", 1)]


def pair():
    return lax.axis_size("fsdp") == 2


def f_scatter_cols(value):
    size = lax.axis_size("fsdp")
    rows, width = value.shape
    part = width // size
    if size == 2:
        own = lax.axis_index("fsdp")
        mine = lax.dynamic_slice_in_dim(value, own * part, part, 1)
        other = lax.dynamic_slice_in_dim(value, (1 - own) * part, part, 1)
        return jnp.concatenate([mine, swap(other, "fsdp", 1)], axis=0)
    cut = jnp.swapaxes(value.reshape(rows, size, part), 0, 1)
    return lax.all_to_all(cut, "fsdp", 0, 0, tiled=True).reshape(size * rows, part)


def f_gather_cols(value):
    size = lax.axis_size("fsdp")
    rows = value.shape[0] // size
    if size == 2:
        own = lax.axis_index("fsdp")
        mine, other = value[:rows], swap(value[rows:], "fsdp", 1)
        return jnp.concatenate(
            [jnp.where(own == 0, mine, other), jnp.where(own == 0, other, mine)], axis=1
        )
    cut = lax.all_to_all(value.reshape(size, rows, -1), "fsdp", 0, 0, tiled=True)
    return jnp.swapaxes(cut, 0, 1).reshape(rows, -1)


def f_gather_rows(value):
    if pair():
        return jnp.concatenate([value, swap(value, "fsdp", 1)], axis=0)
    return lax.all_gather(value, "fsdp", axis=0, tiled=True)


def f_reduce_rows(value):
    size = lax.axis_size("fsdp")
    rows = value.shape[0] // size
    if size == 2:
        return value[:rows].astype(F32) + swap(value[rows:], "fsdp", 1).astype(F32)
    return lax.psum_scatter(value.astype(F32), "fsdp", scatter_dimension=0, tiled=True)


def f_gather_weight(weight, axis):
    if not pair():
        return lax.all_gather(weight, "fsdp", axis=axis, tiled=True)
    own, me = lax.axis_index("fsdp"), lax.axis_index("ctx")
    half = weight.shape[axis]
    part = half // lax.axis_size("ctx")
    piece = lax.dynamic_slice_in_dim(weight, me * part, part, axis)
    pieces = ctx_parts(swap(piece, "fsdp", 1))
    shape = list(weight.shape)
    shape[axis] = 2 * half
    full = jnp.zeros(shape, weight.dtype)
    full = lax.dynamic_update_slice_in_dim(full, weight, own * half, axis)
    for j, received in enumerate(pieces):
        full = lax.dynamic_update_slice_in_dim(
            full, received, (1 - own) * half + (me ^ j) * part, axis
        )
    return full


def f_gather_vector(vector):
    if not pair():
        return lax.all_gather(vector, "fsdp", axis=0, tiled=True)
    own = lax.axis_index("fsdp")
    other = swap(vector, "fsdp", 1)
    return jnp.where(
        own == 0, jnp.concatenate([vector, other]), jnp.concatenate([other, vector])
    )


def z_reduce(value):
    size = lax.axis_size("tp")
    rows, width = value.shape
    cut = value.astype(BF).reshape(size, rows // size, width)
    return jnp.sum(lax.all_to_all(cut, "tp", 0, 0, tiled=True).astype(F32), axis=0)


def z_gather(value):
    return lax.all_gather(value, "tp", axis=0, tiled=True)


def rope_tables(position, width):
    half = HEAD_DIM // 2
    freq = THETA ** (-(jnp.arange(half, dtype=F32) * 2.0 / HEAD_DIM))
    angle = position[:, None] * freq[None, :]
    repeat = width // half
    return jnp.tile(jnp.cos(angle), (1, repeat)), jnp.tile(jnp.sin(angle), (1, repeat))


def first_half(shape):
    lane = lax.broadcasted_iota(jnp.int32, shape, 1)
    return (lane & (HEAD_DIM - 1)) < HEAD_DIM // 2


def rotate(values, cosine, sine):
    half = HEAD_DIM // 2
    turned = jnp.where(
        first_half(values.shape), -jnp.roll(values, -half, 1), jnp.roll(values, half, 1)
    )
    return values * cosine + turned * sine


def unrotate(grads, cosine, sine):
    half = HEAD_DIM // 2
    scaled = grads * sine
    back = jnp.where(
        first_half(grads.shape), jnp.roll(scaled, -half, 1), -jnp.roll(scaled, half, 1)
    )
    return grads * cosine + back


def head_probs(query, keys, allowed, scale):
    scores = jnp.where(allowed, dot(query, keys, 1, 1) * scale, -1e30)
    top = jnp.max(scores, axis=1, keepdims=True)
    expo = jnp.exp(scores - top)
    return expo / jnp.sum(expo, axis=1, keepdims=True)


def attention_kernel(scale, q_ref, k_ref, v_ref, qi_ref, qs_ref, ki_ref, ks_ref, o_ref):
    allowed = (ks_ref[...] == qs_ref[...]) & (ki_ref[...] <= qi_ref[...])
    query, keys, values = q_ref[...], k_ref[...], v_ref[...]
    lane = lax.broadcasted_iota(jnp.int32, query.shape, 1)
    outs = []
    for head in range(2):
        mine = (lane >= HEAD_DIM) == (head == 1)
        prob = head_probs(jnp.where(mine, query, 0), keys, allowed, scale)
        outs.append(dot(prob.astype(BF), values))
    o_ref[...] = jnp.where(lane < HEAD_DIM, outs[0], outs[1]).astype(BF)


def attention_grad_kernel(
    scale, q_ref, k_ref, v_ref, g_ref, qi_ref, qs_ref, ki_ref, ks_ref, dq_ref, dk_ref, dv_ref
):
    allowed = (ks_ref[...] == qs_ref[...]) & (ki_ref[...] <= qi_ref[...])
    query, keys, values, grads = q_ref[...], k_ref[...], v_ref[...], g_ref[...]
    lane = lax.broadcasted_iota(jnp.int32, query.shape, 1)
    wide = lax.broadcasted_iota(jnp.int32, keys.shape, 1)
    dqs, dks, dvs = [], [], []
    for head in range(2):
        mine = (lane >= HEAD_DIM) == (head == 1)
        prob = head_probs(jnp.where(mine, query, 0), keys, allowed, scale)
        dprob = dot(jnp.where(mine, grads, 0), values, 1, 1)
        delta = jnp.sum(prob * dprob, axis=1, keepdims=True)
        dscore = (prob * (dprob - delta)).astype(BF)
        dqs.append(dot(dscore, keys))
        dks.append(dot(dscore, query, 0, 0))
        dvs.append(dot(prob.astype(BF), grads, 0, 0))
    low, wlow = lane < HEAD_DIM, wide < HEAD_DIM
    dq_ref[...] = jnp.where(low, dqs[0], dqs[1]) * scale
    dk_ref[...] = (jnp.where(wlow, dks[0], dks[1]) * scale).astype(BF)
    dv_ref[...] = jnp.where(wlow, dvs[0], dvs[1]).astype(BF)


def attention_specs(rows, keys):
    def col(n):
        return pl.BlockSpec((n, 2 * HEAD_DIM), lambda h: (0, h))

    def whole(shape):
        return pl.BlockSpec(shape, lambda h: (0, 0))

    marks = [whole((rows, 1)), whole((rows, 1)), whole((1, keys)), whole((1, keys))]
    return col, marks


def attention(query, keys, values, marks):
    rows, width = query.shape
    count = keys.shape[0]
    col, mark_specs = attention_specs(rows, count)
    return pl.pallas_call(
        functools.partial(attention_kernel, 1.0 / math.sqrt(HEAD_DIM)),
        grid=(width // (2 * HEAD_DIM),),
        in_specs=[col(rows), col(count), col(count)] + mark_specs,
        out_specs=col(rows),
        out_shape=jax.ShapeDtypeStruct((rows, width), BF),
        compiler_params=params(),
        cost_estimate=cost(8 * rows * count * width, 4 * count * width),
        name="attention",
    )(query, keys, values, *marks)


def attention_grad(query, keys, values, grads, marks):
    rows, width = query.shape
    count = keys.shape[0]
    col, mark_specs = attention_specs(rows, count)
    return pl.pallas_call(
        functools.partial(attention_grad_kernel, 1.0 / math.sqrt(HEAD_DIM)),
        grid=(width // (2 * HEAD_DIM),),
        in_specs=[col(rows), col(count), col(count), col(rows)] + mark_specs,
        out_specs=[col(rows), col(count), col(count)],
        out_shape=[
            jax.ShapeDtypeStruct((rows, width), F32),
            jax.ShapeDtypeStruct((count, width), BF),
            jax.ShapeDtypeStruct((count, width), BF),
        ],
        compiler_params=params(),
        cost_estimate=cost(20 * rows * count * width, 8 * count * width),
        name="attention_grad",
    )(query, keys, values, grads, *marks)


def mlp_kernel(
    x_ref, dy_ref, wg_ref, wu_ref, wd_ref, hid_ref, dg_ref, du_ref, out_ref, dx_ref, acc_o, acc_d
):
    step = pl.program_id(0)
    gate = dot(x_ref[...], wg_ref[...])
    upper = dot(x_ref[...], wu_ref[...])
    dhid = dot(dy_ref[...], wd_ref[...], 1, 1)
    sigma = jax.nn.sigmoid(gate)
    silu = gate * sigma
    hidden = (silu * upper).astype(BF)
    dgate = (dhid * upper * sigma * (1.0 + gate * (1.0 - sigma))).astype(BF)
    dup = (dhid * silu).astype(BF)
    hid_ref[...] = hidden
    dg_ref[...] = dgate
    du_ref[...] = dup
    out = dot(hidden, wd_ref[...])
    grad = dot(dgate, wg_ref[...], 1, 1) + dot(dup, wu_ref[...], 1, 1)

    @pl.when(step == 0)
    def _():
        acc_o[...] = out
        acc_d[...] = grad

    @pl.when(step > 0)
    def _():
        acc_o[...] += out
        acc_d[...] += grad

    @pl.when(step == pl.num_programs(0) - 1)
    def _():
        out_ref[...] = acc_o[...].astype(BF)
        dx_ref[...] = acc_d[...].astype(BF)


def mlp(normed, grads, wgate, wup, wdown, tile=512):
    rows, width = normed.shape
    hidden = wgate.shape[1]
    whole = pl.BlockSpec((rows, width), lambda n: (0, 0))
    cols = pl.BlockSpec((width, tile), lambda n: (0, n))
    lanes = pl.BlockSpec((rows, tile), lambda n: (0, n))
    mid = jax.ShapeDtypeStruct((rows, hidden), BF)
    res = jax.ShapeDtypeStruct((rows, width), BF)
    return pl.pallas_call(
        mlp_kernel,
        grid=(hidden // tile,),
        in_specs=[whole, whole, cols, cols, pl.BlockSpec((tile, width), lambda n: (n, 0))],
        out_specs=[lanes, lanes, lanes, whole, whole],
        out_shape=[mid, mid, mid, res, res],
        scratch_shapes=[pltpu.VMEM((rows, width), F32), pltpu.VMEM((rows, width), F32)],
        compiler_params=params(),
        cost_estimate=cost(12 * rows * width * hidden, 6 * width * hidden),
        name="mlp",
    )(normed, grads, wgate, wup, wdown)


def weight_grad_kernel(count, gained, *refs):
    lefts, rights = refs[:count], refs[count : 2 * count]
    mom_ref = refs[2 * count]
    rest = refs[2 * count + 1 :]
    total = dot(lefts[0][...], rights[0][...], 0, 0)
    for left, right in zip(lefts[1:], rights[1:]):
        total += dot(left[...], right[...], 0, 0)
    mom = MOMENTUM * mom_ref[...] + total
    if gained:
        w_ref, g_ref, m_ref, l_ref, s_ref = rest
        prod = total * w_ref[...].astype(F32)
        lanes = prod[:, :128]
        for k in range(1, prod.shape[1] // 128):
            lanes += prod[:, 128 * k : 128 * (k + 1)]

        @pl.when(pl.program_id(1) == 0)
        def _():
            s_ref[...] = lanes

        @pl.when(pl.program_id(1) > 0)
        def _():
            s_ref[...] += lanes
    else:
        g_ref, m_ref, l_ref = rest
    g_ref[...] = total
    m_ref[...] = mom
    l_ref[...] = (total + MOMENTUM * mom).astype(BF)


def weight_grad(lefts, rights, mom, weight=None, tile=(512, 512)):
    count = len(lefts)
    tok = lefts[0].shape[0]
    height, width = mom.shape
    tm, tn = min(tile[0], height), min(tile[1], width)
    out = pl.BlockSpec((tm, tn), lambda i, j: (i, j))
    in_specs = [pl.BlockSpec((tok, tm), lambda i, j: (0, i))] * count
    in_specs += [pl.BlockSpec((tok, tn), lambda i, j: (0, j))] * count + [out]
    out_specs = [out, out, out]
    out_shape = [
        jax.ShapeDtypeStruct((height, width), F32),
        jax.ShapeDtypeStruct((height, width), F32),
        jax.ShapeDtypeStruct((height, width), BF),
    ]
    args = list(lefts) + list(rights) + [mom]
    if weight is not None:
        in_specs.append(out)
        args.append(weight)
        out_specs.append(pl.BlockSpec((tm, 128), lambda i, j: (i, 0)))
        out_shape.append(jax.ShapeDtypeStruct((height, 128), F32))
    return pl.pallas_call(
        functools.partial(weight_grad_kernel, count, weight is not None),
        grid=(height // tm, width // tn),
        in_specs=in_specs,
        out_specs=out_specs,
        out_shape=out_shape,
        compiler_params=params(),
        cost_estimate=cost(2 * count * tok * height * width, 16 * height * width),
        name="weight_grad",
    )(*args)


def polynomial_kernel(a_ref, b_ref, out_ref):
    size = a_ref.shape[0]
    row = lax.broadcasted_iota(jnp.int32, (size, size), 0)
    column = lax.broadcasted_iota(jnp.int32, (size, size), 1)
    eye = row == column

    def split(full):
        only = jnp.where(eye, full, 0.0)
        return (
            jnp.where(eye, 0.0, full),
            jnp.sum(only, axis=1, keepdims=True),
            jnp.sum(only, axis=0, keepdims=True),
        )

    def times(left, right):
        loff, lcol, lrow = left
        roff, rcol, rrow = right
        full = dot(loff.astype(BF), roff.astype(BF)) + lcol * roff + loff * rrow
        off, dcol, drow = split(full)
        return off, dcol + lcol * rcol, drow + lrow * rrow

    def mix(coefs, first, second, shift):
        off = coefs[0] * first[0] + coefs[1] * second[0]
        dcol = coefs[0] * first[1] + coefs[1] * second[1] + shift
        drow = coefs[0] * first[2] + coefs[1] * second[2] + shift
        return off, dcol, drow

    gram = split(a_ref[...] + b_ref[...])
    norm = jnp.sqrt(jnp.sum(gram[2])) + 1e-07
    inverse = 1.0 / (norm * norm)
    gram = tuple(part * inverse for part in gram)
    total = None
    for step in range(NS_STEPS):
        square = times(gram, gram)
        factor = mix((COEF_B, COEF_C), gram, square, COEF_A)
        total = factor if total is None else times(factor, total)
        if step < NS_STEPS - 1:
            gram = times(factor, times(factor, gram))
    weight = -RATE / norm
    out_ref[0:size, :] = (total[0] * weight).astype(BF)
    diagonal = total[2] * weight
    high = diagonal.astype(BF)
    low = (diagonal - high.astype(F32)).astype(BF)
    line = lax.broadcasted_iota(jnp.int32, (16, size), 0)
    tail = jnp.where(line == 0, high.astype(F32), jnp.where(line == 1, low.astype(F32), 0.0))
    out_ref[size : size + 16, :] = tail.astype(BF)


def polynomial(a, b):
    size = a.shape[0]
    return pl.pallas_call(
        polynomial_kernel,
        in_specs=[pl.BlockSpec(memory_space=pltpu.VMEM)] * 2,
        out_specs=pl.BlockSpec(memory_space=pltpu.VMEM),
        out_shape=jax.ShapeDtypeStruct((size + 16, size), BF),
        compiler_params=params(),
        cost_estimate=cost(34 * size**3, 10 * size * size),
        name="polynomial",
    )(a, b)


def update_kernel(by_columns, me_ref, q_ref, l_ref, w_ref, o_ref):
    size = q_ref.shape[2]
    look = l_ref[...]
    factor = q_ref[0, :size]
    ends = q_ref[0, size:].astype(F32)
    line = ends[0:1] + ends[1:2]
    if by_columns:
        step = dot(look, factor) + look.astype(F32) * line
    else:
        eye = lax.broadcasted_iota(jnp.int32, (size, size), 0) == lax.broadcasted_iota(
            jnp.int32, (size, size), 1
        )
        column = jnp.sum(jnp.where(eye, line, 0.0), axis=1, keepdims=True)
        step = dot(factor, look) + look.astype(F32) * column
    o_ref[...] = w_ref[...].astype(F32) + step


def update(factors, look, weight, by_columns, me):
    count, _, size = factors.shape
    height, width = weight.shape
    if by_columns:
        tile = min(512, height)
        grid = (width // size, height // tile)
        spec = pl.BlockSpec((tile, size), lambda b, i, me_ref: (i, b))
    else:
        tile = min(512, width)
        grid = (height // size, width // tile)
        spec = pl.BlockSpec((size, tile), lambda b, i, me_ref: (b, i))
    return pl.pallas_call(
        functools.partial(update_kernel, by_columns),
        grid_spec=pltpu.PrefetchScalarGridSpec(
            num_scalar_prefetch=1,
            grid=grid,
            in_specs=[
                pl.BlockSpec((1, size + 16, size), lambda b, i, me_ref: (b ^ me_ref[0], 0, 0)),
                spec,
                spec,
            ],
            out_specs=spec,
        ),
        out_shape=jax.ShapeDtypeStruct(weight.shape, F32),
        compiler_params=params(),
        cost_estimate=cost(2 * size * height * width, 8 * height * width),
        name="update",
    )(me, factors, look, weight)


def gram_of(block):
    return dot(block, block, 0, 0)


def body(
    tokens,
    out_grad,
    segment_start,
    norm_attn,
    norm_mlp,
    w_query,
    w_key,
    w_value,
    w_out,
    w_gate,
    w_up,
    w_down,
    mom_query,
    mom_key,
    mom_value,
    mom_out,
    mom_gate,
    mom_up,
    mom_down,
):
    rows = tokens.shape[1]
    me = lax.axis_index("ctx")
    my_t = lax.axis_index("tp")
    my_f = lax.axis_index("fsdp")
    n_tp = lax.axis_size("tp")
    width = w_query.shape[1]
    share = w_query.shape[0]
    low_in = tokens[0]
    inputs = low_in.astype(F32)
    grad_low = out_grad[0]

    gain_one = f_gather_vector(norm_attn).astype(F32)
    gain_two = f_gather_vector(norm_mlp).astype(F32)
    inv_one = lax.rsqrt(jnp.mean(inputs * inputs, axis=1, keepdims=True) + EPS)

    spread = f_scatter_cols(low_in)
    scaled = (spread.astype(F32) * norm_attn.astype(F32)).astype(BF)
    partial = jnp.concatenate(
        [dot(scaled, w).astype(BF) for w in (w_query, w_key, w_value)], axis=1
    )
    qkv = f_reduce_rows(partial) * inv_one

    starts = segment_start[0]
    chunks = [(me ^ j) * rows for j in range(lax.axis_size("ctx"))]
    key_start = jnp.concatenate([lax.dynamic_slice_in_dim(starts, o, rows) for o in chunks])
    key_index = jnp.concatenate([o + jnp.arange(rows, dtype=jnp.int32) for o in chunks])
    query_start, query_index = key_start[:rows], key_index[:rows]
    cosine, sine = rope_tables((query_index - query_start).astype(F32), width)
    marks = (query_index[:, None], query_start[:, None], key_index[None], key_start[None])

    query = rotate(qkv[:, :width], cosine, sine).astype(BF)
    kv_own = jnp.concatenate(
        [rotate(qkv[:, width : 2 * width], cosine, sine), qkv[:, 2 * width :]], axis=1
    ).astype(BF)
    kv = jnp.concatenate(ctx_parts(kv_own), axis=0)
    keys, values = kv[:, :width], kv[:, width:]
    attn = attention(query, keys, values, marks)

    wout = f_gather_weight(w_out, 1)
    wgate = f_gather_weight(w_gate, 0)
    wup = f_gather_weight(w_up, 0)
    wdown = f_gather_weight(w_down, 1)

    piece = rows // n_tp
    own_in = lax.dynamic_slice_in_dim(inputs, my_t * piece, piece, 0)
    own_inv = lax.dynamic_slice_in_dim(inv_one, my_t * piece, piece, 0)
    own_dy = lax.dynamic_slice_in_dim(grad_low, my_t * piece, piece, 0).astype(F32)

    middle = own_in + z_reduce(dot(attn, wout))
    inv_two = lax.rsqrt(jnp.mean(middle * middle, axis=1, keepdims=True) + EPS)
    normed_two = z_gather((middle * inv_two * gain_two).astype(BF))

    hidden, dgate, dup, out_part, dx_part = mlp(normed_two, grad_low, wgate, wup, wdown)

    grad_two = z_reduce(dx_part)
    scaled_two = middle * inv_two
    weighted = grad_two * gain_two
    grad_middle = own_dy + inv_two * (
        weighted - scaled_two * jnp.mean(weighted * scaled_two, axis=1, keepdims=True)
    )
    middle_low = z_gather(grad_middle.astype(BF))
    grad_attn = dot(middle_low, wout, 1, 1).astype(BF)

    result = z_gather((middle + z_reduce(out_part)).astype(BF))

    dquery, dkeys, dvalues = attention_grad(query, keys, values, grad_attn, marks)
    dkv = jnp.concatenate([dkeys, dvalues], axis=1)
    far = dkv[: 2 * rows].astype(F32) + swap(dkv[2 * rows :], "ctx", 2).astype(F32)
    near = far[:rows] + swap(far[rows:].astype(BF), "ctx", 1).astype(F32)
    dqkv = jnp.concatenate(
        [
            unrotate(dquery, cosine, sine),
            unrotate(near[:, :width], cosine, sine),
            near[:, width:],
        ],
        axis=1,
    ).astype(BF)

    dqkv_rows = f_gather_rows(dqkv)
    dx_one = (
        dot(dqkv_rows[:, :width], w_query, 1, 1)
        + dot(dqkv_rows[:, width : 2 * width], w_key, 1, 1)
        + dot(dqkv_rows[:, 2 * width :], w_value, 1, 1)
    )
    groups = lax.axis_size("fsdp")
    cut = jnp.swapaxes(dx_one.reshape(groups, n_tp, piece, share), 0, 1)
    grad_one = f_gather_cols(z_reduce(cut.reshape(groups * rows, share)).astype(BF)).astype(F32)
    scaled_one = own_in * own_inv
    weighted = grad_one * gain_one
    input_grad = grad_middle + own_inv * (
        weighted - scaled_one * jnp.mean(weighted * scaled_one, axis=1, keepdims=True)
    )
    input_grad = z_gather(input_grad.astype(BF)).astype(F32)

    def all_rows(value):
        return ctx_parts(f_gather_rows(value))

    def all_rows_own_cols(value):
        return ctx_parts(f_scatter_cols(value))

    normed = (inputs * inv_one * gain_one).astype(BF)
    dy_all = all_rows_own_cols(grad_low)
    two_all = all_rows_own_cols(normed_two)
    hidden_all, dgate_all, dup_all = all_rows(hidden), all_rows(dgate), all_rows(dup)
    g_down, m_down, l_down = weight_grad(hidden_all, dy_all, mom_down)
    g_gate, m_gate, l_gate, s_gate = weight_grad(two_all, dgate_all, mom_gate, w_gate)
    g_up, m_up, l_up, s_up = weight_grad(two_all, dup_all, mom_up, w_up)

    one_all = all_rows_own_cols(normed)
    attn_all = all_rows(attn)
    mid_all = all_rows_own_cols(middle_low)
    dqkv_all = ctx_parts(dqkv_rows)
    g_out, m_out, l_out = weight_grad(attn_all, mid_all, mom_out)
    parts = [
        [d[:, k * width : (k + 1) * width] for d in dqkv_all] for k in range(3)
    ]
    g_query, m_query, l_query, s_query = weight_grad(one_all, parts[0], mom_query, w_query)
    g_key, m_key, l_key, s_key = weight_grad(one_all, parts[1], mom_key, w_key)
    g_value, m_value, l_value, s_value = weight_grad(one_all, parts[2], mom_value, w_value)

    gains = jnp.stack([jnp.sum(s_query + s_key + s_value, axis=1), jnp.sum(s_gate + s_up, axis=1)])
    gains = jnp.sum(lax.all_gather(gains, "tp", axis=0), axis=0)
    grad_gain_one = gains[0] / norm_attn.astype(F32)
    grad_gain_two = gains[1] / norm_mlp.astype(F32)

    size = width

    def column_block(look):
        return lax.dynamic_slice_in_dim(look, me * size, size, 1)

    gram_down = dot(
        lax.dynamic_slice_in_dim(l_down, me * size, size, 0),
        lax.dynamic_slice_in_dim(l_down, me * size, size, 0),
        1,
        1,
    )
    gram_gate = gram_of(column_block(l_gate))
    gram_up = gram_of(column_block(l_up))
    four = jnp.stack([l_query, l_key, l_value, l_out.T])
    gram_attn = gram_of(lax.dynamic_index_in_dim(four, me, 0, keepdims=False))

    if pair():
        even = my_f == 0
        q_own = polynomial(
            jnp.where(even, gram_down, gram_gate),
            swap(jnp.where(even, gram_gate, gram_down), "fsdp", 1),
        )
        q_other = swap(q_own, "fsdp", 1)
        q_down = jnp.where(even, q_own, q_other)
        q_gate = jnp.where(even, q_other, q_own)
        q_up = polynomial(gram_up, swap(gram_up, "fsdp", 1))
        q_attn = polynomial(gram_attn, swap(gram_attn, "fsdp", 1))
    else:
        grams = lax.psum(jnp.stack([gram_down, gram_gate, gram_up, gram_attn]), "fsdp")
        none = jnp.zeros_like(gram_up)
        q_down, q_gate, q_up, q_attn = (polynomial(grams[k], none) for k in range(4))

    place = me.reshape(1).astype(jnp.int32)
    zero = jnp.zeros((1,), jnp.int32)
    q_down, q_gate, q_up, q_attn = (
        jnp.stack(ctx_parts(q)) for q in (q_down, q_gate, q_up, q_attn)
    )
    new_down = update(q_down, l_down, w_down, False, place)
    new_gate = update(q_gate, l_gate, w_gate, True, place)
    new_up = update(q_up, l_up, w_up, True, place)

    def attn_factor(k):
        return lax.dynamic_index_in_dim(q_attn, me ^ k, 0)

    new_query = update(attn_factor(0), l_query, w_query, True, zero)
    new_key = update(attn_factor(1), l_key, w_key, True, zero)
    new_value = update(attn_factor(2), l_value, w_value, True, zero)
    new_out = update(attn_factor(3), l_out, w_out, False, zero)

    return (
        result[None],
        input_grad[None],
        grad_gain_one,
        grad_gain_two,
        g_query,
        g_key,
        g_value,
        g_out,
        g_gate,
        g_up,
        g_down,
        m_query,
        m_key,
        m_value,
        m_out,
        m_gate,
        m_up,
        m_down,
        new_query,
        new_key,
        new_value,
        new_out,
        new_gate,
        new_up,
        new_down,
    )


def solution(mesh):
    act = P("fsdp", "ctx", None)
    col, row, vec = P("fsdp", "tp"), P("tp", "fsdp"), P("fsdp")
    seven = (col, col, col, row, col, col, row)
    in_specs = (act, act, P("fsdp", None), vec, vec) + seven + seven
    out_specs = (act, act, vec, vec) + seven + seven + seven
    return jax.shard_map(body, mesh=mesh, in_specs=in_specs, out_specs=out_specs, check_vma=False)
```

time: 3160 us -> 681 us (0.22)
  waiting for transfers between devices: 1290 us -> 169 us
  matrix products: 819 us -> 23.7 us
  blocking collectives: 415 us -> 77.5 us
  local copies, waits for them, and re-layouts: 404 us -> 98.9 us
  Pallas kernels: 0 us -> 189 us
  other arithmetic: 194 us -> 39.3 us
  starting transfers between devices: 12 us -> 71.5 us
    dot_general x78 -> x12, matrix products: 819 us -> 23.7 us  [dot(): lax.dot_general(left, right, (((ldim,), (rdim,)), ((), ())), preferred_el...]
    all_gather x14 -> x0, waiting for transfers between devices: 596 us -> none  [the longest x1 103 us: body(): lax.all_gather(w_gate, 'fsdp', axis=0, tiled=True)]
    reduce_scatter x8 -> x0, waiting for transfers between devices: 512 us -> none  [the longest x1 119 us: body(): lax.psum_scatter(regroup(local_up, 0, fsdp_size, ctx_size), ('ctx', 'fsdp...]
    unnamed x1 -> x0, blocking collectives: 193 us -> none
    pallas_call x0 -> x20, Pallas kernels: none -> 189 us  [the longest x7 80.3 us: weight_grad(): pl.pallas_call(functools.partial(weight_grad_kernel, count, weight is not...]
    all_to_all x1 -> x0, blocking collectives: 187 us -> none  [body(): lax.all_to_all(arranged.astype(jnp.bfloat16), 'fsdp', split_axis=0, conca...]
    psum x4 -> x0, waiting for transfers between devices: 177 us -> none  [the longest x1 47 us: body(): lax.psum(product_right(grad_query_pre, wquery) + product_right(grad_key_p...]
    ppermute x0 -> x78, waiting for transfers between devices: none -> 169 us  [swap(): return lax.ppermute(value, axis, [(i, i ^ bit) for i in range(size)])]
  transfers between devices with their start and end apart: 27 -> 82, of which waited for: 25 -> 17; matrix products, arithmetic and copies ran while one was open for 8% -> 22% of each run, Pallas kernels for 0% -> 26%
where the time goes in v1:
time: 681 us; the launch traced here: 671 us
  Pallas kernels  189 us (28%)
  waiting for transfers between devices  169 us (25%)
  local copies, waits for them, and re-layouts  98.9 us (15%)
  blocking collectives  77.5 us (11%)
  starting transfers between devices  71.5 us (10%)
  other arithmetic  39.3 us (6%)
  matrix products  23.7 us (3%)
    ppermute x78, waiting for transfers between devices, swap(): return lax.ppermute(value, axis, [(i, i ^ bit) for i in range(size)])  169 us
    pallas_call x7, Pallas kernels, weight_grad(): pl.pallas_call(functools.partial(weight_grad_kernel, count, weight is not...  80.3 us
    all_gather x4, blocking collectives, z_gather(): return lax.all_gather(value, 'tp', axis=0, tiled=True)  64.2 us
    ppermute x78, starting transfers between devices, swap(): return lax.ppermute(value, axis, [(i, i ^ bit) for i in range(size)])  51.2 us
    pallas_call x7, Pallas kernels, update(): pl.pallas_call(functools.partial(update_kernel, by_columns), grid_spec=pl...  46.6 us
    pallas_call x3, Pallas kernels, polynomial(): pl.pallas_call(polynomial_kernel, in_specs=[pl.BlockSpec(memory_space=plt...  31.2 us
    dynamic_update_slice x16, local copies, waits for them, and re-layouts, f_gather_weight(): lax.dynamic_update_slice_in_dim(full, received, (1 - own) * half + (me ^...  25.4 us
    dot_general x12, matrix products, dot(): lax.dot_general(left, right, (((ldim,), (rdim,)), ((), ())), preferred_el...  23.7 us
  transfers between devices with their start and end apart: 82, of which 17 were waited for; matrix products, arithmetic and copies ran while one was open for 22% of the time, Pallas kernels for 26%

profile of v1, /device:TPU:0, one launch (start us, length us, event | category | flops | bytes accessed | tf_op | source)
XLA Modules:
  0.0 670.7 jit_solution(11280641829666318862)
XLA Ops:
  2.5 2.9 collective-permute-start
  9.1 2.3 constant_dynamic-slice_fusion.11
  15.0 4.5 broadcast.138.clone.1
  19.5 2.3 constant_dynamic-update-slice_fusion.17
  26.2 4.8 broadcast.138.clone.2
  33.0 2.5 constant_dynamic-update-slice_fusion.12
  51.0 2.3 constant_dynamic-slice_fusion.10
  59.6 2.1 convert_element_type.125
  74.3 5.4 attention.1
  79.7 2.2 convolution_convert_fusion
  81.9 4.9 all-to-all-start
  86.7 23.3 %collective-permute-done.26 = bf16[1024]{0:T(1024)(128)(2,1)S(1)} collective-permute-done((bf16[1024]{0:T(1024)(128)(2,1)S(1)}, bf16[1024]{0:T(1024)(128)(2,1)S(1)}, u32[]{:S(2)}, u32[]{:S(2)}) %collective-permute-start.26) | collective-permute-done | bytes 2080 | tf_op jit(solution)/shard_map/ppermute | solution.py:41
  113.9 2.3 constant_dynamic-update-slice_fusion.16
  116.2 2.3 constant_dynamic-update-slice_fusion.21
  118.5 2.3 constant_dynamic-update-slice_fusion.11
  123.3 17.2 %all_gather.18.x_ref = bf16[128,2048]{1,0:T(8,128)(2,1)} all-gather(bf16[32,2048]{1,0:T(8,128)(2,1)S(1)} %multiply_convert_fusion.1), channel_id=1, replica_groups=mesh['ctx'=4,'tp'=4,'fsdp'=2] {'tp'}, dimensions={0}, use_global_device_ids=true | all-gather | bytes 655360 | tf_op jit(solution)/shard_map/all_gather | solution.py:130
  140.5 2.3 constant_dynamic-update-slice_fusion.15
  142.8 2.3 constant_dynamic-update-slice_fusion.14
  145.6 13.3 %collective-permute-done.12 = bf16[256,2048]{1,0:T(8,128)(2,1)} collective-permute-done((bf16[256,2048]{1,0:T(8,128)(2,1)}, bf16[256,2048]{1,0:T(8,128)(2,1)}, u32[]{:S(2)}, u32[]{:S(2)}) %collective-permute-start.12) | collective-permute-done | bytes 1048608 | tf_op jit(solution)/shard_map/ppermute | solution.py:41
  159.0 22.0 %collective-permute-done.20 = bf16[2048,256]{1,0:T(8,128)(2,1)} collective-permute-done((bf16[2048,256]{1,0:T(8,128)(2,1)}, bf16[2048,256]{1,0:T(8,128)(2,1)}, u32[]{:S(2)}, u32[]{:S(2)}) %collective-permute-start.20) | collective-permute-done | bytes 1048608 | tf_op jit(solution)/shard_map/ppermute | solution.py:41
  181.0 2.3 constant_dynamic-update-slice_fusion.20
  183.3 2.3 constant_dynamic-update-slice_fusion.19
  186.6 2.3 constant_dynamic-update-slice_fusion.9
  192.0 18.2 %mlp.1 = (bf16[128,2048]{1,0:T(8,128)(2,1)}, bf16[128,2048]{1,0:T(8,128)(2,1)}, bf16[128,2048]{1,0:T(8,128)(2,1)}, bf16[128,2048]{1,0:T(8,128)(2,1)}, bf16[128,2048]{1,0:T(8,128)(2,1)}) custom-call(bf16[128,2048]{1,0:T(8,128)(2,1)} %all_gather.18.x_ref, bf16[128,2048]{1,0:T(8,128)(2,1)} %bitcast.101, ...), custom_call_target="tpu_custom_call" | custom-call | flops 6442450944 | bytes 25165824 | tf_op jit(solution)/shard_map/mlp/pallas_call | solution.py:294
  210.2 5.0 all-to-all-start.2
  224.0 2.8 collective-permute-done.27
  233.9 15.4 %all_gather.20 = bf16[128,2048]{1,0:T(8,128)(2,1)S(1)} all-gather(bf16[32,2048]{1,0:T(8,128)(2,1)S(1)} %fusion.49), channel_id=1, replica_groups=mesh['ctx'=4,'tp'=4,'fsdp'=2] {'tp'}, dimensions={0}, use_global_device_ids=true | all-gather | bytes 655360 | tf_op jit(solution)/shard_map/all_gather | solution.py:130
  251.6 7.0 %attention_grad.1 = (f32[128,512]{1,0:T(8,128)}, bf16[512,512]{1,0:T(8,128)(2,1)}, bf16[512,512]{1,0:T(8,128)(2,1)}) custom-call(bf16[128,512]{1,0:T(8,128)(2,1)} %get-tuple-element.104.q_ref, bf16[512,512]{1,0:T(8,128)(2,1)} %get-tuple-element.108.k_ref, bf16[512,512]{1,0:T(8,128)(2,1)} %get-tuple-element.107.v_ref, ...), custom_call_target="tpu_custom_call" | custom-call | flops 671088640 | bytes 2097152 | tf_op jit(solution)/shard_map/attention_grad/pallas_call | solution.py:236
  268.5 5.2 all-to-all-start.1
  284.0 2.7 collective-permute-done.29.refs_2_
  293.2 15.5 %collective-permute-done.50 = bf16[128,1024]{1,0:T(8,128)(2,1)S(1)} collective-permute-done((bf16[128,1024]{1,0:T(8,128)(2,1)S(1)}, bf16[128,1024]{1,0:T(8,128)(2,1)S(1)}, u32[]{:S(2)}, u32[]{:S(2)}) %collective-permute-start.50) | collective-permute-done | bytes 262176 | tf_op jit(solution)/shard_map/ppermute | solution.py:41
  311.2 5.3 collective-permute-done.24
  321.7 29.0 %collective-permute-done.36.refs_2_ = bf16[256,1024]{1,0:T(8,128)(2,1)} collective-permute-done((bf16[256,1024]{1,0:T(8,128)(2,1)S(1)}, bf16[256,1024]{1,0:T(8,128)(2,1)}, u32[]{:S(2)}, u32[]{:S(2)}) %collective-permute-start.36) | collective-permute-done | bytes 524320 | tf_op jit(solution)/shard_map/ppermute | solution.py:41
  352.5 7.5 %collective-permute-done.52.refs_6_ = bf16[256,1024]{1,0:T(8,128)(2,1)} collective-permute-done((bf16[256,1024]{1,0:T(8,128)(2,1)}, bf16[256,1024]{1,0:T(8,128)(2,1)}, u32[]{:S(2)}, u32[]{:S(2)}) %collective-permute-start.52) | collective-permute-done | bytes 524320 | tf_op jit(solution)/shard_map/ppermute | solution.py:41
  364.3 5.2 all-to-all-start.3
  370.5 5.2 weight_grad.12
  375.8 3.7 collective-permute-done.44.refs_6_
  380.0 18.7 %weight_grad.13 = (f32[2048,1024]{1,0:T(8,128)}, f32[2048,1024]{1,0:T(8,128)}, bf16[2048,1024]{1,0:T(8,128)(2,1)}) custom-call(bf16[256,2048]{1,0:T(8,128)(2,1)} %constant_dynamic-update-slice_fusion.6.refs_0_, bf16[256,2048]{1,0:T(8,128)(2,1)} %collective-permute-done.55.refs_1_, bf16[256,2048]{1,0:T(8,128)(2,1)} %collective-permute-done.56.refs_2_, ...), custom_call_target="tpu_custom_call" | custom-call | flops 4294967296 | bytes 33554432 | tf_op jit(solution)/shard_map/weight_grad/pallas_call | solution.py:356
  398.7 2.3 fusion.13
  403.2 20.0 %weight_grad.10 = (f32[1024,2048]{1,0:T(8,128)}, f32[1024,2048]{1,0:T(8,128)}, bf16[1024,2048]{1,0:T(8,128)(2,1)}, f32[1024,128]{1,0:T(8,128)}) custom-call(bf16[256,1024]{1,0:T(8,128)(2,1)} %copy-done.15, bf16[256,1024]{1,0:T(8,128)(2,1)} %collective-permute-done.35.refs_1_, bf16[256,1024]{1,0:T(8,128)(2,1)} %collective-permute-done.36.refs_2_, ...), custom_call_target="tpu_custom_call" | custom-call | flops 4294967296 | bytes 33554432 | tf_op jit(solution)/shard_map/weight_grad/pallas_call | solution.py:356
  423.1 3.7 broadcast_select_fusion.2
  428.5 19.9 %weight_grad.11 = (f32[1024,2048]{1,0:T(8,128)}, f32[1024,2048]{1,0:T(8,128)}, bf16[1024,2048]{1,0:T(8,128)(2,1)}, f32[1024,128]{1,0:T(8,128)}) custom-call(bf16[256,1024]{1,0:T(8,128)(2,1)} %copy-done.15, bf16[256,1024]{1,0:T(8,128)(2,1)} %collective-permute-done.35.refs_1_, bf16[256,1024]{1,0:T(8,128)(2,1)} %collective-permute-done.36.refs_2_, ...), custom_call_target="tpu_custom_call" | custom-call | flops 4294967296 | bytes 33554432 | tf_op jit(solution)/shard_map/weight_grad/pallas_call | solution.py:356
  448.5 3.5 fusion.9.a_ref
  460.1 20.7 %collective-permute-done.25 = bf16[32,1024]{1,0:T(8,128)(2,1)S(1)} collective-permute-done((bf16[32,1024]{1,0:T(8,128)(2,1)S(1)}, bf16[32,1024]{1,0:T(8,128)(2,1)S(1)}, u32[]{:S(2)}, u32[]{:S(2)}) %collective-permute-start.25) | collective-permute-done | bytes 65568 | tf_op jit(solution)/shard_map/ppermute | solution.py:41
  482.2 15.9 %all_gather.21 = bf16[128,2048]{1,0:T(8,128)(2,1)S(1)} all-gather(bf16[32,2048]{1,0:T(8,128)(2,1)S(1)} %get-tuple-element.141), channel_id=1, replica_groups=mesh['ctx'=4,'tp'=4,'fsdp'=2] {'tp'}, dimensions={0}, use_global_device_ids=true | all-gather | bytes 655360 | tf_op jit(solution)/shard_map/all_gather | solution.py:130
  499.1 15.8 %all_gather.19 = bf16[128,2048]{1,0:T(8,128)(2,1)S(1)} all-gather(bf16[32,2048]{1,0:T(8,128)(2,1)S(1)} %get-tuple-element.142), channel_id=1, replica_groups=mesh['ctx'=4,'tp'=4,'fsdp'=2] {'tp'}, dimensions={0}, use_global_device_ids=true | all-gather | bytes 655360 | tf_op jit(solution)/shard_map/all_gather | solution.py:130
  516.8 5.5 weight_grad.8
  522.3 5.5 weight_grad.7
  530.5 5.6 weight_grad.9
  536.1 2.3 copy.76
  538.4 4.8 fusion.15.a_ref
  544.7 13.3 %all-gather.1 = f32[4,2,1024]{2,1,0:T(2,128)S(1)} all-gather(f32[1,2,1024]{2,1,0:T(2,128)S(1)} %maximum_bitcast_fusion), channel_id=2, replica_groups=mesh['ctx'=4,'tp'=4,'fsdp'=2] {'tp'}, dimensions={0}, use_global_device_ids=true | all-gather | bytes 40960 | tf_op jit(solution)/shard_map/all_gather | solution.py:622
  558.0 10.3 %polynomial.4 = bf16[528,512]{1,0:T(8,128)(2,1)} custom-call(f32[512,512]{1,0:T(8,128)} %get-tuple-element.102.a_ref, f32[512,512]{1,0:T(8,128)} %collective-permute-done.66.b_ref), custom_call_target="tpu_custom_call" | custom-call | flops 4563402752 | bytes 2621440 | tf_op jit(solution)/shard_map/polynomial/pallas_call | solution.py:418
  569.2 10.6 %polynomial.5 = bf16[528,512]{1,0:T(8,128)(2,1)} custom-call(f32[512,512]{1,0:T(8,128)} %fusion.9.a_ref, f32[512,512]{1,0:T(8,128)} %collective-permute-done.71.b_ref), custom_call_target="tpu_custom_call" | custom-call | flops 4563402752 | bytes 2621440 | tf_op jit(solution)/shard_map/polynomial/pallas_call | solution.py:418
  582.8 12.3 %collective-permute-done.73 = bf16[528,512]{1,0:T(8,128)(2,1)S(1)} collective-permute-done((bf16[528,512]{1,0:T(8,128)(2,1)}, bf16[528,512]{1,0:T(8,128)(2,1)S(1)}, u32[]{:S(2)}, u32[]{:S(2)}) %collective-permute-start.73) | collective-permute-done | bytes 540704 | tf_op jit(solution)/shard_map/ppermute | solution.py:41
  596.1 10.3 %polynomial.3 = bf16[528,512]{1,0:T(8,128)(2,1)} custom-call(f32[512,512]{1,0:T(8,128)} %fusion.15.a_ref, f32[512,512]{1,0:T(8,128)} %copy-done.83), custom_call_target="tpu_custom_call" | custom-call | flops 4563402752 | bytes 2621440 | tf_op jit(solution)/shard_map/polynomial/pallas_call | solution.py:418
  609.5 6.0 collective-permute-done.69
  617.2 11.3 %update.12 = f32[1024,2048]{1,0:T(8,128)} custom-call(s32[1]{0:T(128)} %bitcast.40.me_ref, bf16[4,528,512]{2,1,0:T(8,128)(2,1)} %pad_maximum_fusion.2.q_ref, bf16[1024,2048]{1,0:T(8,128)(2,1)} %get-tuple-element.92.l_ref, bf16[1024,2048]{1,0:T(8,128)(2,1)} %w_ref.12), custom_call_target="tpu_custom_call" | custom-call | flops 2147483648 | bytes 16777216 | tf_op jit(solution)/shard_map/update/pallas_call | solution.py:457
  632.5 11.1 %update.13 = f32[2048,1024]{1,0:T(8,128)} custom-call(s32[1]{0:T(128)} %bitcast.40.me_ref, bf16[4,528,512]{2,1,0:T(8,128)(2,1)} %pad_maximum_fusion.3.q_ref, bf16[2048,1024]{1,0:T(8,128)(2,1)} %get-tuple-element.90.l_ref, bf16[2048,1024]{1,0:T(8,128)(2,1)} %w_ref.13), custom_call_target="tpu_custom_call" | custom-call | flops 2147483648 | bytes 16777216 | tf_op jit(solution)/shard_map/update/pallas_call | solution.py:457
  643.6 11.1 %update.11 = f32[1024,2048]{1,0:T(8,128)} custom-call(s32[1]{0:T(128)} %bitcast.40.me_ref, bf16[4,528,512]{2,1,0:T(8,128)(2,1)} %pad_maximum_fusion.1.q_ref, bf16[1024,2048]{1,0:T(8,128)(2,1)} %get-tuple-element.91.l_ref, bf16[1024,2048]{1,0:T(8,128)(2,1)} %w_ref.11), custom_call_target="tpu_custom_call" | custom-call | flops 2147483648 | bytes 16777216 | tf_op jit(solution)/shard_map/update/pallas_call | solution.py:457
  656.3 3.3 update.10
  659.6 3.3 update.9
  662.9 3.3 update.8
  666.2 3.3 update.7
  (438 shorter events, 156.7 us)
Async XLA Ops:
  2.5 35.0 %collective-permute-start = (bf16[128,1024]{1,0:T(8,128)(2,1)}, bf16[128,1024]{1,0:T(8,128)(2,1)}, u32[]{:S(2)}, u32[]{:S(2)}) collective-permute-start(bf16[128,1024]{1,0:T(8,128)(2,1)} %get-tuple-element.138), channel_id=1, source_target_pairs={{0,1},{1,0},{2,3},{3,2},{4,5},{5,4},{6,7},{7,6},{8,9},{9,8},{10,11... | collective-permute-start | bytes 786440 | tf_op jit(solution)/shard_map/ppermute | solution.py:41
  7.1 46.2 %collective-permute-start.5 = (bf16[512,256]{1,0:T(8,128)(2,1)}, bf16[512,256]{1,0:T(8,128)(2,1)}, u32[]{:S(2)}, u32[]{:S(2)}) collective-permute-start(bf16[512,256]{1,0:T(8,128)(2,1)} %constant_dynamic-slice_fusion.13), channel_id=1, source_target_pairs={{0,1},{1,0},{2,3},{3,2},{4,5},{5,4},{6,7},{7,6},{8,9},{9,8},{10,11... | collective-permute-start | bytes 786440 | tf_op jit(solution)/shard_map/ppermute | solution.py:41
  7.1 55.3 %collective-permute-start.9 = (bf16[1024]{0:T(1024)(128)(2,1)}, bf16[1024]{0:T(1024)(128)(2,1)S(1)}, u32[]{:S(2)}, u32[]{:S(2)}) collective-permute-start(bf16[1024]{0:T(1024)(128)(2,1)} %param.23), channel_id=1, source_target_pairs={{0,1},{1,0},{2,3},{3,2},{4,5},{5,4},{6,7},{7,6},{8,9},{9,8},{10,11... | collective-permute-start | bytes 6152 | tf_op jit(solution)/shard_map/ppermute | solution.py:41
  11.5 98.6 %collective-permute-start.14 = (bf16[256,2048]{1,0:T(8,128)(2,1)}, bf16[256,2048]{1,0:T(8,128)(2,1)}, u32[]{:S(2)}, u32[]{:S(2)}) collective-permute-start(bf16[256,2048]{1,0:T(8,128)(2,1)} %constant_dynamic-slice_fusion.11), channel_id=1, source_target_pairs={{0,1},{1,0},{2,3},{3,2},{4,5},{5,4},{6,7},{7,6},{8,9},{9,8},{10,11... | collective-permute-start | bytes 3145736 | tf_op jit(solution)/shard_map/ppermute | solution.py:41
  62.4 49.3 %collective-permute-start.10 = (bf16[256,2048]{1,0:T(8,128)(2,1)}, bf16[256,2048]{1,0:T(8,128)(2,1)}, u32[]{:S(2)}, u32[]{:S(2)}) collective-permute-start(bf16[256,2048]{1,0:T(8,128)(2,1)} %constant_dynamic-slice_fusion.12), channel_id=1, source_target_pairs={{0,1},{1,0},{2,3},{3,2},{4,5},{5,4},{6,7},{7,6},{8,9},{9,8},{10,11... | collective-permute-start | bytes 3145736 | tf_op jit(solution)/shard_map/ppermute | solution.py:41
  69.0 43.4 %collective-permute-start.18 = (bf16[2048,256]{1,0:T(8,128)(2,1)}, bf16[2048,256]{1,0:T(8,128)(2,1)}, u32[]{:S(2)}, u32[]{:S(2)}) collective-permute-start(bf16[2048,256]{1,0:T(8,128)(2,1)} %constant_dynamic-slice_fusion.10), channel_id=1, source_target_pairs={{0,1},{1,0},{2,3},{3,2},{4,5},{5,4},{6,7},{7,6},{8,9},{9,8},{10,11... | collective-permute-start | bytes 3145736 | tf_op jit(solution)/shard_map/ppermute | solution.py:41
  70.4 39.6 %collective-permute-start.26 = (bf16[1024]{0:T(1024)(128)(2,1)S(1)}, bf16[1024]{0:T(1024)(128)(2,1)S(1)}, u32[]{:S(2)}, u32[]{:S(2)}) collective-permute-start(bf16[1024]{0:T(1024)(128)(2,1)S(1)} %copy-done.59), channel_id=1, source_target_pairs={{0,1},{1,0},{2,3},{3,2},{4,5},{5,4},{6,7},{7,6},{8,9},{9,8},{10,11... | collective-permute-start | bytes 6152 | tf_op jit(solution)/shard_map/ppermute | solution.py:41
  81.9 38.9 %all-to-all-start = ((bf16[4,32,2048]{2,1,0:T(8,128)(2,1)}), bf16[4,32,2048]{2,1,0:T(8,128)(2,1)}, u32[]{:S(2)}, u32[]{:S(2)}) async-start(bf16[4,32,2048]{2,1,0:T(8,128)(2,1)} %bitcast.106), calls=%async_computation | async-start | bytes 1048576 | tf_op jit(solution)/shard_map/all_to_all | solution.py:126
  110.1 13.1 %collective-permute-start.15 = (bf16[256,2048]{1,0:T(8,128)(2,1)}, bf16[256,2048]{1,0:T(8,128)(2,1)}, u32[]{:S(2)}, u32[]{:S(2)}) collective-permute-start(bf16[256,2048]{1,0:T(8,128)(2,1)} %collective-permute-done.14), channel_id=1, source_target_pairs={{0,8},{8,0},{16,24},{24,16},{1,9},{9,1},{17,25},{25,17},{2,10},{10... | collective-permute-start | bytes 3145736 | tf_op jit(solution)/shard_map/ppermute | solution.py:41
  110.1 30.3 %collective-permute-start.16 = (bf16[256,2048]{1,0:T(8,128)(2,1)}, bf16[256,2048]{1,0:T(8,128)(2,1)}, u32[]{:S(2)}, u32[]{:S(2)}) collective-permute-start(bf16[256,2048]{1,0:T(8,128)(2,1)} %collective-permute-done.14), channel_id=1, source_target_pairs={{0,16},{8,24},{16,0},{24,8},{1,17},{9,25},{17,1},{25,9},{2,18},{10... | collective-permute-start | bytes 3145736 | tf_op jit(solution)/shard_map/ppermute | solution.py:41
  111.7 33.3 %collective-permute-start.11 = (bf16[256,2048]{1,0:T(8,128)(2,1)}, bf16[256,2048]{1,0:T(8,128)(2,1)}, u32[]{:S(2)}, u32[]{:S(2)}) collective-permute-start(bf16[256,2048]{1,0:T(8,128)(2,1)} %collective-permute-done.10), channel_id=1, source_target_pairs={{0,8},{8,0},{16,24},{24,16},{1,9},{9,1},{17,25},{25,17},{2,10},{10... | collective-permute-start | bytes 3145736 | tf_op jit(solution)/shard_map/ppermute | solution.py:41
  111.9 47.1 %collective-permute-start.12 = (bf16[256,2048]{1,0:T(8,128)(2,1)}, bf16[256,2048]{1,0:T(8,128)(2,1)}, u32[]{:S(2)}, u32[]{:S(2)}) collective-permute-start(bf16[256,2048]{1,0:T(8,128)(2,1)} %collective-permute-done.10), channel_id=1, source_target_pairs={{0,16},{8,24},{16,0},{24,8},{1,17},{9,25},{17,1},{25,9},{2,18},{10... | collective-permute-start | bytes 3145736 | tf_op jit(solution)/shard_map/ppermute | solution.py:41
  112.4 68.6 %collective-permute-start.20 = (bf16[2048,256]{1,0:T(8,128)(2,1)}, bf16[2048,256]{1,0:T(8,128)(2,1)}, u32[]{:S(2)}, u32[]{:S(2)}) collective-permute-start(bf16[2048,256]{1,0:T(8,128)(2,1)} %collective-permute-done.18), channel_id=1, source_target_pairs={{0,16},{8,24},{16,0},{24,8},{1,17},{9,25},{17,1},{25,9},{2,18},{10... | collective-permute-start | bytes 3145736 | tf_op jit(solution)/shard_map/ppermute | solution.py:41
  123.2 62.4 %collective-permute-start.19 = (bf16[2048,256]{1,0:T(8,128)(2,1)}, bf16[2048,256]{1,0:T(8,128)(2,1)S(1)}, u32[]{:S(2)}, u32[]{:S(2)}) collective-permute-start(bf16[2048,256]{1,0:T(8,128)(2,1)} %collective-permute-done.18), channel_id=1, source_target_pairs={{0,8},{8,0},{16,24},{24,16},{1,9},{9,1},{17,25},{25,17},{2,10},{10... | collective-permute-start | bytes 3145736 | tf_op jit(solution)/shard_map/ppermute | solution.py:41
  140.4 48.4 %collective-permute-start.17 = (bf16[256,2048]{1,0:T(8,128)(2,1)}, bf16[256,2048]{1,0:T(8,128)(2,1)S(1)}, u32[]{:S(2)}, u32[]{:S(2)}) collective-permute-start(bf16[256,2048]{1,0:T(8,128)(2,1)} %collective-permute-done.16), channel_id=1, source_target_pairs={{0,8},{8,0},{16,24},{24,16},{1,9},{9,1},{17,25},{25,17},{2,10},{10... | collective-permute-start | bytes 3145736 | tf_op jit(solution)/shard_map/ppermute | solution.py:41
  145.1 75.5 %collective-permute-start.58 = (bf16[128,1024]{1,0:T(8,128)(2,1)}, bf16[128,1024]{1,0:T(8,128)(2,1)}, u32[]{:S(2)}, u32[]{:S(2)}) collective-permute-start(bf16[128,1024]{1,0:T(8,128)(2,1)} %get-tuple-element.130), channel_id=1, source_target_pairs={{0,1},{1,0},{2,3},{3,2},{4,5},{5,4},{6,7},{7,6},{8,9},{9,8},{10,11... | collective-permute-start | bytes 786440 | tf_op jit(solution)/shard_map/ppermute | solution.py:41
  158.9 31.0 %collective-permute-start.13 = (bf16[256,2048]{1,0:T(8,128)(2,1)}, bf16[256,2048]{1,0:T(8,128)(2,1)S(1)}, u32[]{:S(2)}, u32[]{:S(2)}) collective-permute-start(bf16[256,2048]{1,0:T(8,128)(2,1)} %collective-permute-done.12), channel_id=1, source_target_pairs={{0,8},{8,0},{16,24},{24,16},{1,9},{9,1},{17,25},{25,17},{2,10},{10... | collective-permute-start | bytes 3145736 | tf_op jit(solution)/shard_map/ppermute | solution.py:41
  210.2 20.6 %all-to-all-start.2 = ((bf16[4,32,2048]{2,1,0:T(8,128)(2,1)}), bf16[4,32,2048]{2,1,0:T(8,128)(2,1)}, u32[]{:S(2)}, u32[]{:S(2)}) async-start(bf16[4,32,2048]{2,1,0:T(8,128)(2,1)} %bitcast.127), calls=%async_computation.2 | async-start | bytes 1048576 | tf_op jit(solution)/shard_map/all_to_all | solution.py:126
  222.5 51.3 %collective-permute-start.60 = (bf16[256,1024]{1,0:T(8,128)(2,1)}, bf16[256,1024]{1,0:T(8,128)(2,1)}, u32[]{:S(2)}, u32[]{:S(2)}) collective-permute-start(bf16[256,1024]{1,0:T(8,128)(2,1)} %pad_maximum_fusion.10.refs_4_), channel_id=1, source_target_pairs={{0,16},{8,24},{16,0},{24,8},{1,17},{9,25},{17,1},{25,9},{2,18},{10... | collective-permute-start | bytes 1572872 | tf_op jit(solution)/shard_map/ppermute | solution.py:41
  224.0 58.4 %collective-permute-start.59 = (bf16[256,1024]{1,0:T(8,128)(2,1)}, bf16[256,1024]{1,0:T(8,128)(2,1)}, u32[]{:S(2)}, u32[]{:S(2)}) collective-permute-start(bf16[256,1024]{1,0:T(8,128)(2,1)} %pad_maximum_fusion.10.refs_4_), channel_id=1, source_target_pairs={{0,8},{8,0},{16,24},{24,16},{1,9},{9,1},{17,25},{25,17},{2,10},{10... | collective-permute-start | bytes 1572872 | tf_op jit(solution)/shard_map/ppermute | solution.py:41
  230.3 44.0 %collective-permute-start.54 = (bf16[128,2048]{1,0:T(8,128)(2,1)}, bf16[128,2048]{1,0:T(8,128)(2,1)}, u32[]{:S(2)}, u32[]{:S(2)}) collective-permute-start(bf16[128,2048]{1,0:T(8,128)(2,1)} %get-tuple-element.77), channel_id=1, source_target_pairs={{0,1},{1,0},{2,3},{3,2},{4,5},{5,4},{6,7},{7,6},{8,9},{9,8},{10,11... | collective-permute-start | bytes 1572872 | tf_op jit(solution)/shard_map/ppermute | solution.py:41
  261.7 14.5 %collective-permute-start.22 = (bf16[256,1024]{1,0:T(8,128)(2,1)}, bf16[256,1024]{1,0:T(8,128)(2,1)}, u32[]{:S(2)}, u32[]{:S(2)}) collective-permute-start(bf16[256,1024]{1,0:T(8,128)(2,1)} %slice.218), channel_id=1, source_target_pairs={{0,16},{8,24},{16,0},{24,8},{1,17},{9,25},{17,1},{25,9},{2,18},{10... | collective-permute-start | bytes 1572872 | tf_op jit(solution)/shard_map/ppermute | solution.py:41
  265.1 14.1 %collective-permute-start.38 = (bf16[128,2048]{1,0:T(8,128)(2,1)}, bf16[128,2048]{1,0:T(8,128)(2,1)}, u32[]{:S(2)}, u32[]{:S(2)}) collective-permute-start(bf16[128,2048]{1,0:T(8,128)(2,1)} %get-tuple-element.67), channel_id=1, source_target_pairs={{0,1},{1,0},{2,3},{3,2},{4,5},{5,4},{6,7},{7,6},{8,9},{9,8},{10,11... | collective-permute-start | bytes 1572872 | tf_op jit(solution)/shard_map/ppermute | solution.py:41
  268.5 50.1 %all-to-all-start.1 = ((bf16[4,32,2048]{2,1,0:T(8,128)(2,1)}), bf16[4,32,2048]{2,1,0:T(8,128)(2,1)}, u32[]{:S(2)}, u32[]{:S(2)}) async-start(bf16[4,32,2048]{2,1,0:T(8,128)(2,1)} %bitcast.15), calls=%async_computation.1 | async-start | bytes 1048576 | tf_op jit(solution)/shard_map/all_to_all | solution.py:126
  274.3 13.9 %collective-permute-start.61 = (bf16[256,1024]{1,0:T(8,128)(2,1)}, bf16[256,1024]{1,0:T(8,128)(2,1)S(1)}, u32[]{:S(2)}, u32[]{:S(2)}) collective-permute-start(bf16[256,1024]{1,0:T(8,128)(2,1)} %collective-permute-done.60.refs_6_), channel_id=1, source_target_pairs={{0,8},{8,0},{16,24},{24,16},{1,9},{9,1},{17,25},{25,17},{2,10},{10... | collective-permute-start | bytes 1572872 | tf_op jit(solution)/shard_map/ppermute | solution.py:41
  276.2 14.4 %collective-permute-start.48 = (bf16[256,512]{1,0:T(8,128)(2,1)}, bf16[256,512]{1,0:T(8,128)(2,1)S(1)}, u32[]{:S(2)}, u32[]{:S(2)}) collective-permute-start(bf16[256,512]{1,0:T(8,128)(2,1)} %pad_maximum_fusion.13.refs_0_), channel_id=1, source_target_pairs={{0,16},{8,24},{16,0},{24,8},{1,17},{9,25},{17,1},{25,9},{2,18},{10... | collective-permute-start | bytes 786440 | tf_op jit(solution)/shard_map/ppermute | solution.py:41
  286.7 24.2 %collective-permute-start.42 = (bf16[128,2048]{1,0:T(8,128)(2,1)S(1)}, bf16[128,2048]{1,0:T(8,128)(2,1)S(1)}, u32[]{:S(2)}, u32[]{:S(2)}) collective-permute-start(bf16[128,2048]{1,0:T(8,128)(2,1)S(1)} %copy-done.51), channel_id=1, source_target_pairs={{0,1},{1,0},{2,3},{3,2},{4,5},{5,4},{6,7},{7,6},{8,9},{9,8},{10,11... | collective-permute-start | bytes 1572872 | tf_op jit(solution)/shard_map/ppermute | solution.py:41
  288.2 20.5 %collective-permute-start.50 = (bf16[128,1024]{1,0:T(8,128)(2,1)S(1)}, bf16[128,1024]{1,0:T(8,128)(2,1)S(1)}, u32[]{:S(2)}, u32[]{:S(2)}) collective-permute-start(bf16[128,1024]{1,0:T(8,128)(2,1)S(1)} %get-tuple-element.132), channel_id=1, source_target_pairs={{0,1},{1,0},{2,3},{3,2},{4,5},{5,4},{6,7},{7,6},{8,9},{9,8},{10,11... | collective-permute-start | bytes 786440 | tf_op jit(solution)/shard_map/ppermute | solution.py:41
  290.6 61.4 %collective-permute-start.56 = (bf16[256,2048]{1,0:T(8,128)(2,1)}, bf16[256,2048]{1,0:T(8,128)(2,1)}, u32[]{:S(2)}, u32[]{:S(2)}) collective-permute-start(bf16[256,2048]{1,0:T(8,128)(2,1)} %constant_dynamic-update-slice_fusion.6.refs_0_), channel_id=1, source_target_pairs={{0,16},{8,24},{16,0},{24,8},{1,17},{9,25},{17,1},{25,9},{2,18},{10... | collective-permute-start | bytes 3145736 | tf_op jit(solution)/shard_map/ppermute | solution.py:41
  291.8 60.4 %collective-permute-start.40 = (bf16[256,2048]{1,0:T(8,128)(2,1)}, bf16[256,2048]{1,0:T(8,128)(2,1)}, u32[]{:S(2)}, u32[]{:S(2)}) collective-permute-start(bf16[256,2048]{1,0:T(8,128)(2,1)} %constant_dynamic-update-slice_fusion.2.refs_4_), channel_id=1, source_target_pairs={{0,16},{8,24},{16,0},{24,8},{1,17},{9,25},{17,1},{25,9},{2,18},{10... | collective-permute-start | bytes 3145736 | tf_op jit(solution)/shard_map/ppermute | solution.py:41
  292.6 23.9 %collective-permute-start.24 = (bf16[128,1536]{1,0:T(8,128)(2,1)S(1)}, bf16[128,1536]{1,0:T(8,128)(2,1)S(1)}, u32[]{:S(2)}, u32[]{:S(2)}) collective-permute-start(bf16[128,1536]{1,0:T(8,128)(2,1)S(1)} %pad_maximum_fusion.11), channel_id=1, source_target_pairs={{0,1},{1,0},{2,3},{3,2},{4,5},{5,4},{6,7},{7,6},{8,9},{9,8},{10,11... | collective-permute-start | bytes 1179656 | tf_op jit(solution)/shard_map/ppermute | solution.py:41
  310.4 40.3 %collective-permute-start.36 = (bf16[256,1024]{1,0:T(8,128)(2,1)S(1)}, bf16[256,1024]{1,0:T(8,128)(2,1)}, u32[]{:S(2)}, u32[]{:S(2)}) collective-permute-start(bf16[256,1024]{1,0:T(8,128)(2,1)S(1)} %pad_maximum_fusion.8.refs_0_), channel_id=1, source_target_pairs={{0,16},{8,24},{16,0},{24,8},{1,17},{9,25},{17,1},{25,9},{2,18},{10... | collective-permute-start | bytes 1572872 | tf_op jit(solution)/shard_map/ppermute | solution.py:41
  310.9 39.8 %collective-permute-start.35 = (bf16[256,1024]{1,0:T(8,128)(2,1)S(1)}, bf16[256,1024]{1,0:T(8,128)(2,1)}, u32[]{:S(2)}, u32[]{:S(2)}) collective-permute-start(bf16[256,1024]{1,0:T(8,128)(2,1)S(1)} %pad_maximum_fusion.8.refs_0_), channel_id=1, source_target_pairs={{0,8},{8,0},{16,24},{24,16},{1,9},{9,1},{17,25},{25,17},{2,10},{10... | collective-permute-start | bytes 1572872 | tf_op jit(solution)/shard_map/ppermute | solution.py:41
  317.2 42.7 %collective-permute-start.52 = (bf16[256,1024]{1,0:T(8,128)(2,1)}, bf16[256,1024]{1,0:T(8,128)(2,1)}, u32[]{:S(2)}, u32[]{:S(2)}) collective-permute-start(bf16[256,1024]{1,0:T(8,128)(2,1)} %pad_maximum_fusion.9.refs_4_), channel_id=1, source_target_pairs={{0,16},{8,24},{16,0},{24,8},{1,17},{9,25},{17,1},{25,9},{2,18},{10... | collective-permute-start | bytes 1572872 | tf_op jit(solution)/shard_map/ppermute | solution.py:41
  350.7 25.0 %collective-permute-start.55 = (bf16[256,2048]{1,0:T(8,128)(2,1)}, bf16[256,2048]{1,0:T(8,128)(2,1)}, u32[]{:S(2)}, u32[]{:S(2)}) collective-permute-start(bf16[256,2048]{1,0:T(8,128)(2,1)} %constant_dynamic-update-slice_fusion.6.refs_0_), channel_id=1, source_target_pairs={{0,8},{8,0},{16,24},{24,16},{1,9},{9,1},{17,25},{25,17},{2,10},{10... | collective-permute-start | bytes 3145736 | tf_op jit(solution)/shard_map/ppermute | solution.py:41
  350.7 28.8 %collective-permute-start.44 = (bf16[256,2048]{1,0:T(8,128)(2,1)}, bf16[256,2048]{1,0:T(8,128)(2,1)}, u32[]{:S(2)}, u32[]{:S(2)}) collective-permute-start(bf16[256,2048]{1,0:T(8,128)(2,1)} %constant_dynamic-update-slice_fusion.4.refs_4_), channel_id=1, source_target_pairs={{0,16},{8,24},{16,0},{24,8},{1,17},{9,25},{17,1},{25,9},{2,18},{10... | collective-permute-start | bytes 3145736 | tf_op jit(solution)/shard_map/ppermute | solution.py:41
  352.2 27.4 %collective-permute-start.57 = (bf16[256,2048]{1,0:T(8,128)(2,1)}, bf16[256,2048]{1,0:T(8,128)(2,1)}, u32[]{:S(2)}, u32[]{:S(2)}) collective-permute-start(bf16[256,2048]{1,0:T(8,128)(2,1)} %collective-permute-done.56.refs_2_), channel_id=1, source_target_pairs={{0,8},{8,0},{16,24},{24,16},{1,9},{9,1},{17,25},{25,17},{2,10},{10... | collective-permute-start | bytes 3145736 | tf_op jit(solution)/shard_map/ppermute | solution.py:41
  360.9 40.3 %collective-permute-start.39 = (bf16[256,2048]{1,0:T(8,128)(2,1)}, bf16[256,2048]{1,0:T(8,128)(2,1)}, u32[]{:S(2)}, u32[]{:S(2)}) collective-permute-start(bf16[256,2048]{1,0:T(8,128)(2,1)} %constant_dynamic-update-slice_fusion.2.refs_4_), channel_id=1, source_target_pairs={{0,8},{8,0},{16,24},{24,16},{1,9},{9,1},{17,25},{25,17},{2,10},{10... | collective-permute-start | bytes 3145736 | tf_op jit(solution)/shard_map/ppermute | solution.py:41
  362.8 38.8 %collective-permute-start.41 = (bf16[256,2048]{1,0:T(8,128)(2,1)}, bf16[256,2048]{1,0:T(8,128)(2,1)}, u32[]{:S(2)}, u32[]{:S(2)}) collective-permute-start(bf16[256,2048]{1,0:T(8,128)(2,1)} %collective-permute-done.40.refs_6_), channel_id=1, source_target_pairs={{0,8},{8,0},{16,24},{24,16},{1,9},{9,1},{17,25},{25,17},{2,10},{10... | collective-permute-start | bytes 3145736 | tf_op jit(solution)/shard_map/ppermute | solution.py:41
  364.3 88.4 %all-to-all-start.3 = ((bf16[4,64,1024]{2,1,0:T(8,128)(2,1)}), bf16[4,64,1024]{2,1,0:T(8,128)(2,1)}, u32[]{:S(2)}, u32[]{:S(2)}) async-start(bf16[4,64,1024]{2,1,0:T(8,128)(2,1)} %bitcast.21), calls=%async_computation.3 | async-start | bytes 1048576 | tf_op jit(solution)/shard_map/all_to_all | solution.py:126
  375.7 25.4 %collective-permute-start.37 = (bf16[256,1024]{1,0:T(8,128)(2,1)}, bf16[256,1024]{1,0:T(8,128)(2,1)S(1)}, u32[]{:S(2)}, u32[]{:S(2)}) collective-permute-start(bf16[256,1024]{1,0:T(8,128)(2,1)} %collective-permute-done.36.refs_2_), channel_id=1, source_target_pairs={{0,8},{8,0},{16,24},{24,16},{1,9},{9,1},{17,25},{25,17},{2,10},{10... | collective-permute-start | bytes 1572872 | tf_op jit(solution)/shard_map/ppermute | solution.py:41
  379.5 47.3 %collective-permute-start.43 = (bf16[256,2048]{1,0:T(8,128)(2,1)}, bf16[256,2048]{1,0:T(8,128)(2,1)S(1)}, u32[]{:S(2)}, u32[]{:S(2)}) collective-permute-start(bf16[256,2048]{1,0:T(8,128)(2,1)} %constant_dynamic-update-slice_fusion.4.refs_4_), channel_id=1, source_target_pairs={{0,8},{8,0},{16,24},{24,16},{1,9},{9,1},{17,25},{25,17},{2,10},{10... | collective-permute-start | bytes 3145736 | tf_op jit(solution)/shard_map/ppermute | solution.py:41
  379.5 47.3 %collective-permute-start.45 = (bf16[256,2048]{1,0:T(8,128)(2,1)}, bf16[256,2048]{1,0:T(8,128)(2,1)S(1)}, u32[]{:S(2)}, u32[]{:S(2)}) collective-permute-start(bf16[256,2048]{1,0:T(8,128)(2,1)} %collective-permute-done.44.refs_6_), channel_id=1, source_target_pairs={{0,8},{8,0},{16,24},{24,16},{1,9},{9,1},{17,25},{25,17},{2,10},{10... | collective-permute-start | bytes 3145736 | tf_op jit(solution)/shard_map/ppermute | solution.py:41
  401.1 114.8 %collective-permute-start.28 = (bf16[256,1024]{1,0:T(8,128)(2,1)S(1)}, bf16[256,1024]{1,0:T(8,128)(2,1)S(1)}, u32[]{:S(2)}, u32[]{:S(2)}) collective-permute-start(bf16[256,1024]{1,0:T(8,128)(2,1)S(1)} %copy-done.10), channel_id=1, source_target_pairs={{0,8},{8,0},{16,24},{24,16},{1,9},{9,1},{17,25},{25,17},{2,10},{10... | collective-permute-start | bytes 1572872 | tf_op jit(solution)/shard_map/ppermute | solution.py:41
  401.2 114.7 %collective-permute-start.30 = (bf16[256,1024]{1,0:T(8,128)(2,1)S(1)}, bf16[256,1024]{1,0:T(8,128)(2,1)S(1)}, u32[]{:S(2)}, u32[]{:S(2)}) collective-permute-start(bf16[256,1024]{1,0:T(8,128)(2,1)S(1)} %collective-permute-done.29.refs_2_), channel_id=1, source_target_pairs={{0,8},{8,0},{16,24},{24,16},{1,9},{9,1},{17,25},{25,17},{2,10},{10... | collective-permute-start | bytes 1572872 | tf_op jit(solution)/shard_map/ppermute | solution.py:41
  401.7 52.3 %collective-permute-start.32 = (bf16[256,1536]{1,0:T(8,128)(2,1)S(1)}, bf16[256,1536]{1,0:T(8,128)(2,1)}, u32[]{:S(2)}, u32[]{:S(2)}) collective-permute-start(bf16[256,1536]{1,0:T(8,128)(2,1)S(1)} %pad_maximum_fusion.6), channel_id=1, source_target_pairs={{0,16},{8,24},{16,0},{24,8},{1,17},{9,25},{17,1},{25,9},{2,18},{10... | collective-permute-start | bytes 2359304 | tf_op jit(solution)/shard_map/ppermute | solution.py:41
  426.8 30.4 %collective-permute-start.31 = (bf16[256,1536]{1,0:T(8,128)(2,1)S(1)}, bf16[256,1536]{1,0:T(8,128)(2,1)}, u32[]{:S(2)}, u32[]{:S(2)}) collective-permute-start(bf16[256,1536]{1,0:T(8,128)(2,1)S(1)} %pad_maximum_fusion.6), channel_id=1, source_target_pairs={{0,8},{8,0},{16,24},{24,16},{1,9},{9,1},{17,25},{25,17},{2,10},{10... | collective-permute-start | bytes 2359304 | tf_op jit(solution)/shard_map/ppermute | solution.py:41
  426.9 131.1 %collective-permute-start.66 = (f32[512,512]{1,0:T(8,128)}, f32[512,512]{1,0:T(8,128)}, u32[]{:S(2)}, u32[]{:S(2)}) collective-permute-start(f32[512,512]{1,0:T(8,128)} %get-tuple-element.101), channel_id=1, source_target_pairs={{0,1},{1,0},{2,3},{3,2},{4,5},{5,4},{6,7},{7,6},{8,9},{9,8},{10,11... | collective-permute-start | bytes 3145736 | tf_op jit(solution)/shard_map/ppermute | solution.py:41
  454.0 115.2 %collective-permute-start.71 = (f32[512,512]{1,0:T(8,128)}, f32[512,512]{1,0:T(8,128)}, u32[]{:S(2)}, u32[]{:S(2)}) collective-permute-start(f32[512,512]{1,0:T(8,128)} %fusion.9.a_ref), channel_id=1, source_target_pairs={{0,1},{1,0},{2,3},{3,2},{4,5},{5,4},{6,7},{7,6},{8,9},{9,8},{10,11... | collective-permute-start | bytes 3145736 | tf_op jit(solution)/shard_map/ppermute | solution.py:41
  457.3 23.5 %collective-permute-start.25 = (bf16[32,1024]{1,0:T(8,128)(2,1)S(1)}, bf16[32,1024]{1,0:T(8,128)(2,1)S(1)}, u32[]{:S(2)}, u32[]{:S(2)}) collective-permute-start(bf16[32,1024]{1,0:T(8,128)(2,1)S(1)} %slice.231), channel_id=1, source_target_pairs={{0,1},{1,0},{2,3},{3,2},{4,5},{5,4},{6,7},{7,6},{8,9},{9,8},{10,11... | collective-permute-start | bytes 196616 | tf_op jit(solution)/shard_map/ppermute | solution.py:41
  480.8 34.2 %collective-permute-start.33 = (bf16[256,1536]{1,0:T(8,128)(2,1)}, bf16[256,1536]{1,0:T(8,128)(2,1)S(1)}, u32[]{:S(2)}, u32[]{:S(2)}) collective-permute-start(bf16[256,1536]{1,0:T(8,128)(2,1)} %collective-permute-done.32), channel_id=1, source_target_pairs={{0,8},{8,0},{16,24},{24,16},{1,9},{9,1},{17,25},{25,17},{2,10},{10... | collective-permute-start | bytes 2359304 | tf_op jit(solution)/shard_map/ppermute | solution.py:41
  543.2 51.9 %collective-permute-start.62 = (f32[512,512]{1,0:T(8,128)}, f32[512,512]{1,0:T(8,128)S(1)}, u32[]{:S(2)}, u32[]{:S(2)}) collective-permute-start(f32[512,512]{1,0:T(8,128)} %fusion.15.a_ref), channel_id=1, source_target_pairs={{0,1},{1,0},{2,3},{3,2},{4,5},{5,4},{6,7},{7,6},{8,9},{9,8},{10,11... | collective-permute-start | bytes 3145736 | tf_op jit(solution)/shard_map/ppermute | solution.py:41
  579.7 15.4 %collective-permute-start.73 = (bf16[528,512]{1,0:T(8,128)(2,1)}, bf16[528,512]{1,0:T(8,128)(2,1)S(1)}, u32[]{:S(2)}, u32[]{:S(2)}) collective-permute-start(bf16[528,512]{1,0:T(8,128)(2,1)} %polynomial.5), channel_id=1, source_target_pairs={{0,16},{8,24},{16,0},{24,8},{1,17},{9,25},{17,1},{25,9},{2,18},{10... | collective-permute-start | bytes 1622024 | tf_op jit(solution)/shard_map/ppermute | solution.py:41
  579.7 26.6 %collective-permute-start.72 = (bf16[528,512]{1,0:T(8,128)(2,1)}, bf16[528,512]{1,0:T(8,128)(2,1)S(1)}, u32[]{:S(2)}, u32[]{:S(2)}) collective-permute-start(bf16[528,512]{1,0:T(8,128)(2,1)} %polynomial.5), channel_id=1, source_target_pairs={{0,8},{8,0},{16,24},{24,16},{1,9},{9,1},{17,25},{25,17},{2,10},{10... | collective-permute-start | bytes 1622024 | tf_op jit(solution)/shard_map/ppermute | solution.py:41
  579.9 28.5 %collective-permute-start.76 = (bf16[528,512]{1,0:T(8,128)(2,1)S(1)}, bf16[528,512]{1,0:T(8,128)(2,1)S(1)}, u32[]{:S(2)}, u32[]{:S(2)}) collective-permute-start(bf16[528,512]{1,0:T(8,128)(2,1)S(1)} %get-tuple-element.105), channel_id=1, source_target_pairs={{0,16},{8,24},{16,0},{24,8},{1,17},{9,25},{17,1},{25,9},{2,18},{10... | collective-permute-start | bytes 1622024 | tf_op jit(solution)/shard_map/ppermute | solution.py:41
  582.6 45.9 %collective-permute-start.75 = (bf16[528,512]{1,0:T(8,128)(2,1)S(1)}, bf16[528,512]{1,0:T(8,128)(2,1)S(1)}, u32[]{:S(2)}, u32[]{:S(2)}) collective-permute-start(bf16[528,512]{1,0:T(8,128)(2,1)S(1)} %get-tuple-element.105), channel_id=1, source_target_pairs={{0,8},{8,0},{16,24},{24,16},{1,9},{9,1},{17,25},{25,17},{2,10},{10... | collective-permute-start | bytes 1622024 | tf_op jit(solution)/shard_map/ppermute | solution.py:41
  595.1 20.4 %collective-permute-start.69 = (bf16[528,512]{1,0:T(8,128)(2,1)S(1)}, bf16[528,512]{1,0:T(8,128)(2,1)S(1)}, u32[]{:S(2)}, u32[]{:S(2)}) collective-permute-start(bf16[528,512]{1,0:T(8,128)(2,1)S(1)} %get-tuple-element.106), channel_id=1, source_target_pairs={{0,16},{8,24},{16,0},{24,8},{1,17},{9,25},{17,1},{25,9},{2,18},{10... | collective-permute-start | bytes 1622024 | tf_op jit(solution)/shard_map/ppermute | solution.py:41
  595.1 13.9 %collective-permute-start.74 = (bf16[528,512]{1,0:T(8,128)(2,1)S(1)}, bf16[528,512]{1,0:T(8,128)(2,1)S(1)}, u32[]{:S(2)}, u32[]{:S(2)}) collective-permute-start(bf16[528,512]{1,0:T(8,128)(2,1)S(1)} %collective-permute-done.73), channel_id=1, source_target_pairs={{0,8},{8,0},{16,24},{24,16},{1,9},{9,1},{17,25},{25,17},{2,10},{10... | collective-permute-start | bytes 1622024 | tf_op jit(solution)/shard_map/ppermute | solution.py:41
  606.4 22.7 %collective-permute-start.64 = (bf16[528,512]{1,0:T(8,128)(2,1)}, bf16[528,512]{1,0:T(8,128)(2,1)S(1)}, u32[]{:S(2)}, u32[]{:S(2)}) collective-permute-start(bf16[528,512]{1,0:T(8,128)(2,1)} %polynomial.3), channel_id=1, source_target_pairs={{0,16},{8,24},{16,0},{24,8},{1,17},{9,25},{17,1},{25,9},{2,18},{10... | collective-permute-start | bytes 1622024 | tf_op jit(solution)/shard_map/ppermute | solution.py:41
  608.4 20.7 %collective-permute-start.77 = (bf16[528,512]{1,0:T(8,128)(2,1)S(1)}, bf16[528,512]{1,0:T(8,128)(2,1)S(1)}, u32[]{:S(2)}, u32[]{:S(2)}) collective-permute-start(bf16[528,512]{1,0:T(8,128)(2,1)S(1)} %collective-permute-done.76), channel_id=1, source_target_pairs={{0,8},{8,0},{16,24},{24,16},{1,9},{9,1},{17,25},{25,17},{2,10},{10... | collective-permute-start | bytes 1622024 | tf_op jit(solution)/shard_map/ppermute | solution.py:41
  609.0 21.8 %collective-permute-start.68 = (bf16[528,512]{1,0:T(8,128)(2,1)S(1)}, bf16[528,512]{1,0:T(8,128)(2,1)S(1)}, u32[]{:S(2)}, u32[]{:S(2)}) collective-permute-start(bf16[528,512]{1,0:T(8,128)(2,1)S(1)} %get-tuple-element.106), channel_id=1, source_target_pairs={{0,8},{8,0},{16,24},{24,16},{1,9},{9,1},{17,25},{25,17},{2,10},{10... | collective-permute-start | bytes 1622024 | tf_op jit(solution)/shard_map/ppermute | solution.py:41
  615.5 15.3 %collective-permute-start.70 = (bf16[528,512]{1,0:T(8,128)(2,1)S(1)}, bf16[528,512]{1,0:T(8,128)(2,1)S(1)}, u32[]{:S(2)}, u32[]{:S(2)}) collective-permute-start(bf16[528,512]{1,0:T(8,128)(2,1)S(1)} %collective-permute-done.69), channel_id=1, source_target_pairs={{0,8},{8,0},{16,24},{24,16},{1,9},{9,1},{17,25},{25,17},{2,10},{10... | collective-permute-start | bytes 1622024 | tf_op jit(solution)/shard_map/ppermute | solution.py:41
  628.5 26.2 %collective-permute-start.63 = (bf16[528,512]{1,0:T(8,128)(2,1)S(1)}, bf16[528,512]{1,0:T(8,128)(2,1)S(1)}, u32[]{:S(2)}, u32[]{:S(2)}) collective-permute-start(bf16[528,512]{1,0:T(8,128)(2,1)S(1)} %copy-done.43), channel_id=1, source_target_pairs={{0,8},{8,0},{16,24},{24,16},{1,9},{9,1},{17,25},{25,17},{2,10},{10... | collective-permute-start | bytes 1622024 | tf_op jit(solution)/shard_map/ppermute | solution.py:41
  629.1 25.6 %collective-permute-start.65 = (bf16[528,512]{1,0:T(8,128)(2,1)S(1)}, bf16[528,512]{1,0:T(8,128)(2,1)S(1)}, u32[]{:S(2)}, u32[]{:S(2)}) collective-permute-start(bf16[528,512]{1,0:T(8,128)(2,1)S(1)} %collective-permute-done.64), channel_id=1, source_target_pairs={{0,8},{8,0},{16,24},{24,16},{1,9},{9,1},{17,25},{25,17},{2,10},{10... | collective-permute-start | bytes 1622024 | tf_op jit(solution)/shard_map/ppermute | solution.py:41
  (103 other events, 1160.2 us)

commit v2 on v1

v2 whole, which is shorter than its diff:
```python
import functools
import math

import jax
import jax.numpy as jnp
from jax import lax
from jax.experimental import pallas as pl
from jax.experimental.pallas import tpu as pltpu
from jax.sharding import PartitionSpec as P

HEAD_DIM = 64
NS_STEPS = 5
EPS = 1e-05
THETA = 130000.0
MOMENTUM = 0.95
COEF_A = 3.4445
COEF_B = -4.775
COEF_C = 2.0315
RATE = 0.5
BF = jnp.bfloat16
F32 = jnp.float32
VMEM_LIMIT = 56 * 1024 * 1024


def dot(left, right, ldim=1, rdim=0):
    return lax.dot_general(
        left, right, (((ldim,), (rdim,)), ((), ())), preferred_element_type=F32
    )


def params():
    return pltpu.CompilerParams(vmem_limit_bytes=VMEM_LIMIT)


def cost(flops, nbytes):
    return pl.CostEstimate(flops=int(flops), bytes_accessed=int(nbytes), transcendentals=0)


def swap(value, axis, bit):
    size = lax.axis_size(axis)
    return lax.ppermute(value, axis, [(i, i ^ bit) for i in range(size)])


def later(value, *others):
    return lax.optimization_barrier((value, others))[0]


def ctx_two(value):
    return [value, swap(value, "ctx", 2)]


def ctx_four(two):
    value, far = two
    return [value, swap(value, "ctx", 1), far, swap(far, "ctx", 1)]


def ctx_parts(value):
    return ctx_four(ctx_two(value))


def pair():
    return lax.axis_size("fsdp") == 2


def f_scatter_cols(value):
    size = lax.axis_size("fsdp")
    rows, width = value.shape
    part = width // size
    if size == 2:
        own = lax.axis_index("fsdp")
        mine = lax.dynamic_slice_in_dim(value, own * part, part, 1)
        other = lax.dynamic_slice_in_dim(value, (1 - own) * part, part, 1)
        return jnp.concatenate([mine, swap(other, "fsdp", 1)], axis=0)
    cut = jnp.swapaxes(value.reshape(rows, size, part), 0, 1)
    return lax.all_to_all(cut, "fsdp", 0, 0, tiled=True).reshape(size * rows, part)


def f_gather_cols(value):
    size = lax.axis_size("fsdp")
    rows = value.shape[0] // size
    if size == 2:
        own = lax.axis_index("fsdp")
        mine, other = value[:rows], swap(value[rows:], "fsdp", 1)
        return jnp.concatenate(
            [jnp.where(own == 0, mine, other), jnp.where(own == 0, other, mine)], axis=1
        )
    cut = lax.all_to_all(value.reshape(size, rows, -1), "fsdp", 0, 0, tiled=True)
    return jnp.swapaxes(cut, 0, 1).reshape(rows, -1)


def f_gather_rows(value):
    if pair():
        return jnp.concatenate([value, swap(value, "fsdp", 1)], axis=0)
    return lax.all_gather(value, "fsdp", axis=0, tiled=True)


def f_reduce_rows(value):
    size = lax.axis_size("fsdp")
    rows = value.shape[0] // size
    if size == 2:
        return value[:rows].astype(F32) + swap(value[rows:].astype(BF), "fsdp", 1).astype(F32)
    return lax.psum_scatter(value.astype(F32), "fsdp", scatter_dimension=0, tiled=True)


def flip(value):
    half = value.shape[0] // 2
    return jnp.concatenate([value[half:], value[:half]], axis=0)


def f_all(value):
    if pair():
        return value + flip(swap(value, "fsdp", 1))
    return lax.psum(value, "fsdp")


def f_reduce_list(parts):
    rows = parts[0].shape[0] // 2
    sent = jnp.concatenate([p[rows:].astype(BF) for p in parts], axis=1)
    return jnp.concatenate([p[:rows] for p in parts], axis=1) + swap(sent, "fsdp", 1).astype(F32)


def z_shift(value, k):
    size = lax.axis_size("tp")
    return lax.ppermute(value, "tp", [(i, (i + k) % size) for i in range(size)])


def z_shifts():
    size = lax.axis_size("tp")
    return sorted(range(1, size), key=lambda k: -min(k, size - k))


def by_quarter(value):
    size, groups = lax.axis_size("tp"), lax.axis_size("fsdp")
    rows, width = value.shape
    part = rows // (size * groups)
    cut = jnp.swapaxes(value.reshape(groups, size, part, width), 0, 1)
    return cut.reshape(size, groups * part, width)


def own_quarter(value):
    return lax.dynamic_index_in_dim(by_quarter(value), lax.axis_index("tp"), 0, keepdims=False)


def z_reduce(value):
    sent = by_quarter(value.astype(BF))
    return jnp.sum(lax.all_to_all(sent, "tp", 0, 0, tiled=True).astype(F32), axis=0)


def z_gather(value):
    size, groups = lax.axis_size("tp"), lax.axis_size("fsdp")
    rows, width = value.shape
    full = lax.all_gather(value, "tp", axis=0)
    full = jnp.swapaxes(full.reshape(size, groups, rows // groups, width), 0, 1)
    return full.reshape(size * rows, width)


def z_reduce_slow(value):
    size, me = lax.axis_size("tp"), lax.axis_index("tp")
    cut = by_quarter(value)
    total = lax.dynamic_index_in_dim(cut, me, 0, keepdims=False).astype(F32)
    for k in z_shifts():
        sent = lax.dynamic_index_in_dim(cut, (me + k) % size, 0, keepdims=False).astype(BF)
        total = total + z_shift(sent, k).astype(F32)
    return total


def z_gather_groups_slow(value, wait=()):
    size, groups = lax.axis_size("tp"), lax.axis_size("fsdp")
    rows, width = value.shape
    full = z_gather_slow(value, wait).reshape(size, groups, rows // groups, width)
    return jnp.swapaxes(full, 0, 1).reshape(size * rows, width)


def z_gather_slow(value, wait=()):
    size, me = lax.axis_size("tp"), lax.axis_index("tp")
    by_place = {k: later(z_shift(value, k), wait) for k in z_shifts()}
    by_place[0] = value
    ordered = []
    for at in range(size):
        chosen = value
        for k in z_shifts():
            chosen = jnp.where((me - k) % size == at, by_place[k], chosen)
        ordered.append(chosen)
    return jnp.concatenate(ordered, axis=0)


def all_sum(value, axes):
    for axis in axes:
        size = lax.axis_size(axis)
        if axis == "tp":
            value = value + sum(z_shift(value, k) for k in z_shifts())
        else:
            bit = 1
            while bit < size:
                value = value + swap(value, axis, bit)
                bit *= 2
    return value


def rope_tables(position, width):
    half = HEAD_DIM // 2
    freq = THETA ** (-(jnp.arange(half, dtype=F32) * 2.0 / HEAD_DIM))
    angle = position[:, None] * freq[None, :]
    repeat = width // half
    return jnp.tile(jnp.cos(angle), (1, repeat)), jnp.tile(jnp.sin(angle), (1, repeat))


def first_half(shape):
    lane = lax.broadcasted_iota(jnp.int32, shape, 1)
    return (lane & (HEAD_DIM - 1)) < HEAD_DIM // 2


def rotate(values, cosine, sine):
    half = HEAD_DIM // 2
    turned = jnp.where(
        first_half(values.shape), -jnp.roll(values, -half, 1), jnp.roll(values, half, 1)
    )
    return values * cosine + turned * sine


def unrotate(grads, cosine, sine):
    half = HEAD_DIM // 2
    scaled = grads * sine
    back = jnp.where(
        first_half(grads.shape), jnp.roll(scaled, -half, 1), -jnp.roll(scaled, half, 1)
    )
    return grads * cosine + back


def head_probs(query, keys, allowed, scale):
    scores = jnp.where(allowed, dot(query, keys, 1, 1) * scale, -1e30)
    top = jnp.max(scores, axis=1, keepdims=True)
    expo = jnp.exp(scores - top)
    return expo / jnp.sum(expo, axis=1, keepdims=True)


def attention_kernel(scale, q_ref, k_ref, v_ref, qi_ref, qs_ref, ki_ref, ks_ref, o_ref):
    allowed = (ks_ref[...] == qs_ref[...]) & (ki_ref[...] <= qi_ref[...])
    query, keys, values = q_ref[...], k_ref[...], v_ref[...]
    lane = lax.broadcasted_iota(jnp.int32, query.shape, 1)
    outs = []
    for head in range(2):
        mine = (lane >= HEAD_DIM) == (head == 1)
        prob = head_probs(jnp.where(mine, query, 0), keys, allowed, scale)
        outs.append(dot(prob.astype(BF), values))
    o_ref[...] = jnp.where(lane < HEAD_DIM, outs[0], outs[1]).astype(BF)


def attention_grad_kernel(
    scale, q_ref, k_ref, v_ref, g_ref, qi_ref, qs_ref, ki_ref, ks_ref, dq_ref, dk_ref, dv_ref
):
    allowed = (ks_ref[...] == qs_ref[...]) & (ki_ref[...] <= qi_ref[...])
    query, keys, values, grads = q_ref[...], k_ref[...], v_ref[...], g_ref[...]
    lane = lax.broadcasted_iota(jnp.int32, query.shape, 1)
    wide = lax.broadcasted_iota(jnp.int32, keys.shape, 1)
    dqs, dks, dvs = [], [], []
    for head in range(2):
        mine = (lane >= HEAD_DIM) == (head == 1)
        prob = head_probs(jnp.where(mine, query, 0), keys, allowed, scale)
        dprob = dot(jnp.where(mine, grads, 0), values, 1, 1)
        delta = jnp.sum(prob * dprob, axis=1, keepdims=True)
        dscore = (prob * (dprob - delta)).astype(BF)
        dqs.append(dot(dscore, keys))
        dks.append(dot(dscore, query, 0, 0))
        dvs.append(dot(prob.astype(BF), grads, 0, 0))
    low, wlow = lane < HEAD_DIM, wide < HEAD_DIM
    dq_ref[...] = jnp.where(low, dqs[0], dqs[1]) * scale
    dk_ref[...] = (jnp.where(wlow, dks[0], dks[1]) * scale).astype(BF)
    dv_ref[...] = jnp.where(wlow, dvs[0], dvs[1]).astype(BF)


def attention_specs(rows, keys):
    def col(n):
        return pl.BlockSpec((n, 2 * HEAD_DIM), lambda h: (0, h))

    def whole(shape):
        return pl.BlockSpec(shape, lambda h: (0, 0))

    marks = [whole((rows, 1)), whole((rows, 1)), whole((1, keys)), whole((1, keys))]
    return col, marks


def attention(query, keys, values, marks):
    rows, width = query.shape
    count = keys.shape[0]
    col, mark_specs = attention_specs(rows, count)
    return pl.pallas_call(
        functools.partial(attention_kernel, 1.0 / math.sqrt(HEAD_DIM)),
        grid=(width // (2 * HEAD_DIM),),
        in_specs=[col(rows), col(count), col(count)] + mark_specs,
        out_specs=col(rows),
        out_shape=jax.ShapeDtypeStruct((rows, width), BF),
        compiler_params=params(),
        cost_estimate=cost(8 * rows * count * width, 4 * count * width),
        name="attention",
    )(query, keys, values, *marks)


def attention_grad(query, keys, values, grads, marks):
    rows, width = query.shape
    count = keys.shape[0]
    col, mark_specs = attention_specs(rows, count)
    return pl.pallas_call(
        functools.partial(attention_grad_kernel, 1.0 / math.sqrt(HEAD_DIM)),
        grid=(width // (2 * HEAD_DIM),),
        in_specs=[col(rows), col(count), col(count), col(rows)] + mark_specs,
        out_specs=[col(rows), col(count), col(count)],
        out_shape=[
            jax.ShapeDtypeStruct((rows, width), F32),
            jax.ShapeDtypeStruct((count, width), BF),
            jax.ShapeDtypeStruct((count, width), BF),
        ],
        compiler_params=params(),
        cost_estimate=cost(20 * rows * count * width, 8 * count * width),
        name="attention_grad",
    )(query, keys, values, grads, *marks)


def smem():
    return pl.BlockSpec(memory_space=pltpu.SMEM)


def units_kernel(x_ref, wg_ref, wu_ref, own_ref, sent_ref):
    for k, w_ref in enumerate((wg_ref, wu_ref)):
        part = dot(x_ref[...], w_ref[...])
        own_ref[k] = part
        sent_ref[k] = part.astype(BF)


def units(x, wgate, wup, at, count, tile=512):
    rows, depth = x.shape
    steps = count // tile
    weight = pl.BlockSpec((depth, tile), lambda n: (0, at * steps + n))
    out = pl.BlockSpec((2, rows, tile), lambda n: (0, 0, n))
    return pl.pallas_call(
        units_kernel,
        grid=(steps,),
        in_specs=[pl.BlockSpec((rows, depth), lambda n: (0, 0)), weight, weight],
        out_specs=[out, out],
        out_shape=[
            jax.ShapeDtypeStruct((2, rows, count), F32),
            jax.ShapeDtypeStruct((2, rows, count), BF),
        ],
        compiler_params=params(),
        cost_estimate=cost(1, 1),
        name="units",
    )(x, wgate, wup)


def hidden_kernel(paired, first, own_ref, got_ref, dh_ref, dgot_ref, wg_ref, wu_ref, *refs):
    if first:
        out_ref, acc_ref = refs
    else:
        before_ref, out_ref, acc_ref = refs
    half = dh_ref.shape[0] // 2

    def total(own, got):
        if not paired:
            return own
        got = got.astype(F32)
        return own + jnp.concatenate([got[half:], got[:half]], axis=0)

    gate = total(own_ref[0], got_ref[0])
    upper = total(own_ref[1], got_ref[1])
    dhid = total(dh_ref[...], dgot_ref[...])
    sigma = jax.nn.sigmoid(gate)
    silu = gate * sigma
    dgate = (dhid * upper * sigma * (1.0 + gate * (1.0 - sigma))).astype(BF)
    dup = (dhid * silu).astype(BF)
    out_ref[0] = (silu * upper).astype(BF)
    out_ref[1] = dgate
    out_ref[2] = dup
    grad = dot(dgate, wg_ref[...], 1, 1) + dot(dup, wu_ref[...], 1, 1)

    @pl.when(pl.program_id(0) == 0)
    def _():
        acc_ref[...] = grad if first else grad + before_ref[...]

    @pl.when(pl.program_id(0) > 0)
    def _():
        acc_ref[...] += grad


def hidden_units(own, got, dhid, dgot, wgate, wup, at, before=None, tile=512):
    _, rows, count = own.shape
    depth = wgate.shape[0]
    steps = count // tile
    weight = pl.BlockSpec((depth, tile), lambda n: (0, at * steps + n))
    trio = pl.BlockSpec((2, rows, tile), lambda n: (0, 0, n))
    lanes = pl.BlockSpec((rows, tile), lambda n: (0, at * steps + n))
    total = pl.BlockSpec((rows, depth), lambda n: (0, 0))
    args = [own, got, dhid, dgot, wgate, wup] + ([] if before is None else [before])
    return pl.pallas_call(
        functools.partial(hidden_kernel, pair(), before is None),
        grid=(steps,),
        in_specs=[trio, trio, lanes, lanes, weight, weight] + [total] * (len(args) - 6),
        out_specs=[pl.BlockSpec((3, rows, tile), lambda n: (0, 0, n)), total],
        out_shape=[
            jax.ShapeDtypeStruct((3, rows, count), BF),
            jax.ShapeDtypeStruct((rows, depth), F32),
        ],
        compiler_params=params(),
        cost_estimate=cost(1, 1),
        name="hidden_units",
    )(*args)


def joined(parts):
    return jnp.concatenate([r[...].reshape(r.shape[-2:]) for r in parts], axis=0)


def moved(total, mom_ref, g_ref, m_ref, l_ref):
    mom = MOMENTUM * mom_ref[...] + total
    g_ref[...] = total
    m_ref[...] = mom
    l_ref[...] = (total + MOMENTUM * mom).astype(BF)


def add_gram(gram_ref, look_ref, by_columns, hit, first):
    half = gram_ref.shape[1]

    def three():
        if by_columns:
            low, high = look_ref[:, :half], look_ref[:, half:]
        else:
            low, high = look_ref[:half, :], look_ref[half:, :]
        dim = 0 if by_columns else 1
        return [dot(x, y, dim, dim) for x, y in ((low, low), (low, high), (high, high))]

    @pl.when(jnp.logical_and(hit, first))
    def _():
        for k, value in enumerate(three()):
            gram_ref[k] = value

    @pl.when(jnp.logical_and(hit, jnp.logical_not(first)))
    def _():
        for k, value in enumerate(three()):
            gram_ref[k] += value


def gram_spec(size):
    half = size // 2
    return (
        pl.BlockSpec((3, half, half), lambda *at: (0, 0, 0)),
        jax.ShapeDtypeStruct((3, half, half), F32),
    )


def weight_grad_kernel(nl, nr, by_columns, base, filled, place_ref, *refs):
    lefts, rights = refs[:nl], refs[nl : nl + nr]
    mom_ref, g_ref, m_ref, l_ref, gram_ref = refs[nl + nr], *refs[-4:]
    tall, wide = g_ref.shape
    moved(dot(joined(lefts), joined(rights), 0, 0), mom_ref, g_ref, m_ref, l_ref)
    i, j = pl.program_id(0), pl.program_id(1)
    outer, inner = (j, i) if by_columns else (i, j)
    size = 2 * gram_ref.shape[1]
    count = (wide if by_columns else tall) // size

    if filled:

        @pl.when(jnp.logical_and(i == 0, j == 0))
        def _():
            gram_ref[...] = refs[nl + nr + 4][...]

    for k in range(count):
        at = pl.ds(k * size, size)
        look = l_ref.at[:, at] if by_columns else l_ref.at[at, :]
        add_gram(gram_ref, look, by_columns, base + outer * count + k == place_ref[0], inner == 0)


def weight_grad(
    place, lefts, rights, mom, size, by_columns, tile, planes=(None, None), span=None, into=None
):
    height, width = mom.shape
    part, parts = span or (0, 1)
    tm, tn = min(tile[0], height), min(tile[1], width)
    grid = [height // tm, width // tn]
    axis = 1 if by_columns else 0
    grid[axis] //= parts
    start = [0, 0]
    start[axis] = part * grid[axis]
    out = pl.BlockSpec((tm, tn), lambda i, j: (start[0] + i, start[1] + j))
    tok = sum(v.shape[-2] for v in lefts)

    def specs(values, plane, lanes, place_of):
        if plane is None:
            return [pl.BlockSpec((v.shape[0], lanes), lambda i, j: (0, place_of(i, j))) for v in values]
        return [
            pl.BlockSpec((1, v.shape[1], lanes), lambda i, j: (plane, 0, place_of(i, j)))
            for v in values
        ]

    whole_gram, gram_shape = gram_spec(size)
    in_specs = [smem()]
    in_specs += specs(lefts, planes[0], tm, lambda i, j: i)
    in_specs += specs(rights, planes[1], tn, lambda i, j: j)
    in_specs += [out]
    args = [place, *lefts, *rights, mom]
    aliases = {}
    if into is not None:
        aliases = {len(args) + k: k for k in range(3)}
        in_specs += [pl.BlockSpec(memory_space=pl.ANY)] * 3 + [whole_gram]
        args += list(into)
    blocks = (width if by_columns else height) // size // parts
    return pl.pallas_call(
        functools.partial(
            weight_grad_kernel, len(lefts), len(rights), by_columns, part * blocks, into is not None
        ),
        grid=tuple(grid),
        in_specs=in_specs,
        out_specs=[out, out, out, whole_gram],
        out_shape=[
            jax.ShapeDtypeStruct((height, width), F32),
            jax.ShapeDtypeStruct((height, width), F32),
            jax.ShapeDtypeStruct((height, width), BF),
            gram_shape,
        ],
        input_output_aliases=aliases,
        compiler_params=params(),
        cost_estimate=cost(2 * tok * height * width // parts, 14 * height * width // parts),
        name="weight_grad",
    )(*args)


def attention_weights_kernel(count, place_ref, *refs):
    ones, grads, attns, mids = (refs[k * count : (k + 1) * count] for k in range(4))
    refs = refs[4 * count :]
    moms, outs, gram_ref = refs[:4], refs[4:16], refs[16]
    first = pl.program_id(0) == 0
    left = joined(ones)
    width = moms[0].shape[1]
    for k in range(3):
        right = jnp.concatenate([r[:, k * width : (k + 1) * width] for r in grads], axis=0)
        moved(dot(left, right, 0, 0), moms[k], *outs[3 * k : 3 * k + 3])
        add_gram(gram_ref, outs[3 * k + 2], True, place_ref[0] == k, first)
    moved(dot(joined(attns), joined(mids), 0, 0), moms[3], *outs[9:12])
    add_gram(gram_ref, outs[11], False, place_ref[0] == 3, first)


def attention_weights(place, ones, grads, attns, mids, moms, tile=256):
    share, width = moms[0].shape
    tile = min(tile, share)

    def cols(v):
        return pl.BlockSpec((v.shape[0], tile), lambda i: (0, i))

    def whole(v):
        return pl.BlockSpec(v.shape, lambda i: (0, 0))

    tall = pl.BlockSpec((tile, width), lambda i: (i, 0))
    wide = pl.BlockSpec((width, tile), lambda i: (0, i))
    gram, gram_shape = gram_spec(width)
    shapes = []
    for mom in moms:
        shapes += [jax.ShapeDtypeStruct(mom.shape, kind) for kind in (F32, F32, BF)]
    out = pl.pallas_call(
        functools.partial(attention_weights_kernel, len(ones)),
        grid=(share // tile,),
        in_specs=[smem()]
        + [cols(v) for v in ones]
        + [whole(v) for v in grads]
        + [whole(v) for v in attns]
        + [cols(v) for v in mids]
        + [tall, tall, tall, wide],
        out_specs=[tall] * 9 + [wide] * 3 + [gram],
        out_shape=shapes + [gram_shape],
        compiler_params=params(),
        cost_estimate=cost(8 * len(ones) * ones[0].shape[0] * share * width, 56 * share * width),
        name="attention_weights",
    )(place, *ones, *grads, *attns, *mids, *moms)
    return out[:3], out[3:6], out[6:9], out[9:12], out[12]


def mlp_weights_kernel(count, base, filled, place_ref, *refs):
    twos, hids, dgates, dups, dys = (refs[k * count : (k + 1) * count] for k in range(5))
    refs = refs[5 * count :]
    moms, refs = refs[:3], refs[3:]
    before, refs = (refs[9:12], refs[12:]) if filled else (None, refs)
    outs, grams = refs[:9], refs[9:]
    j, i = pl.program_id(0), pl.program_id(1)

    if filled:

        @pl.when(jnp.logical_and(i == 0, j == 0))
        def _():
            for gram_ref, old in zip(grams, before):
                gram_ref[...] = old[...]

    two = joined(twos)
    hit, first = base + j == place_ref[0], i == 0
    moved(dot(two, joined(dgates), 0, 0), moms[0], *outs[:3])
    add_gram(grams[0], outs[2], True, hit, first)
    moved(dot(two, joined(dups), 0, 0), moms[1], *outs[3:6])
    add_gram(grams[1], outs[5], True, hit, first)
    moved(dot(joined(hids), joined(dys), 0, 0), moms[2], *outs[6:9])
    add_gram(grams[2], outs[8], False, hit, first)


def mlp_weights(place, twos, trios, dys, moms, size, span, into, tile=512):
    share, width = moms[0].shape
    part, parts = span
    blocks = width // size // parts
    tile = min(tile, share)

    def cols(v):
        return pl.BlockSpec((v.shape[0], tile), lambda j, i: (0, i))

    def plane(v, k):
        return pl.BlockSpec((1, v.shape[1], size), lambda j, i: (k, 0, j))

    tall = pl.BlockSpec((tile, size), lambda j, i: (i, part * blocks + j))
    wide = pl.BlockSpec((size, tile), lambda j, i: (part * blocks + j, i))
    gram, gram_shape = gram_spec(size)
    shapes = []
    for mom in moms:
        shapes += [jax.ShapeDtypeStruct(mom.shape, kind) for kind in (F32, F32, BF)]
    in_specs = [smem()] + [cols(v) for v in twos]
    for k in range(3):
        in_specs += [plane(v, k) for v in trios]
    in_specs += [cols(v) for v in dys] + [tall, tall, wide]
    args = [place, *twos, *trios, *trios, *trios, *dys, *moms]
    aliases = {len(args) + k: k for k in range(9)}
    in_specs += [pl.BlockSpec(memory_space=pl.ANY)] * 9 + [gram] * 3
    args += [v for out in into for v in out[:3]] + [out[3] for out in into]
    tok = sum(v.shape[0] for v in twos)
    out = pl.pallas_call(
        functools.partial(mlp_weights_kernel, len(twos), part * blocks, True),
        grid=(blocks, share // tile),
        in_specs=in_specs,
        out_specs=[tall] * 6 + [wide] * 3 + [gram] * 3,
        out_shape=shapes + [gram_shape] * 3,
        input_output_aliases=aliases,
        compiler_params=params(),
        cost_estimate=cost(6 * tok * share * width // parts, 42 * share * width // parts),
        name="mlp_weights",
    )(*args)
    return [(*out[3 * k : 3 * k + 3], out[9 + k]) for k in range(3)]


def polynomial_kernel(a_ref, b_ref, out_ref, full_ref):
    size, half = full_ref.shape[0], full_ref.shape[0] // 2
    corner = a_ref[1] + b_ref[1]
    full_ref[:half, :half] = a_ref[0] + b_ref[0]
    full_ref[:half, half:] = corner
    full_ref[half:, :half] = corner.T
    full_ref[half:, half:] = a_ref[2] + b_ref[2]
    row = lax.broadcasted_iota(jnp.int32, (size, size), 0)
    column = lax.broadcasted_iota(jnp.int32, (size, size), 1)
    eye = row == column

    def split(full):
        only = jnp.where(eye, full, 0.0)
        return (
            jnp.where(eye, 0.0, full),
            jnp.sum(only, axis=1, keepdims=True),
            jnp.sum(only, axis=0, keepdims=True),
        )

    def times(left, right):
        loff, lcol, lrow = left
        roff, rcol, rrow = right
        full = dot(loff.astype(BF), roff.astype(BF)) + lcol * roff + loff * rrow
        off, dcol, drow = split(full)
        return off, dcol + lcol * rcol, drow + lrow * rrow

    def mix(coefs, first, second, shift):
        off = coefs[0] * first[0] + coefs[1] * second[0]
        dcol = coefs[0] * first[1] + coefs[1] * second[1] + shift
        drow = coefs[0] * first[2] + coefs[1] * second[2] + shift
        return off, dcol, drow

    gram = split(full_ref[...])
    norm = jnp.sqrt(jnp.sum(gram[2])) + 1e-07
    inverse = 1.0 / (norm * norm)
    gram = tuple(part * inverse for part in gram)
    total = None
    for step in range(NS_STEPS):
        square = times(gram, gram)
        factor = mix((COEF_B, COEF_C), gram, square, COEF_A)
        total = factor if total is None else times(factor, total)
        if step < NS_STEPS - 1:
            gram = times(factor, times(factor, gram))
    weight = -RATE / norm
    off = (total[0] * weight).astype(BF)
    out_ref[:half] = off[:half, :half]
    out_ref[half:size] = off[:half, half:]
    out_ref[size : size + half] = off[half:, half:]
    diagonal = total[2] * weight
    high = diagonal.astype(BF).astype(F32)
    low = diagonal - high
    line = lax.broadcasted_iota(jnp.int32, (16, half), 0)
    tail = jnp.zeros((16, half), F32)
    for k, part in enumerate((high[:, :half], high[:, half:], low[:, :half], low[:, half:])):
        tail = jnp.where(line == k, part, tail)
    out_ref[size + half :] = tail.astype(BF)


def polynomial(a, b):
    half = a.shape[1]
    size = 2 * half
    return pl.pallas_call(
        polynomial_kernel,
        in_specs=[pl.BlockSpec(memory_space=pltpu.VMEM)] * 2,
        out_specs=pl.BlockSpec(memory_space=pltpu.VMEM),
        out_shape=jax.ShapeDtypeStruct((3 * half + 16, half), BF),
        scratch_shapes=[pltpu.VMEM((size, size), F32)],
        compiler_params=params(),
        cost_estimate=cost(34 * size**3, 10 * size * size),
        name="polynomial",
    )(a, b)


def unpack(packed, factor_ref, column):
    half = packed.shape[1]
    corner = packed[half : 2 * half]
    factor_ref[:half, :half] = packed[:half]
    factor_ref[:half, half:] = corner
    factor_ref[half:, :half] = corner.astype(F32).T.astype(BF)
    factor_ref[half:, half:] = packed[2 * half : 3 * half]
    ends = packed[3 * half :].astype(F32)
    line = jnp.concatenate([ends[0:1] + ends[2:3], ends[1:2] + ends[3:4]], axis=1)
    if not column:
        return line
    size = 2 * half
    eye = lax.broadcasted_iota(jnp.int32, (size, size), 0) == lax.broadcasted_iota(
        jnp.int32, (size, size), 1
    )
    return jnp.sum(jnp.where(eye, line, 0.0), axis=1, keepdims=True)


def stepped(look_ref, w_ref, o_ref, factor, diagonal, by_columns):
    look = look_ref[...]
    step = dot(look, factor) if by_columns else dot(factor, look)
    o_ref[...] = w_ref[...].astype(F32) + (step + look.astype(F32) * diagonal)


def update_kernel(by_columns, me_ref, q_ref, l_ref, w_ref, o_ref, factor_ref, line_ref):
    @pl.when(pl.program_id(1) == 0)
    def _():
        line_ref[...] = unpack(q_ref[0], factor_ref, not by_columns)

    stepped(l_ref, w_ref, o_ref, factor_ref[...], line_ref[...], by_columns)


def update(factors, look, weight, by_columns, me):
    _, packed, half = factors.shape
    size = 2 * half
    height, width = weight.shape
    if by_columns:
        tile = min(1024, height)
        grid = (width // size, height // tile)
        spec = pl.BlockSpec((tile, size), lambda b, i, me_ref: (i, b))
    else:
        tile = min(1024, width)
        grid = (height // size, width // tile)
        spec = pl.BlockSpec((size, tile), lambda b, i, me_ref: (b, i))
    return pl.pallas_call(
        functools.partial(update_kernel, by_columns),
        grid_spec=pltpu.PrefetchScalarGridSpec(
            num_scalar_prefetch=1,
            grid=grid,
            in_specs=[
                pl.BlockSpec((1, packed, half), lambda b, i, me_ref: (b ^ me_ref[0], 0, 0)),
                spec,
                spec,
            ],
            out_specs=spec,
            scratch_shapes=[
                pltpu.VMEM((size, size), BF),
                pltpu.VMEM((1, size) if by_columns else (size, 1), F32),
            ],
        ),
        out_shape=jax.ShapeDtypeStruct(weight.shape, F32),
        compiler_params=params(),
        cost_estimate=cost(2 * size * height * width, 8 * height * width),
        name="update",
    )(me, factors, look, weight)


def attention_update_kernel(me_ref, *refs):
    qs, looks, weights, outs = refs[:4], refs[4:8], refs[8:12], refs[12:16]
    factor_ref, row_ref, column_ref = refs[16:]

    @pl.when(pl.program_id(0) == 0)
    def _():
        for k in range(3):
            row_ref[k] = unpack(qs[k][0], factor_ref.at[k], False)
        column_ref[...] = unpack(qs[3][0], factor_ref.at[3], True)

    for k in range(3):
        stepped(looks[k], weights[k], outs[k], factor_ref[k], row_ref[k], True)
    stepped(looks[3], weights[3], outs[3], factor_ref[3], column_ref[...], False)


def attention_update(factors, looks, weights, me, tile=256):
    _, packed, half = factors.shape
    size = 2 * half
    share, width = weights[0].shape
    tile = min(tile, share)
    tall = pl.BlockSpec((tile, width), lambda i, me_ref: (i, 0))
    wide = pl.BlockSpec((width, tile), lambda i, me_ref: (0, i))

    def factor(k):
        return pl.BlockSpec((1, packed, half), lambda i, me_ref: (me_ref[0] ^ k, 0, 0))

    specs = [tall, tall, tall, wide]
    return pl.pallas_call(
        attention_update_kernel,
        grid_spec=pltpu.PrefetchScalarGridSpec(
            num_scalar_prefetch=1,
            grid=(share // tile,),
            in_specs=[factor(k) for k in range(4)] + specs + specs,
            out_specs=specs,
            scratch_shapes=[
                pltpu.VMEM((4, size, size), BF),
                pltpu.VMEM((3, 1, size), F32),
                pltpu.VMEM((size, 1), F32),
            ],
        ),
        out_shape=[jax.ShapeDtypeStruct(w.shape, F32) for w in weights],
        compiler_params=params(),
        cost_estimate=cost(8 * size * share * width, 32 * share * width),
        name="attention_update",
    )(me, factors, factors, factors, factors, *looks, *weights)


def body(
    tokens,
    out_grad,
    segment_start,
    norm_attn,
    norm_mlp,
    w_query,
    w_key,
    w_value,
    w_out,
    w_gate,
    w_up,
    w_down,
    mom_query,
    mom_key,
    mom_value,
    mom_out,
    mom_gate,
    mom_up,
    mom_down,
):
    rows = tokens.shape[1]
    me = lax.axis_index("ctx")
    groups = lax.axis_size("fsdp")
    place = jnp.stack([me, me]).astype(jnp.int32)
    width = w_query.shape[1]
    depth = tokens.shape[2]
    low_in = tokens[0]
    inputs = low_in.astype(F32)
    gain_one, gain_two = norm_attn.astype(F32), norm_mlp.astype(F32)

    spread = f_scatter_cols(low_in)
    inv_one = lax.rsqrt(jnp.mean(inputs * inputs, axis=1, keepdims=True) + EPS)
    inv_spread = f_gather_rows(inv_one)
    scaled = (spread.astype(F32) * gain_one).astype(BF)
    one_spread = (spread.astype(F32) * inv_spread * gain_one).astype(BF)

    partial = [dot(scaled, w) for w in (w_query, w_key, w_value)]
    if pair():
        qkv = f_reduce_list(partial)
    else:
        qkv = jnp.concatenate([f_reduce_rows(part) for part in partial], axis=1)
    qkv = later(qkv * inv_one, inv_spread)
    dy_spread = f_scatter_cols(out_grad[0])
    one_two, dy_two = ctx_two(one_spread), ctx_two(dy_spread)

    starts = segment_start[0]
    chunks = [(me ^ j) * rows for j in range(lax.axis_size("ctx"))]
    key_start = jnp.concatenate([lax.dynamic_slice_in_dim(starts, o, rows) for o in chunks])
    key_index = jnp.concatenate([o + jnp.arange(rows, dtype=jnp.int32) for o in chunks])
    query_start, query_index = key_start[:rows], key_index[:rows]
    cosine, sine = rope_tables((query_index - query_start).astype(F32), width)
    marks = (query_index[:, None], query_start[:, None], key_index[None], key_start[None])

    query = rotate(qkv[:, :width], cosine, sine).astype(BF)
    kv_own = jnp.concatenate(
        [rotate(qkv[:, width : 2 * width], cosine, sine), qkv[:, 2 * width :]], axis=1
    ).astype(BF)
    kv = jnp.concatenate(ctx_parts(kv_own), axis=0)
    keys, values = kv[:, :width], kv[:, width:]
    query = later(query, dy_spread)
    attn = attention(query, keys, values, marks)
    attn_rows = f_gather_rows(attn)

    dhid = dot(dy_spread, w_down, 1, 1)
    attn_two = ctx_two(attn_rows)
    attn_rows = later(attn_rows, dhid)

    own_in = own_quarter(spread).astype(F32)
    own_inv = own_quarter(inv_spread)
    own_dy = own_quarter(dy_spread).astype(F32)

    middle = own_in + later(z_reduce(dot(attn_rows, w_out)), dy_two[1], attn_two[1])
    squares = f_all(jnp.sum(middle * middle, axis=1, keepdims=True))
    inv_two = lax.rsqrt(squares * (1.0 / depth) + EPS)
    own_two = (middle * inv_two * gain_two).astype(BF)
    if pair():
        dhid_got = swap(later(dhid.astype(BF), own_two), "fsdp", 1)
    else:
        dhid_got = dhid = lax.psum(dhid, "fsdp")
    two_spread = later(z_gather(own_two), dhid_got)
    two_two = ctx_two(two_spread)

    halves = 2
    count = w_gate.shape[1] // halves
    parts = [units(two_spread, w_gate, w_up, p, count) for p in range(halves)]
    if pair():
        got = [swap(sent, "fsdp", 1) for _, sent in parts]
        owns = [own for own, _ in parts]
    else:
        owns = [lax.psum(own, "fsdp") for own, _ in parts]
        got = owns
    owns[0] = later(owns[0], owns[1], two_two[1], one_two[1])
    trios, dx_two = [], None
    for p in range(halves):
        trio, dx_two = hidden_units(
            owns[p], got[p], dhid, dhid_got, w_gate, w_up, p, before=dx_two
        )
        trios.append(trio)

    trio_twos = [ctx_two(trio) for trio in trios]
    grad_two = z_reduce_slow(dx_two)
    trio_alls = [ctx_four(later(trio_twos[0], dx_two)), ctx_four(later(trio_twos[1], grad_two))]
    two_all, dy_all = ctx_four(later(two_two, dx_two)), ctx_four(later(dy_two, dx_two))
    scaled_two = middle * inv_two
    weighted = grad_two * gain_two
    mean = f_all(jnp.sum(weighted * scaled_two, axis=1, keepdims=True)) * (1.0 / depth)
    grad_middle = own_dy + inv_two * (weighted - scaled_two * mean)
    own_mid = later(grad_middle.astype(BF), trio_twos[0][1], trio_twos[1][1])
    span = (0, halves)
    gate_out = weight_grad(
        later(place, own_mid), two_all, trio_alls[0], mom_gate, width, True, (1024, 512), (None, 1),
        span=span,
    )
    mid_spread = z_gather_groups_slow(own_mid, gate_out)
    grad_attn = f_reduce_rows(dot(mid_spread, w_out, 1, 1)).astype(BF)

    dquery, dkeys, dvalues = attention_grad(query, keys, values, grad_attn, marks)
    dkv = jnp.concatenate([dkeys, dvalues], axis=1)
    up_out = weight_grad(
        later(place, dkv), two_all, trio_alls[0], mom_up, width, True, (1024, 512), (None, 2),
        span=span,
    )
    got_dkv = later(swap(dkv[2 * rows :], "ctx", 2), up_out)
    far = dkv[: 2 * rows].astype(F32) + got_dkv.astype(F32)
    near = far[:rows] + swap(far[rows:].astype(BF), "ctx", 1).astype(F32)
    dqkv = jnp.concatenate(
        [
            unrotate(dquery, cosine, sine),
            unrotate(near[:, :width], cosine, sine),
            near[:, width:],
        ],
        axis=1,
    ).astype(BF)
    dqkv_rows = f_gather_rows(dqkv)

    one_all = ctx_four(one_two)
    down_out = weight_grad(
        later(place, dqkv), trio_alls[0], dy_all, mom_down, width, False, (512, 1024), (0, None),
        span=span,
    )
    gate_out, up_out, down_out = mlp_weights(
        later(place, dqkv_rows), two_all, trio_alls[1], dy_all, (mom_gate, mom_up, mom_down),
        width, (1, halves), (gate_out, up_out, down_out),
    )
    g_gate, m_gate, l_gate, gram_gate = gate_out
    g_up, m_up, l_up, gram_up = up_out
    g_down, m_down, l_down, gram_down = down_out

    mid_all, attn_all = ctx_parts(mid_spread), ctx_four(attn_two)
    dqkv_all = ctx_parts(dqkv_rows)
    query_out, key_out, value_out, out_out, gram_attn = attention_weights(
        later(place, g_down), one_all, dqkv_all, attn_all, mid_all,
        (mom_query, mom_key, mom_value, mom_out),
    )
    g_query, m_query, l_query = query_out
    g_key, m_key, l_key = key_out
    g_value, m_value, l_value = value_out
    g_out, m_out, l_out = out_out

    trios, dqkv_rows = later((trios, dqkv_rows), down_out[3])
    out_part = sum(
        dot(trio[0], w_down[p * count : (p + 1) * count]) for p, trio in enumerate(trios)
    )
    result = f_gather_cols((middle + z_reduce(out_part)).astype(BF))
    result = z_gather_slow(result)

    dx_one = (
        dot(dqkv_rows[:, :width], w_query, 1, 1)
        + dot(dqkv_rows[:, width : 2 * width], w_key, 1, 1)
        + dot(dqkv_rows[:, 2 * width :], w_value, 1, 1)
    )
    grad_one = z_reduce(dx_one)
    scaled_one = own_in * own_inv
    weighted = grad_one * gain_one
    mean = f_all(jnp.sum(weighted * scaled_one, axis=1, keepdims=True)) * (1.0 / depth)
    input_grad = grad_middle + own_inv * (weighted - scaled_one * mean)
    input_grad = z_gather_slow(f_gather_cols(input_grad.astype(BF))).astype(F32)

    gain_parts = jnp.stack(
        [
            jnp.sum(dx_one * one_spread.astype(F32), axis=0),
            jnp.sum(dx_two * two_spread.astype(F32), axis=0),
        ]
    )
    gain_sums = all_sum(gain_parts, ("ctx", "tp"))
    grad_gain_one = gain_sums[0] / gain_one
    grad_gain_two = gain_sums[1] / gain_two

    if pair():
        even = lax.axis_index("fsdp") == 0
        kept = jnp.where(even, gram_down, gram_gate)
        sent = jnp.where(even, gram_gate, gram_down)
        both = later((kept, swap(sent, "fsdp", 1)), g_value, result, input_grad)
        q_own = polynomial(*both)
        got_attn = swap(gram_attn, "fsdp", 1)
        both = later((gram_up, swap(gram_up, "fsdp", 1)), q_own, gain_sums)
        q_up = polynomial(*both)
        q_other = swap(q_own, "fsdp", 1)
        q_down = ctx_two(jnp.where(even, q_own, q_other))
        q_gate = ctx_two(jnp.where(even, q_other, q_own))
        q_up = ctx_two(q_up)
        both = later((gram_attn, got_attn), q_up[0])
        q_attn = ctx_two(polynomial(*both))
    else:
        grams = lax.psum(jnp.stack([gram_down, gram_gate, gram_up, gram_attn]), "fsdp")
        none = jnp.zeros_like(gram_up)
        q_down, q_gate, q_up, q_attn = (ctx_two(polynomial(grams[k], none)) for k in range(4))
        got_attn = grams
    q_down, q_gate, q_up, q_attn = (
        jnp.stack(ctx_four(q)) for q in (q_down, q_gate, q_up, q_attn)
    )
    ctx_place = place[:1]
    new_down = update(q_down, l_down, w_down, False, ctx_place)
    new_gate = update(q_gate, l_gate, w_gate, True, ctx_place)
    new_up = update(q_up, l_up, w_up, True, ctx_place)

    new_query, new_key, new_value, new_out = attention_update(
        q_attn, (l_query, l_key, l_value, l_out), (w_query, w_key, w_value, w_out), ctx_place
    )

    return (
        result[None],
        input_grad[None],
        grad_gain_one,
        grad_gain_two,
        g_query,
        g_key,
        g_value,
        g_out,
        g_gate,
        g_up,
        g_down,
        m_query,
        m_key,
        m_value,
        m_out,
        m_gate,
        m_up,
        m_down,
        new_query,
        new_key,
        new_value,
        new_out,
        new_gate,
        new_up,
        new_down,
    )


def solution(mesh):
    act = P("fsdp", "ctx", None)
    col, row, vec = P("fsdp", "tp"), P("tp", "fsdp"), P("fsdp")
    seven = (col, col, col, row, col, col, row)
    in_specs = (act, act, P("fsdp", None), vec, vec) + seven + seven
    out_specs = (act, act, vec, vec) + seven + seven + seven
    return jax.shard_map(body, mesh=mesh, in_specs=in_specs, out_specs=out_specs, check_vma=False)
```

time: 681 us -> 509 us (0.75)
  the two profiles are of different devices: /device:TPU:0 before, /device:TPU:21 now
where the time goes in v2:
time: 509 us; the launch traced here: 499 us
  Pallas kernels  169 us (33%)
  waiting for transfers between devices  136 us (27%)
  starting transfers between devices  108 us (21%)
  local copies, waits for them, and re-layouts  31.4 us (6%)
  other arithmetic  29.8 us (6%)
  blocking collectives  11.7 us (2%)
  matrix products  11 us (2%)
    ppermute x62, waiting for transfers between devices, swap(): return lax.ppermute(value, axis, [(i, i ^ bit) for i in range(size)])  96.8 us
    ppermute x62, starting transfers between devices, swap(): return lax.ppermute(value, axis, [(i, i ^ bit) for i in range(size)])  76.5 us
    pallas_call x3, Pallas kernels, polynomial(): pl.pallas_call(polynomial_kernel, in_specs=[pl.BlockSpec(memory_space=plt...  30 us
    pallas_call x1, Pallas kernels, mlp_weights(): pl.pallas_call(functools.partial(mlp_weights_kernel, len(twos), part * bl...  27.1 us
    pallas_call x3, Pallas kernels, update(): pl.pallas_call(functools.partial(update_kernel, by_columns), grid_spec=pl...  26.2 us
    pallas_call x3, Pallas kernels, weight_grad(): pl.pallas_call(functools.partial(weight_grad_kernel, len(lefts), len(righ...  24.7 us
    ppermute x15, waiting for transfers between devices, z_shift(): return lax.ppermute(value, 'tp', [(i, (i + k) % size) for i in range(size)])  21.1 us
    all_to_all x3, waiting for transfers between devices, z_reduce(): lax.all_to_all(sent, 'tp', 0, 0, tiled=True).astype(F32)  17.9 us
  transfers between devices with their start and end apart: 80, of which 31 were waited for; matrix products, arithmetic and copies ran while one was open for 9% of the time, Pallas kernels for 22%

profile of v2, /device:TPU:21, one launch (start us, length us, event | category | flops | bytes accessed | tf_op | source)
XLA Modules:
  0.0 499.4 jit_solution(12654312368421492778)
XLA Ops:
  4.7 1.8 dynamic-slice_bitcast_fusion.1
  17.1 5.9 %collective-permute-done.1 = bf16[128,1536]{1,0:T(8,128)(2,1)S(1)} collective-permute-done((bf16[128,1536]{1,0:T(8,128)(2,1)S(1)}, bf16[128,1536]{1,0:T(8,128)(2,1)S(1)}, u32[]{:S(2)}, u32[]{:S(2)}) %collective-permute-start.1) | collective-permute-done | bytes 393248 | tf_op jit(solution)/shard_map/ppermute | solution.py:41
  24.8 2.0 collective-permute-start.4
  26.8 3.8 collective-permute-done.5
  30.7 2.6 collective-permute-start.6
  36.5 6.0 %attention.1 = bf16[128,512]{1,0:T(8,128)(2,1)} custom-call(bf16[128,512]{1,0:T(8,128)(2,1)} %get-tuple-element.112.q_ref, bf16[512,512]{1,0:T(8,128)(2,1)} %get-tuple-element.215.k_ref, bf16[512,512]{1,0:T(8,128)(2,1)} %get-tuple-element.214.v_ref, s32[128,1]{1,0:T(8,128)} %iota_add_fusion.qi_ref, s32[128,1]{1,0:T(8,128)} %copy.66.qs_ref, ...), custom_call_target="tpu_custom_call" | custom-call | flops 268435456 | bytes 1048576 | tf_op jit(solution)/shard_map/attention/pallas_call | solution.py:287
  43.8 2.9 fusion.79
  49.3 4.7 all-to-all-start
  56.4 8.6 %all-to-all-done = bf16[4,64,1024]{2,1,0:T(8,128)(2,1)S(1)} async-done(((bf16[4,64,1024]{2,1,0:T(8,128)(2,1)}), bf16[4,64,1024]{2,1,0:T(8,128)(2,1)S(1)}, u32[]{:S(2)}, u32[]{:S(2)}) %all-to-all-start) | async-done | bytes 524320 | tf_op jit(solution)/shard_map/all_to_all | solution.py:146
  66.1 5.7 %collective-permute-done.9.refs_10_ = bf16[256,512]{1,0:T(8,128)(2,1)} collective-permute-done((bf16[256,512]{1,0:T(8,128)(2,1)S(1)}, bf16[256,512]{1,0:T(8,128)(2,1)}, u32[]{:S(2)}, u32[]{:S(2)}) %collective-permute-start.9) | collective-permute-done | bytes 262176 | tf_op jit(solution)/shard_map/ppermute | solution.py:41
  76.9 11.7 %all-gather = bf16[256,1024]{1,0:T(8,128)(2,1)S(1)} all-gather(bf16[64,1024]{1,0:T(8,128)(2,1)S(1)} %multiply_convert_fusion), channel_id=2, replica_groups=mesh['ctx'=4,'tp'=4,'fsdp'=2] {'tp'}, dimensions={0}, use_global_device_ids=true | all-gather | bytes 655360 | tf_op jit(solution)/shard_map/all_gather | solution.py:152
  89.5 7.6 %collective-permute-done.11.dgot_ref = bf16[256,2048]{1,0:T(8,128)(2,1)S(1)} collective-permute-done((bf16[256,2048]{1,0:T(8,128)(2,1)}, bf16[256,2048]{1,0:T(8,128)(2,1)S(1)}, u32[]{:S(2)}, u32[]{:S(2)}) %collective-permute-start.11) | collective-permute-done | bytes 1048608 | tf_op jit(solution)/shard_map/ppermute | solution.py:41
  97.1 5.0 %units.2 = (f32[2,256,1024]{2,1,0:T(8,128)}, bf16[2,256,1024]{2,1,0:T(8,128)(2,1)}) custom-call(bf16[256,1024]{1,0:T(8,128)(2,1)} %bitcast.153, bf16[1024,2048]{1,0:T(8,128)(2,1)} %w_ref.3, bf16[1024,2048]{1,0:T(8,128)(2,1)} %w_ref.4), custom_call_target="tpu_custom_call" | custom-call | flops 1 | bytes 1 | tf_op jit(solution)/shard_map/units/pallas_call | solution.py:335
  105.2 4.3 units.3
  109.5 3.0 collective-permute-done.13.refs_2_
  112.5 11.2 %collective-permute-done.12.refs_2_ = bf16[256,1024]{1,0:T(8,128)(2,1)S(1)} collective-permute-done((bf16[256,1024]{1,0:T(8,128)(2,1)S(1)}, bf16[256,1024]{1,0:T(8,128)(2,1)S(1)}, u32[]{:S(2)}, u32[]{:S(2)}) %collective-permute-start.12) | collective-permute-done | bytes 524320 | tf_op jit(solution)/shard_map/ppermute | solution.py:41
  124.7 5.7 %hidden_units.2 = (bf16[3,256,1024]{2,1,0:T(8,128)(2,1)}, f32[256,1024]{1,0:T(8,128)}) custom-call(f32[2,256,1024]{2,1,0:T(8,128)} %get-tuple-element.119.own_ref, bf16[2,256,1024]{2,1,0:T(8,128)(2,1)} %copy-done.43, f32[256,2048]{1,0:T(8,128)} %get-tuple-element.275.dh_ref, bf16[256,2048]{1,0:T(8,128)(2,1)} %copy-done.28, bf16[1024,2048]{1,0:T(8,128)(2,1)} %w_ref.3, ...), custom_call_target="tpu_custom_call" | custom-call | flops 1 | bytes 1 | tf_op jit(solution)/shard_map/hidden_units/pallas_call | solution.py:393
  131.1 18.7 %collective-permute-done.15.got_ref = bf16[2,256,1024]{2,1,0:T(8,128)(2,1)S(1)} collective-permute-done((bf16[2,256,1024]{2,1,0:T(8,128)(2,1)S(1)}, bf16[2,256,1024]{2,1,0:T(8,128)(2,1)S(1)}, u32[]{:S(2)}, u32[]{:S(2)}) %collective-permute-start.15) | collective-permute-done | bytes 1048608 | tf_op jit(solution)/shard_map/ppermute | solution.py:41
  150.8 6.2 %hidden_units.3 = (bf16[3,256,1024]{2,1,0:T(8,128)(2,1)}, f32[256,1024]{1,0:T(8,128)}) custom-call(f32[2,256,1024]{2,1,0:T(8,128)} %get-tuple-element.118.own_ref, bf16[2,256,1024]{2,1,0:T(8,128)(2,1)} %copy-done.45, f32[256,2048]{1,0:T(8,128)} %get-tuple-element.275.dh_ref, bf16[256,2048]{1,0:T(8,128)(2,1)} %copy-done.28, bf16[1024,2048]{1,0:T(8,128)(2,1)} %w_ref.3, ...), custom_call_target="tpu_custom_call" | custom-call | flops 1 | bytes 1 | tf_op jit(solution)/shard_map/hidden_units/pallas_call | solution.py:393
  158.2 3.1 collective-permute-done.20.refs_6_.refs_2_
  161.2 12.5 %collective-permute-start.25 = (bf16[3,256,1024]{2,1,0:T(8,128)(2,1)S(1)}, bf16[3,256,1024]{2,1,0:T(8,128)(2,1)}, u32[]{:S(2)}, u32[]{:S(2)}) collective-permute-start(bf16[3,256,1024]{2,1,0:T(8,128)(2,1)S(1)} %copy-done.5), channel_id=1, source_target_pairs={{0,8},{8,0},{16,24},{24,16},{1,9},{9,1},{17,25},{25,17},{2,10},{10... | collective-permute-start | bytes 4718600 | tf_op jit(solution)/shard_map/ppermute | solution.py:41
  178.4 7.3 %collective-permute-done.16 = bf16[64,1024]{1,0:T(8,128)(2,1)S(1)} collective-permute-done((bf16[64,1024]{1,0:T(8,128)(2,1)S(1)}, bf16[64,1024]{1,0:T(8,128)(2,1)S(1)}, u32[]{:S(2)}, u32[]{:S(2)}) %collective-permute-start.16) | collective-permute-done | bytes 131104 | tf_op jit(solution)/shard_map/ppermute | solution.py:124
  186.3 2.6 collective-permute-done.17
  192.8 2.2 collective-permute-start.23
  195.1 1.9 collective-permute-start.24
  197.3 3.2 collective-permute-start.28
  202.1 8.2 %weight_grad.3 = (f32[1024,2048]{1,0:T(8,128)}, f32[1024,2048]{1,0:T(8,128)}, bf16[1024,2048]{1,0:T(8,128)(2,1)}, f32[3,256,256]{2,1,0:T(8,128)}) custom-call(s32[2]{0:T(128)} %pad_add_fusion.2.place_ref, bf16[256,1024]{1,0:T(8,128)(2,1)} %bitcast.155, bf16[256,1024]{1,0:T(8,128)(2,1)} %copy-done.15, bf16[256,1024]{1,0:T(8,128)(2,1)} %copy-done.13, ...), custom_call_target="tpu_custom_call" | custom-call | flops 2147483648 | bytes 14680064 | tf_op jit(solution)/shard_map/weight_grad/pallas_call | solution.py:505
  212.8 3.6 collective-permute-done.29
  217.1 7.0 %attention_grad.1 = (f32[128,512]{1,0:T(8,128)}, bf16[512,512]{1,0:T(8,128)(2,1)}, bf16[512,512]{1,0:T(8,128)(2,1)}) custom-call(bf16[128,512]{1,0:T(8,128)(2,1)} %get-tuple-element.112.q_ref, bf16[512,512]{1,0:T(8,128)(2,1)} %get-tuple-element.215.k_ref, bf16[512,512]{1,0:T(8,128)(2,1)} %get-tuple-element.214.v_ref, bf16[128,512]{1,0:T(8,128)(2,1)} %fusion.31.g_ref, ...), custom_call_target="tpu_custom_call" | custom-call | flops 671088640 | bytes 2097152 | tf_op jit(solution)/shard_map/attention_grad/pallas_call | solution.py:303
  226.8 8.3 %weight_grad.4 = (f32[1024,2048]{1,0:T(8,128)}, f32[1024,2048]{1,0:T(8,128)}, bf16[1024,2048]{1,0:T(8,128)(2,1)}, f32[3,256,256]{2,1,0:T(8,128)}) custom-call(s32[2]{0:T(128)} %pad_add_fusion.2.place_ref, bf16[256,1024]{1,0:T(8,128)(2,1)} %bitcast.156, bf16[256,1024]{1,0:T(8,128)(2,1)} %copy-done.15, bf16[256,1024]{1,0:T(8,128)(2,1)} %copy-done.13, ...), custom_call_target="tpu_custom_call" | custom-call | flops 2147483648 | bytes 14680064 | tf_op jit(solution)/shard_map/weight_grad/pallas_call | solution.py:505
  235.1 2.2 collective-permute-done.30
  239.1 3.6 collective-permute-start.31
  249.6 8.2 %weight_grad.5 = (f32[2048,1024]{1,0:T(8,128)}, f32[2048,1024]{1,0:T(8,128)}, bf16[2048,1024]{1,0:T(8,128)(2,1)}, f32[3,256,256]{2,1,0:T(8,128)}) custom-call(s32[2]{0:T(128)} %pad_add_fusion.2.place_ref, bf16[3,256,1024]{2,1,0:T(8,128)(2,1)} %get-tuple-element.159.refs_4_.refs_0_, bf16[3,256,1024]{2,1,0:T(8,128)(2,1)} %collective-permute-done.25.refs_5_.refs_1_, ...), custom_call_target="tpu_custom_call" | custom-call | flops 2147483648 | bytes 14680064 | tf_op jit(solution)/shard_map/weight_grad/pallas_call | solution.py:505
  261.3 27.1 %mlp_weights.1 = (f32[1024,2048]{1,0:T(8,128)}, f32[1024,2048]{1,0:T(8,128)}, bf16[1024,2048]{1,0:T(8,128)(2,1)}, f32[1024,2048]{1,0:T(8,128)}, f32[1024,2048]{1...) custom-call(s32[2]{0:T(128)} %pad_add_fusion.2.place_ref, ...), custom_call_target="tpu_custom_call", output_to_operand_aliasing={{0}: (24, {}), {1}: (25, {}), {2}: (26, {}), {3}: (27, {}),... | custom-call | flops 6442450944 | bytes 44040192 | tf_op jit(solution)/shard_map/mlp_weights/pallas_call | solution.py:626
  292.4 5.3 %all-to-all-start.2 = ((bf16[4,64,1024]{2,1,0:T(8,128)(2,1)}), bf16[4,64,1024]{2,1,0:T(8,128)(2,1)S(1)}, u32[]{:S(2)}, u32[]{:S(2)}) async-start(bf16[4,64,1024]{2,1,0:T(8,128)(2,1)} %bitcast.56), calls=%async_computation.2 | async-start | bytes 1048576 | tf_op jit(solution)/shard_map/all_to_all | solution.py:146
  297.8 2.6 fusion
  300.7 1.8 fusion.7
  303.5 2.2 collective-permute-start.49
  305.8 3.1 all-to-all-done.2
  308.9 6.7 %all-to-all-start.1 = ((bf16[4,64,1024]{2,1,0:T(8,128)(2,1)}), bf16[4,64,1024]{2,1,0:T(8,128)(2,1)S(1)}, u32[]{:S(2)}, u32[]{:S(2)}) async-start(bf16[4,64,1024]{2,1,0:T(8,128)(2,1)} %bitcast.50), calls=%async_computation.1 | async-start | bytes 1048576 | tf_op jit(solution)/shard_map/all_to_all | solution.py:146
  315.6 2.7 broadcast_select_fusion.2
  320.3 6.2 %all-to-all-done.1 = bf16[4,64,1024]{2,1,0:T(8,128)(2,1)S(1)} async-done(((bf16[4,64,1024]{2,1,0:T(8,128)(2,1)}), bf16[4,64,1024]{2,1,0:T(8,128)(2,1)S(1)}, u32[]{:S(2)}, u32[]{:S(2)}) %all-to-all-start.1) | async-done | bytes 524320 | tf_op jit(solution)/shard_map/all_to_all | solution.py:146
  332.9 3.0 collective-permute-start.45
  338.0 4.3 collective-permute-start.51
  342.3 4.6 collective-permute-start.52
  347.0 2.6 collective-permute-done.38
  350.9 4.7 collective-permute-done.40
  355.6 3.6 collective-permute-start.56
  360.4 2.6 collective-permute-start.60
  363.1 13.0 %collective-permute-done.54.refs_6_ = bf16[256,1536]{1,0:T(8,128)(2,1)S(1)} collective-permute-done((bf16[256,1536]{1,0:T(8,128)(2,1)S(1)}, bf16[256,1536]{1,0:T(8,128)(2,1)S(1)}, u32[]{:S(2)}, u32[]{:S(2)}) %collective-permute-start.54) | collective-permute-done | bytes 786464 | tf_op jit(solution)/shard_map/ppermute | solution.py:41
  376.1 2.1 collective-permute-start.55
  378.3 3.1 collective-permute-start.63
  384.2 17.7 %attention_weights.1 = (f32[1024,512]{1,0:T(8,128)}, f32[1024,512]{1,0:T(8,128)}, bf16[1024,512]{1,0:T(8,128)(2,1)}, f32[1024,512]{1,0:T(8,128)}, f32[1024,512]{...) custom-call(s32[2]{0:T(128)} %pad_add_fusion.2.place_ref, ...), custom_call_target="tpu_custom_call" | custom-call | flops 4294967296 | bytes 29360128 | tf_op jit(solution)/shard_map/attention_weights/pallas_call | solution.py:556
  401.9 10.0 %polynomial.3 = bf16[784,256]{1,0:T(8,128)(2,1)} custom-call(f32[3,256,256]{2,1,0:T(8,128)} %get-tuple-element.180.a_ref, f32[3,256,256]{2,1,0:T(8,128)} %collective-permute-done.63.b_ref), custom_call_target="tpu_custom_call" | custom-call | flops 4563402752 | bytes 2621440 | tf_op jit(solution)/shard_map/polynomial/pallas_call | solution.py:701
  413.3 2.9 collective-permute-done.62.b_ref
  417.5 10.1 %polynomial.4 = bf16[784,256]{1,0:T(8,128)(2,1)} custom-call(f32[3,256,256]{2,1,0:T(8,128)} %get-tuple-element.182.a_ref, f32[3,256,256]{2,1,0:T(8,128)} %collective-permute-done.62.b_ref), custom_call_target="tpu_custom_call" | custom-call | flops 4563402752 | bytes 2621440 | tf_op jit(solution)/shard_map/polynomial/pallas_call | solution.py:701
  432.3 4.9 collective-permute-done.72
  437.2 4.4 collective-permute-done.61.b_ref
  442.5 9.9 %polynomial.5 = bf16[784,256]{1,0:T(8,128)(2,1)} custom-call(f32[3,256,256]{2,1,0:T(8,128)} %get-tuple-element.184.a_ref, f32[3,256,256]{2,1,0:T(8,128)} %copy-done.79), custom_call_target="tpu_custom_call" | custom-call | flops 4563402752 | bytes 2621440 | tf_op jit(solution)/shard_map/polynomial/pallas_call | solution.py:701
  455.2 2.5 collective-permute-start.70
  459.1 8.9 %update.4 = f32[1024,2048]{1,0:T(8,128)} custom-call(s32[1]{0:T(128)} %bitcast.42.me_ref, bf16[4,784,256]{2,1,0:T(8,128)(2,1)} %pad_maximum_fusion.2.q_ref, bf16[1024,2048]{1,0:T(8,128)(2,1)} %get-tuple-element.195.l_ref, bf16[1024,2048]{1,0:T(8,128)(2,1)} %w_ref.4), custom_call_target="tpu_custom_call" | custom-call | flops 2147483648 | bytes 16777216 | tf_op jit(solution)/shard_map/update/pallas_call | solution.py:757
  471.3 8.7 %update.5 = f32[2048,1024]{1,0:T(8,128)} custom-call(s32[1]{0:T(128)} %bitcast.42.me_ref, bf16[4,784,256]{2,1,0:T(8,128)(2,1)} %pad_maximum_fusion.3.q_ref, bf16[2048,1024]{1,0:T(8,128)(2,1)} %get-tuple-element.196.l_ref, bf16[2048,1024]{1,0:T(8,128)(2,1)} %w_ref.5), custom_call_target="tpu_custom_call" | custom-call | flops 2147483648 | bytes 16777216 | tf_op jit(solution)/shard_map/update/pallas_call | solution.py:757
  480.0 8.6 %update.3 = f32[1024,2048]{1,0:T(8,128)} custom-call(s32[1]{0:T(128)} %bitcast.42.me_ref, bf16[4,784,256]{2,1,0:T(8,128)(2,1)} %pad_maximum_fusion.1.q_ref, bf16[1024,2048]{1,0:T(8,128)(2,1)} %get-tuple-element.194.l_ref, bf16[1024,2048]{1,0:T(8,128)(2,1)} %w_ref.3), custom_call_target="tpu_custom_call" | custom-call | flops 2147483648 | bytes 16777216 | tf_op jit(solution)/shard_map/update/pallas_call | solution.py:757
  490.0 9.0 %attention_update.1 = (f32[1024,512]{1,0:T(8,128)}, f32[1024,512]{1,0:T(8,128)}, f32[1024,512]{1,0:T(8,128)}, f32[512,1024]{1,0:T(8,128)}) custom-call(s32[1]{0:T(128)} %bitcast.42.me_ref, bf16[4,784,256]{2,1,0:T(8,128)(2,1)} %pad_maximum_fusion.refs_0_.refs_1_.refs_2_.refs_3_, bf16[4,784,256]{2,1,0:T(8,128)(2,1)} %pad_maximum_fusion.refs_0_.refs_1_.refs_2_.refs_3_, ...), custom_call_target="tpu_custom_call" | custom-call | flops 2147483648 | bytes 16777216 | tf_op jit(solution)/shard_map/attention_update/pallas_call | solution.py:807
  (403 shorter events, 106.3 us)
Async XLA Ops:
  1.9 7.2 %collective-permute-start = (bf16[128,1024]{1,0:T(8,128)(2,1)S(1)}, bf16[128,1024]{1,0:T(8,128)(2,1)S(1)}, u32[]{:S(2)}, u32[]{:S(2)}) collective-permute-start(bf16[128,1024]{1,0:T(8,128)(2,1)S(1)} %get-tuple-element.239), channel_id=1, source_target_pairs={{0,1},{1,0},{2,3},{3,2},{4,5},{5,4},{6,7},{7,6},{8,9},{9,8},{10,11... | collective-permute-start | bytes 786440 | tf_op jit(solution)/shard_map/ppermute | solution.py:41
  4.4 8.9 %collective-permute-start.2 = (f32[128,1]{0,1:T(1,128)S(1)}, f32[128,1]{0,1:T(1,128)S(1)}, u32[]{:S(2)}, u32[]{:S(2)}) collective-permute-start(f32[128,1]{0,1:T(1,128)S(1)} %get-tuple-element.272), channel_id=1, source_target_pairs={{0,1},{1,0},{2,3},{3,2},{4,5},{5,4},{6,7},{7,6},{8,9},{9,8},{10,11... | collective-permute-start | bytes 1544 | tf_op jit(solution)/shard_map/ppermute | solution.py:41
  6.5 28.8 %collective-permute-start.3 = (bf16[128,1024]{1,0:T(8,128)(2,1)}, bf16[128,1024]{1,0:T(8,128)(2,1)S(1)}, u32[]{:S(2)}, u32[]{:S(2)}) collective-permute-start(bf16[128,1024]{1,0:T(8,128)(2,1)} %get-tuple-element.237), channel_id=1, source_target_pairs={{0,1},{1,0},{2,3},{3,2},{4,5},{5,4},{6,7},{7,6},{8,9},{9,8},{10,11... | collective-permute-start | bytes 786440 | tf_op jit(solution)/shard_map/ppermute | solution.py:41
  11.5 11.5 %collective-permute-start.1 = (bf16[128,1536]{1,0:T(8,128)(2,1)S(1)}, bf16[128,1536]{1,0:T(8,128)(2,1)S(1)}, u32[]{:S(2)}, u32[]{:S(2)}) collective-permute-start(bf16[128,1536]{1,0:T(8,128)(2,1)S(1)} %pad_maximum_fusion.10), channel_id=1, source_target_pairs={{0,1},{1,0},{2,3},{3,2},{4,5},{5,4},{6,7},{7,6},{8,9},{9,8},{10,11... | collective-permute-start | bytes 1179656 | tf_op jit(solution)/shard_map/ppermute | solution.py:41
  24.8 10.5 %collective-permute-start.4 = (bf16[128,1024]{1,0:T(8,128)(2,1)S(1)}, bf16[128,1024]{1,0:T(8,128)(2,1)S(1)}, u32[]{:S(2)}, u32[]{:S(2)}) collective-permute-start(bf16[128,1024]{1,0:T(8,128)(2,1)S(1)} %pad_maximum_fusion.12), channel_id=1, source_target_pairs={{0,8},{8,0},{16,24},{24,16},{1,9},{9,1},{17,25},{25,17},{2,10},{10... | collective-permute-start | bytes 786440 | tf_op jit(solution)/shard_map/ppermute | solution.py:41
  49.3 15.7 %all-to-all-start = ((bf16[4,64,1024]{2,1,0:T(8,128)(2,1)}), bf16[4,64,1024]{2,1,0:T(8,128)(2,1)S(1)}, u32[]{:S(2)}, u32[]{:S(2)}) async-start(bf16[4,64,1024]{2,1,0:T(8,128)(2,1)} %bitcast.171), calls=%async_computation | async-start | bytes 1048576 | tf_op jit(solution)/shard_map/all_to_all | solution.py:146
  54.1 12.1 %collective-permute-start.8 = (bf16[256,1024]{1,0:T(8,128)(2,1)S(1)}, bf16[256,1024]{1,0:T(8,128)(2,1)S(1)}, u32[]{:S(2)}, u32[]{:S(2)}) collective-permute-start(bf16[256,1024]{1,0:T(8,128)(2,1)S(1)} %pad_maximum_fusion.7.refs_4_.refs_16_), channel_id=1, source_target_pairs={{0,16},{8,24},{16,0},{24,8},{1,17},{9,25},{17,1},{25,9},{2,18},{10... | collective-permute-start | bytes 1572872 | tf_op jit(solution)/shard_map/ppermute | solution.py:41
  54.3 17.6 %collective-permute-start.9 = (bf16[256,512]{1,0:T(8,128)(2,1)S(1)}, bf16[256,512]{1,0:T(8,128)(2,1)}, u32[]{:S(2)}, u32[]{:S(2)}) collective-permute-start(bf16[256,512]{1,0:T(8,128)(2,1)S(1)} %pad_maximum_fusion.13.refs_8_), channel_id=1, source_target_pairs={{0,16},{8,24},{16,0},{24,8},{1,17},{9,25},{17,1},{25,9},{2,18},{10... | collective-permute-start | bytes 786440 | tf_op jit(solution)/shard_map/ppermute | solution.py:41
  75.6 21.5 %collective-permute-start.11 = (bf16[256,2048]{1,0:T(8,128)(2,1)}, bf16[256,2048]{1,0:T(8,128)(2,1)S(1)}, u32[]{:S(2)}, u32[]{:S(2)}) collective-permute-start(bf16[256,2048]{1,0:T(8,128)(2,1)} %get-tuple-element.115), channel_id=1, source_target_pairs={{0,1},{1,0},{2,3},{3,2},{4,5},{5,4},{6,7},{7,6},{8,9},{9,8},{10,11... | collective-permute-start | bytes 3145736 | tf_op jit(solution)/shard_map/ppermute | solution.py:41
  102.1 21.6 %collective-permute-start.14 = (bf16[2,256,1024]{2,1,0:T(8,128)(2,1)}, bf16[2,256,1024]{2,1,0:T(8,128)(2,1)S(1)}, u32[]{:S(2)}, u32[]{:S(2)}) collective-permute-start(bf16[2,256,1024]{2,1,0:T(8,128)(2,1)} %get-tuple-element.120), channel_id=1, source_target_pairs={{0,1},{1,0},{2,3},{3,2},{4,5},{5,4},{6,7},{7,6},{8,9},{9,8},{10,11... | collective-permute-start | bytes 3145736 | tf_op jit(solution)/shard_map/ppermute | solution.py:41
  103.7 8.9 %collective-permute-start.13 = (bf16[256,1024]{1,0:T(8,128)(2,1)S(1)}, bf16[256,1024]{1,0:T(8,128)(2,1)S(1)}, u32[]{:S(2)}, u32[]{:S(2)}) collective-permute-start(bf16[256,1024]{1,0:T(8,128)(2,1)S(1)} %fusion.12.refs_0_), channel_id=1, source_target_pairs={{0,16},{8,24},{16,0},{24,8},{1,17},{9,25},{17,1},{25,9},{2,18},{10... | collective-permute-start | bytes 1572872 | tf_op jit(solution)/shard_map/ppermute | solution.py:41
  104.0 19.8 %collective-permute-start.12 = (bf16[256,1024]{1,0:T(8,128)(2,1)S(1)}, bf16[256,1024]{1,0:T(8,128)(2,1)S(1)}, u32[]{:S(2)}, u32[]{:S(2)}) collective-permute-start(bf16[256,1024]{1,0:T(8,128)(2,1)S(1)} %bitcast.158), channel_id=1, source_target_pairs={{0,16},{8,24},{16,0},{24,8},{1,17},{9,25},{17,1},{25,9},{2,18},{10... | collective-permute-start | bytes 1572872 | tf_op jit(solution)/shard_map/ppermute | solution.py:41
  130.5 30.7 %collective-permute-start.20 = (bf16[3,256,1024]{2,1,0:T(8,128)(2,1)}, bf16[3,256,1024]{2,1,0:T(8,128)(2,1)}, u32[]{:S(2)}, u32[]{:S(2)}) collective-permute-start(bf16[3,256,1024]{2,1,0:T(8,128)(2,1)} %get-tuple-element.159.refs_4_.refs_0_), channel_id=1, source_target_pairs={{0,16},{8,24},{16,0},{24,8},{1,17},{9,25},{17,1},{25,9},{2,18},{10... | collective-permute-start | bytes 4718600 | tf_op jit(solution)/shard_map/ppermute | solution.py:41
  130.9 19.0 %collective-permute-start.15 = (bf16[2,256,1024]{2,1,0:T(8,128)(2,1)S(1)}, bf16[2,256,1024]{2,1,0:T(8,128)(2,1)S(1)}, u32[]{:S(2)}, u32[]{:S(2)}) collective-permute-start(bf16[2,256,1024]{2,1,0:T(8,128)(2,1)S(1)} %copy-done.77), channel_id=1, source_target_pairs={{0,1},{1,0},{2,3},{3,2},{4,5},{5,4},{6,7},{7,6},{8,9},{9,8},{10,11... | collective-permute-start | bytes 3145736 | tf_op jit(solution)/shard_map/ppermute | solution.py:41
  156.9 40.3 %collective-permute-start.21 = (bf16[3,256,1024]{2,1,0:T(8,128)(2,1)}, bf16[3,256,1024]{2,1,0:T(8,128)(2,1)}, u32[]{:S(2)}, u32[]{:S(2)}) collective-permute-start(bf16[3,256,1024]{2,1,0:T(8,128)(2,1)} %get-tuple-element.160.refs_4_.refs_8_.refs_12_), channel_id=1, source_target_pairs={{0,16},{8,24},{16,0},{24,8},{1,17},{9,25},{17,1},{25,9},{2,18},{10... | collective-permute-start | bytes 4718600 | tf_op jit(solution)/shard_map/ppermute | solution.py:41
  161.2 40.9 %collective-permute-start.25 = (bf16[3,256,1024]{2,1,0:T(8,128)(2,1)S(1)}, bf16[3,256,1024]{2,1,0:T(8,128)(2,1)}, u32[]{:S(2)}, u32[]{:S(2)}) collective-permute-start(bf16[3,256,1024]{2,1,0:T(8,128)(2,1)S(1)} %copy-done.5), channel_id=1, source_target_pairs={{0,8},{8,0},{16,24},{24,16},{1,9},{9,1},{17,25},{25,17},{2,10},{10... | collective-permute-start | bytes 4718600 | tf_op jit(solution)/shard_map/ppermute | solution.py:41
  173.8 28.3 %collective-permute-start.26 = (bf16[3,256,1024]{2,1,0:T(8,128)(2,1)}, bf16[3,256,1024]{2,1,0:T(8,128)(2,1)}, u32[]{:S(2)}, u32[]{:S(2)}) collective-permute-start(bf16[3,256,1024]{2,1,0:T(8,128)(2,1)} %collective-permute-done.20.refs_6_.refs_2_), channel_id=1, source_target_pairs={{0,8},{8,0},{16,24},{24,16},{1,9},{9,1},{17,25},{25,17},{2,10},{10... | collective-permute-start | bytes 4718600 | tf_op jit(solution)/shard_map/ppermute | solution.py:41
  176.9 8.8 %collective-permute-start.16 = (bf16[64,1024]{1,0:T(8,128)(2,1)S(1)}, bf16[64,1024]{1,0:T(8,128)(2,1)S(1)}, u32[]{:S(2)}, u32[]{:S(2)}) collective-permute-start(bf16[64,1024]{1,0:T(8,128)(2,1)S(1)} %get-tuple-element.211), channel_id=1, source_target_pairs={{0,4},{2,6},{4,0},{6,2},{1,5},{3,7},{5,1},{7,3},{8,12},{10,14},{12... | collective-permute-start | bytes 393224 | tf_op jit(solution)/shard_map/ppermute | solution.py:124
  177.4 11.5 %collective-permute-start.17 = (bf16[64,1024]{1,0:T(8,128)(2,1)}, bf16[64,1024]{1,0:T(8,128)(2,1)}, u32[]{:S(2)}, u32[]{:S(2)}) collective-permute-start(bf16[64,1024]{1,0:T(8,128)(2,1)} %get-tuple-element.213), channel_id=1, source_target_pairs={{0,2},{2,4},{4,6},{6,0},{1,3},{3,5},{5,7},{7,1},{8,10},{10,12},{12... | collective-permute-start | bytes 393224 | tf_op jit(solution)/shard_map/ppermute | solution.py:124
  192.8 7.6 %collective-permute-start.23 = (bf16[256,1024]{1,0:T(8,128)(2,1)S(1)}, bf16[256,1024]{1,0:T(8,128)(2,1)S(1)}, u32[]{:S(2)}, u32[]{:S(2)}) collective-permute-start(bf16[256,1024]{1,0:T(8,128)(2,1)S(1)} %bitcast.159), channel_id=1, source_target_pairs={{0,8},{8,0},{16,24},{24,16},{1,9},{9,1},{17,25},{25,17},{2,10},{10... | collective-permute-start | bytes 1572872 | tf_op jit(solution)/shard_map/ppermute | solution.py:41
  197.3 13.1 %collective-permute-start.28 = (bf16[64,1024]{1,0:T(8,128)(2,1)S(1)}, bf16[64,1024]{1,0:T(8,128)(2,1)S(1)}, u32[]{:S(2)}, u32[]{:S(2)}) collective-permute-start(bf16[64,1024]{1,0:T(8,128)(2,1)S(1)} %fusion.64), channel_id=1, source_target_pairs={{0,4},{2,6},{4,0},{6,2},{1,5},{3,7},{5,1},{7,3},{8,12},{10,14},{12... | collective-permute-start | bytes 393224 | tf_op jit(solution)/shard_map/ppermute | solution.py:124
  200.4 10.0 %collective-permute-start.27 = (bf16[64,1024]{1,0:T(8,128)(2,1)S(1)}, bf16[64,1024]{1,0:T(8,128)(2,1)S(1)}, u32[]{:S(2)}, u32[]{:S(2)}) collective-permute-start(bf16[64,1024]{1,0:T(8,128)(2,1)S(1)} %fusion.64), channel_id=1, source_target_pairs={{0,2},{2,4},{4,6},{6,0},{1,3},{3,5},{5,7},{7,1},{8,10},{10,12},{12... | collective-permute-start | bytes 393224 | tf_op jit(solution)/shard_map/ppermute | solution.py:124
  200.6 11.3 %collective-permute-start.22 = (bf16[64,1024]{1,0:T(8,128)(2,1)S(1)}, bf16[64,1024]{1,0:T(8,128)(2,1)S(1)}, u32[]{:S(2)}, u32[]{:S(2)}) collective-permute-start(bf16[64,1024]{1,0:T(8,128)(2,1)S(1)} %fusion.64), channel_id=1, source_target_pairs={{0,6},{2,0},{4,2},{6,4},{1,7},{3,1},{5,3},{7,5},{8,14},{10,8},{12,... | collective-permute-start | bytes 393224 | tf_op jit(solution)/shard_map/ppermute | solution.py:124
  226.4 10.8 %collective-permute-start.30 = (bf16[256,1024]{1,0:T(8,128)(2,1)S(1)}, bf16[256,1024]{1,0:T(8,128)(2,1)S(1)}, u32[]{:S(2)}, u32[]{:S(2)}) collective-permute-start(bf16[256,1024]{1,0:T(8,128)(2,1)S(1)} %slice.251), channel_id=1, source_target_pairs={{0,16},{8,24},{16,0},{24,8},{1,17},{9,25},{17,1},{25,9},{2,18},{10... | collective-permute-start | bytes 1572872 | tf_op jit(solution)/shard_map/ppermute | solution.py:41
  243.4 16.2 %collective-permute-start.33 = (bf16[3,256,1024]{2,1,0:T(8,128)(2,1)S(1)}, bf16[3,256,1024]{2,1,0:T(8,128)(2,1)S(1)}, u32[]{:S(2)}, u32[]{:S(2)}) collective-permute-start(bf16[3,256,1024]{2,1,0:T(8,128)(2,1)S(1)} %copy-done.6), channel_id=1, source_target_pairs={{0,8},{8,0},{16,24},{24,16},{1,9},{9,1},{17,25},{25,17},{2,10},{10... | collective-permute-start | bytes 4718600 | tf_op jit(solution)/shard_map/ppermute | solution.py:41
  243.5 16.1 %collective-permute-start.34 = (bf16[3,256,1024]{2,1,0:T(8,128)(2,1)}, bf16[3,256,1024]{2,1,0:T(8,128)(2,1)S(1)}, u32[]{:S(2)}, u32[]{:S(2)}) collective-permute-start(bf16[3,256,1024]{2,1,0:T(8,128)(2,1)} %collective-permute-done.21.refs_6_.refs_10_.refs_14_), channel_id=1, source_target_pairs={{0,8},{8,0},{16,24},{24,16},{1,9},{9,1},{17,25},{25,17},{2,10},{10... | collective-permute-start | bytes 4718600 | tf_op jit(solution)/shard_map/ppermute | solution.py:41
  247.9 10.6 %collective-permute-start.32 = (bf16[128,1536]{1,0:T(8,128)(2,1)}, bf16[128,1536]{1,0:T(8,128)(2,1)}, u32[]{:S(2)}, u32[]{:S(2)}) collective-permute-start(bf16[128,1536]{1,0:T(8,128)(2,1)} %pad_maximum_fusion.11), channel_id=1, source_target_pairs={{0,1},{1,0},{2,3},{3,2},{4,5},{5,4},{6,7},{7,6},{8,9},{9,8},{10,11... | collective-permute-start | bytes 1179656 | tf_op jit(solution)/shard_map/ppermute | solution.py:41
  291.5 8.9 %collective-permute-start.46 = (f32[2,1024]{1,0:T(2,128)S(1)}, f32[2,1024]{1,0:T(2,128)S(1)}, u32[]{:S(2)}, u32[]{:S(2)}) collective-permute-start(f32[2,1024]{1,0:T(2,128)S(1)} %pad_maximum_fusion.16), channel_id=1, source_target_pairs={{0,8},{8,0},{16,24},{24,16},{1,9},{9,1},{17,25},{25,17},{2,10},{10... | collective-permute-start | bytes 24584 | tf_op jit(solution)/shard_map/ppermute | solution.py:41
  292.4 16.5 %all-to-all-start.2 = ((bf16[4,64,1024]{2,1,0:T(8,128)(2,1)}), bf16[4,64,1024]{2,1,0:T(8,128)(2,1)S(1)}, u32[]{:S(2)}, u32[]{:S(2)}) async-start(bf16[4,64,1024]{2,1,0:T(8,128)(2,1)} %bitcast.56), calls=%async_computation.2 | async-start | bytes 1048576 | tf_op jit(solution)/shard_map/all_to_all | solution.py:146
  303.4 15.0 %collective-permute-start.48 = (f32[2,1024]{1,0:T(2,128)S(1)}, f32[2,1024]{1,0:T(2,128)S(1)}, u32[]{:S(2)}, u32[]{:S(2)}) collective-permute-start(f32[2,1024]{1,0:T(2,128)S(1)} %fusion.92), channel_id=1, source_target_pairs={{0,4},{2,6},{4,0},{6,2},{1,5},{3,7},{5,1},{7,3},{8,12},{10,14},{12... | collective-permute-start | bytes 24584 | tf_op jit(solution)/shard_map/ppermute | solution.py:124
  303.5 14.9 %collective-permute-start.49 = (f32[2,1024]{1,0:T(2,128)S(1)}, f32[2,1024]{1,0:T(2,128)S(1)}, u32[]{:S(2)}, u32[]{:S(2)}) collective-permute-start(f32[2,1024]{1,0:T(2,128)S(1)} %fusion.92), channel_id=1, source_target_pairs={{0,2},{2,4},{4,6},{6,0},{1,3},{3,5},{5,7},{7,1},{8,10},{10,12},{12... | collective-permute-start | bytes 24584 | tf_op jit(solution)/shard_map/ppermute | solution.py:124
  305.6 12.7 %collective-permute-start.50 = (f32[2,1024]{1,0:T(2,128)S(1)}, f32[2,1024]{1,0:T(2,128)S(1)}, u32[]{:S(2)}, u32[]{:S(2)}) collective-permute-start(f32[2,1024]{1,0:T(2,128)S(1)} %fusion.92), channel_id=1, source_target_pairs={{0,6},{2,0},{4,2},{6,4},{1,7},{3,1},{5,3},{7,5},{8,14},{10,8},{12,... | collective-permute-start | bytes 24584 | tf_op jit(solution)/shard_map/ppermute | solution.py:124
  308.9 17.6 %all-to-all-start.1 = ((bf16[4,64,1024]{2,1,0:T(8,128)(2,1)}), bf16[4,64,1024]{2,1,0:T(8,128)(2,1)S(1)}, u32[]{:S(2)}, u32[]{:S(2)}) async-start(bf16[4,64,1024]{2,1,0:T(8,128)(2,1)} %bitcast.50), calls=%async_computation.1 | async-start | bytes 1048576 | tf_op jit(solution)/shard_map/all_to_all | solution.py:146
  319.7 6.9 %collective-permute-start.41 = (f32[64,1]{0,1:T(1,128)S(1)}, f32[64,1]{0,1:T(1,128)S(1)}, u32[]{:S(2)}, u32[]{:S(2)}) collective-permute-start(f32[64,1]{0,1:T(1,128)S(1)} %bitcast.214), channel_id=1, source_target_pairs={{0,1},{1,0},{2,3},{3,2},{4,5},{5,4},{6,7},{7,6},{8,9},{9,8},{10,11... | collective-permute-start | bytes 776 | tf_op jit(solution)/shard_map/ppermute | solution.py:41
  331.2 6.8 %collective-permute-start.43 = (bf16[32,2048]{1,0:T(8,128)(2,1)S(1)}, bf16[32,2048]{1,0:T(8,128)(2,1)S(1)}, u32[]{:S(2)}, u32[]{:S(2)}) collective-permute-start(bf16[32,2048]{1,0:T(8,128)(2,1)S(1)} %pad_maximum_fusion.15), channel_id=1, source_target_pairs={{0,6},{2,0},{4,2},{6,4},{1,7},{3,1},{5,3},{7,5},{8,14},{10,8},{12,... | collective-permute-start | bytes 393224 | tf_op jit(solution)/shard_map/ppermute | solution.py:124
  331.3 11.1 %collective-permute-start.44 = (bf16[32,2048]{1,0:T(8,128)(2,1)S(1)}, bf16[32,2048]{1,0:T(8,128)(2,1)S(1)}, u32[]{:S(2)}, u32[]{:S(2)}) collective-permute-start(bf16[32,2048]{1,0:T(8,128)(2,1)S(1)} %pad_maximum_fusion.15), channel_id=1, source_target_pairs={{0,2},{2,4},{4,6},{6,0},{1,3},{3,5},{5,7},{7,1},{8,10},{10,12},{12... | collective-permute-start | bytes 393224 | tf_op jit(solution)/shard_map/ppermute | solution.py:124
  332.9 14.1 %collective-permute-start.45 = (bf16[32,2048]{1,0:T(8,128)(2,1)S(1)}, bf16[32,2048]{1,0:T(8,128)(2,1)S(1)}, u32[]{:S(2)}, u32[]{:S(2)}) collective-permute-start(bf16[32,2048]{1,0:T(8,128)(2,1)S(1)} %pad_maximum_fusion.15), channel_id=1, source_target_pairs={{0,4},{2,6},{4,0},{6,2},{1,5},{3,7},{5,1},{7,3},{8,12},{10,14},{12... | collective-permute-start | bytes 393224 | tf_op jit(solution)/shard_map/ppermute | solution.py:124
  335.9 13.8 %collective-permute-start.38 = (bf16[32,2048]{1,0:T(8,128)(2,1)S(1)}, bf16[32,2048]{1,0:T(8,128)(2,1)S(1)}, u32[]{:S(2)}, u32[]{:S(2)}) collective-permute-start(bf16[32,2048]{1,0:T(8,128)(2,1)S(1)} %pad_maximum_fusion.14), channel_id=1, source_target_pairs={{0,6},{2,0},{4,2},{6,4},{1,7},{3,1},{5,3},{7,5},{8,14},{10,8},{12,... | collective-permute-start | bytes 393224 | tf_op jit(solution)/shard_map/ppermute | solution.py:124
  337.3 13.4 %collective-permute-start.39 = (bf16[32,2048]{1,0:T(8,128)(2,1)S(1)}, bf16[32,2048]{1,0:T(8,128)(2,1)S(1)}, u32[]{:S(2)}, u32[]{:S(2)}) collective-permute-start(bf16[32,2048]{1,0:T(8,128)(2,1)S(1)} %pad_maximum_fusion.14), channel_id=1, source_target_pairs={{0,2},{2,4},{4,6},{6,0},{1,3},{3,5},{5,7},{7,1},{8,10},{10,12},{12... | collective-permute-start | bytes 393224 | tf_op jit(solution)/shard_map/ppermute | solution.py:124
  338.0 21.9 %collective-permute-start.51 = (bf16[256,1024]{1,0:T(8,128)(2,1)S(1)}, bf16[256,1024]{1,0:T(8,128)(2,1)S(1)}, u32[]{:S(2)}, u32[]{:S(2)}) collective-permute-start(bf16[256,1024]{1,0:T(8,128)(2,1)S(1)} %copy-done.18), channel_id=1, source_target_pairs={{0,8},{8,0},{16,24},{24,16},{1,9},{9,1},{17,25},{25,17},{2,10},{10... | collective-permute-start | bytes 1572872 | tf_op jit(solution)/shard_map/ppermute | solution.py:41
  342.3 17.6 %collective-permute-start.52 = (bf16[256,1024]{1,0:T(8,128)(2,1)S(1)}, bf16[256,1024]{1,0:T(8,128)(2,1)S(1)}, u32[]{:S(2)}, u32[]{:S(2)}) collective-permute-start(bf16[256,1024]{1,0:T(8,128)(2,1)S(1)} %copy-done.51), channel_id=1, source_target_pairs={{0,8},{8,0},{16,24},{24,16},{1,9},{9,1},{17,25},{25,17},{2,10},{10... | collective-permute-start | bytes 1572872 | tf_op jit(solution)/shard_map/ppermute | solution.py:41
  347.0 13.5 %collective-permute-start.59 = (bf16[256,1024]{1,0:T(8,128)(2,1)S(1)}, bf16[256,1024]{1,0:T(8,128)(2,1)S(1)}, u32[]{:S(2)}, u32[]{:S(2)}) collective-permute-start(bf16[256,1024]{1,0:T(8,128)(2,1)S(1)} %bitcast.164), channel_id=1, source_target_pairs={{0,16},{8,24},{16,0},{24,8},{1,17},{9,25},{17,1},{25,9},{2,18},{10... | collective-permute-start | bytes 1572872 | tf_op jit(solution)/shard_map/ppermute | solution.py:41
  349.6 26.5 %collective-permute-start.54 = (bf16[256,1536]{1,0:T(8,128)(2,1)S(1)}, bf16[256,1536]{1,0:T(8,128)(2,1)S(1)}, u32[]{:S(2)}, u32[]{:S(2)}) collective-permute-start(bf16[256,1536]{1,0:T(8,128)(2,1)S(1)} %pad_maximum_fusion.5.refs_4_), channel_id=1, source_target_pairs={{0,16},{8,24},{16,0},{24,8},{1,17},{9,25},{17,1},{25,9},{2,18},{10... | collective-permute-start | bytes 2359304 | tf_op jit(solution)/shard_map/ppermute | solution.py:41
  355.6 7.4 %collective-permute-start.56 = (bf16[256,512]{1,0:T(8,128)(2,1)S(1)}, bf16[256,512]{1,0:T(8,128)(2,1)}, u32[]{:S(2)}, u32[]{:S(2)}) collective-permute-start(bf16[256,512]{1,0:T(8,128)(2,1)S(1)} %copy-done.32), channel_id=1, source_target_pairs={{0,8},{8,0},{16,24},{24,16},{1,9},{9,1},{17,25},{25,17},{2,10},{10... | collective-permute-start | bytes 786440 | tf_op jit(solution)/shard_map/ppermute | solution.py:41
  359.9 18.3 %collective-permute-start.57 = (bf16[256,512]{1,0:T(8,128)(2,1)}, bf16[256,512]{1,0:T(8,128)(2,1)S(1)}, u32[]{:S(2)}, u32[]{:S(2)}) collective-permute-start(bf16[256,512]{1,0:T(8,128)(2,1)} %collective-permute-done.9.refs_10_), channel_id=1, source_target_pairs={{0,8},{8,0},{16,24},{24,16},{1,9},{9,1},{17,25},{25,17},{2,10},{10... | collective-permute-start | bytes 786440 | tf_op jit(solution)/shard_map/ppermute | solution.py:41
  359.9 22.1 %collective-permute-start.58 = (bf16[256,1024]{1,0:T(8,128)(2,1)S(1)}, bf16[256,1024]{1,0:T(8,128)(2,1)S(1)}, u32[]{:S(2)}, u32[]{:S(2)}) collective-permute-start(bf16[256,1024]{1,0:T(8,128)(2,1)S(1)} %bitcast.165), channel_id=1, source_target_pairs={{0,8},{8,0},{16,24},{24,16},{1,9},{9,1},{17,25},{25,17},{2,10},{10... | collective-permute-start | bytes 1572872 | tf_op jit(solution)/shard_map/ppermute | solution.py:41
  360.4 21.7 %collective-permute-start.60 = (bf16[256,1024]{1,0:T(8,128)(2,1)S(1)}, bf16[256,1024]{1,0:T(8,128)(2,1)S(1)}, u32[]{:S(2)}, u32[]{:S(2)}) collective-permute-start(bf16[256,1024]{1,0:T(8,128)(2,1)S(1)} %collective-permute-done.59.refs_14_), channel_id=1, source_target_pairs={{0,8},{8,0},{16,24},{24,16},{1,9},{9,1},{17,25},{25,17},{2,10},{10... | collective-permute-start | bytes 1572872 | tf_op jit(solution)/shard_map/ppermute | solution.py:41
  363.0 19.1 %collective-permute-start.53 = (bf16[256,1536]{1,0:T(8,128)(2,1)S(1)}, bf16[256,1536]{1,0:T(8,128)(2,1)S(1)}, u32[]{:S(2)}, u32[]{:S(2)}) collective-permute-start(bf16[256,1536]{1,0:T(8,128)(2,1)S(1)} %pad_maximum_fusion.5.refs_4_), channel_id=1, source_target_pairs={{0,8},{8,0},{16,24},{24,16},{1,9},{9,1},{17,25},{25,17},{2,10},{10... | collective-permute-start | bytes 2359304 | tf_op jit(solution)/shard_map/ppermute | solution.py:41
  378.3 23.6 %collective-permute-start.63 = (f32[3,256,256]{2,1,0:T(8,128)S(1)}, f32[3,256,256]{2,1,0:T(8,128)}, u32[]{:S(2)}, u32[]{:S(2)}) collective-permute-start(f32[3,256,256]{2,1,0:T(8,128)S(1)} %copy-done.49), channel_id=1, source_target_pairs={{0,1},{1,0},{2,3},{3,2},{4,5},{5,4},{6,7},{7,6},{8,9},{9,8},{10,11... | collective-permute-start | bytes 2359304 | tf_op jit(solution)/shard_map/ppermute | solution.py:41
  382.1 34.2 %collective-permute-start.62 = (f32[3,256,256]{2,1,0:T(8,128)}, f32[3,256,256]{2,1,0:T(8,128)}, u32[]{:S(2)}, u32[]{:S(2)}) collective-permute-start(f32[3,256,256]{2,1,0:T(8,128)} %get-tuple-element.182.a_ref), channel_id=1, source_target_pairs={{0,1},{1,0},{2,3},{3,2},{4,5},{5,4},{6,7},{7,6},{8,9},{9,8},{10,11... | collective-permute-start | bytes 2359304 | tf_op jit(solution)/shard_map/ppermute | solution.py:41
  411.9 18.5 %collective-permute-start.67 = (bf16[784,256]{1,0:T(8,128)(2,1)}, bf16[784,256]{1,0:T(8,128)(2,1)S(1)}, u32[]{:S(2)}, u32[]{:S(2)}) collective-permute-start(bf16[784,256]{1,0:T(8,128)(2,1)} %polynomial.3), channel_id=1, source_target_pairs={{0,1},{1,0},{2,3},{3,2},{4,5},{5,4},{6,7},{7,6},{8,9},{9,8},{10,11... | collective-permute-start | bytes 1204232 | tf_op jit(solution)/shard_map/ppermute | solution.py:41
  416.2 25.3 %collective-permute-start.61 = (f32[3,256,256]{2,1,0:T(8,128)S(1)}, f32[3,256,256]{2,1,0:T(8,128)S(1)}, u32[]{:S(2)}, u32[]{:S(2)}) collective-permute-start(f32[3,256,256]{2,1,0:T(8,128)S(1)} %copy-done.78), channel_id=1, source_target_pairs={{0,1},{1,0},{2,3},{3,2},{4,5},{5,4},{6,7},{7,6},{8,9},{9,8},{10,11... | collective-permute-start | bytes 2359304 | tf_op jit(solution)/shard_map/ppermute | solution.py:41
  427.6 9.5 %collective-permute-start.72 = (bf16[784,256]{1,0:T(8,128)(2,1)}, bf16[784,256]{1,0:T(8,128)(2,1)S(1)}, u32[]{:S(2)}, u32[]{:S(2)}) collective-permute-start(bf16[784,256]{1,0:T(8,128)(2,1)} %polynomial.4), channel_id=1, source_target_pairs={{0,16},{8,24},{16,0},{24,8},{1,17},{9,25},{17,1},{25,9},{2,18},{10... | collective-permute-start | bytes 1204232 | tf_op jit(solution)/shard_map/ppermute | solution.py:41
  428.7 23.7 %collective-permute-start.71 = (bf16[784,256]{1,0:T(8,128)(2,1)}, bf16[784,256]{1,0:T(8,128)(2,1)S(1)}, u32[]{:S(2)}, u32[]{:S(2)}) collective-permute-start(bf16[784,256]{1,0:T(8,128)(2,1)} %polynomial.4), channel_id=1, source_target_pairs={{0,8},{8,0},{16,24},{24,16},{1,9},{9,1},{17,25},{25,17},{2,10},{10... | collective-permute-start | bytes 1204232 | tf_op jit(solution)/shard_map/ppermute | solution.py:41
  430.5 22.7 %collective-permute-start.75 = (bf16[784,256]{1,0:T(8,128)(2,1)S(1)}, bf16[784,256]{1,0:T(8,128)(2,1)S(1)}, u32[]{:S(2)}, u32[]{:S(2)}) collective-permute-start(bf16[784,256]{1,0:T(8,128)(2,1)S(1)} %get-tuple-element.216), channel_id=1, source_target_pairs={{0,16},{8,24},{16,0},{24,8},{1,17},{9,25},{17,1},{25,9},{2,18},{10... | collective-permute-start | bytes 1204232 | tf_op jit(solution)/shard_map/ppermute | solution.py:41
  432.0 36.0 %collective-permute-start.74 = (bf16[784,256]{1,0:T(8,128)(2,1)S(1)}, bf16[784,256]{1,0:T(8,128)(2,1)S(1)}, u32[]{:S(2)}, u32[]{:S(2)}) collective-permute-start(bf16[784,256]{1,0:T(8,128)(2,1)S(1)} %get-tuple-element.216), channel_id=1, source_target_pairs={{0,8},{8,0},{16,24},{24,16},{1,9},{9,1},{17,25},{25,17},{2,10},{10... | collective-permute-start | bytes 1204232 | tf_op jit(solution)/shard_map/ppermute | solution.py:41
  437.2 18.0 %collective-permute-start.69 = (bf16[784,256]{1,0:T(8,128)(2,1)S(1)}, bf16[784,256]{1,0:T(8,128)(2,1)S(1)}, u32[]{:S(2)}, u32[]{:S(2)}) collective-permute-start(bf16[784,256]{1,0:T(8,128)(2,1)S(1)} %get-tuple-element.217), channel_id=1, source_target_pairs={{0,16},{8,24},{16,0},{24,8},{1,17},{9,25},{17,1},{25,9},{2,18},{10... | collective-permute-start | bytes 1204232 | tf_op jit(solution)/shard_map/ppermute | solution.py:41
  441.6 13.6 %collective-permute-start.73 = (bf16[784,256]{1,0:T(8,128)(2,1)S(1)}, bf16[784,256]{1,0:T(8,128)(2,1)S(1)}, u32[]{:S(2)}, u32[]{:S(2)}) collective-permute-start(bf16[784,256]{1,0:T(8,128)(2,1)S(1)} %collective-permute-done.72), channel_id=1, source_target_pairs={{0,8},{8,0},{16,24},{24,16},{1,9},{9,1},{17,25},{25,17},{2,10},{10... | collective-permute-start | bytes 1204232 | tf_op jit(solution)/shard_map/ppermute | solution.py:41
  452.4 15.7 %collective-permute-start.65 = (bf16[784,256]{1,0:T(8,128)(2,1)}, bf16[784,256]{1,0:T(8,128)(2,1)S(1)}, u32[]{:S(2)}, u32[]{:S(2)}) collective-permute-start(bf16[784,256]{1,0:T(8,128)(2,1)} %polynomial.5), channel_id=1, source_target_pairs={{0,16},{8,24},{16,0},{24,8},{1,17},{9,25},{17,1},{25,9},{2,18},{10... | collective-permute-start | bytes 1204232 | tf_op jit(solution)/shard_map/ppermute | solution.py:41
  453.2 15.4 %collective-permute-start.76 = (bf16[784,256]{1,0:T(8,128)(2,1)S(1)}, bf16[784,256]{1,0:T(8,128)(2,1)S(1)}, u32[]{:S(2)}, u32[]{:S(2)}) collective-permute-start(bf16[784,256]{1,0:T(8,128)(2,1)S(1)} %collective-permute-done.75), channel_id=1, source_target_pairs={{0,8},{8,0},{16,24},{24,16},{1,9},{9,1},{17,25},{25,17},{2,10},{10... | collective-permute-start | bytes 1204232 | tf_op jit(solution)/shard_map/ppermute | solution.py:41
  455.2 14.7 %collective-permute-start.68 = (bf16[784,256]{1,0:T(8,128)(2,1)S(1)}, bf16[784,256]{1,0:T(8,128)(2,1)S(1)}, u32[]{:S(2)}, u32[]{:S(2)}) collective-permute-start(bf16[784,256]{1,0:T(8,128)(2,1)S(1)} %get-tuple-element.217), channel_id=1, source_target_pairs={{0,8},{8,0},{16,24},{24,16},{1,9},{9,1},{17,25},{25,17},{2,10},{10... | collective-permute-start | bytes 1204232 | tf_op jit(solution)/shard_map/ppermute | solution.py:41
  455.2 14.7 %collective-permute-start.70 = (bf16[784,256]{1,0:T(8,128)(2,1)S(1)}, bf16[784,256]{1,0:T(8,128)(2,1)S(1)}, u32[]{:S(2)}, u32[]{:S(2)}) collective-permute-start(bf16[784,256]{1,0:T(8,128)(2,1)S(1)} %collective-permute-done.69), channel_id=1, source_target_pairs={{0,8},{8,0},{16,24},{24,16},{1,9},{9,1},{17,25},{25,17},{2,10},{10... | collective-permute-start | bytes 1204232 | tf_op jit(solution)/shard_map/ppermute | solution.py:41
  468.0 20.6 %collective-permute-start.64 = (bf16[784,256]{1,0:T(8,128)(2,1)S(1)}, bf16[784,256]{1,0:T(8,128)(2,1)S(1)}, u32[]{:S(2)}, u32[]{:S(2)}) collective-permute-start(bf16[784,256]{1,0:T(8,128)(2,1)S(1)} %copy-done.60), channel_id=1, source_target_pairs={{0,8},{8,0},{16,24},{24,16},{1,9},{9,1},{17,25},{25,17},{2,10},{10... | collective-permute-start | bytes 1204232 | tf_op jit(solution)/shard_map/ppermute | solution.py:41
  468.1 20.5 %collective-permute-start.66 = (bf16[784,256]{1,0:T(8,128)(2,1)S(1)}, bf16[784,256]{1,0:T(8,128)(2,1)S(1)}, u32[]{:S(2)}, u32[]{:S(2)}) collective-permute-start(bf16[784,256]{1,0:T(8,128)(2,1)S(1)} %collective-permute-done.65), channel_id=1, source_target_pairs={{0,8},{8,0},{16,24},{24,16},{1,9},{9,1},{17,25},{25,17},{2,10},{10... | collective-permute-start | bytes 1204232 | tf_op jit(solution)/shard_map/ppermute | solution.py:41
  (96 other events, 965.2 us)

commit v3 on v2

--- a/solution.py
+++ b/solution.py
@@ -32,8 +32,10 @@
     return pltpu.CompilerParams(vmem_limit_bytes=VMEM_LIMIT)
 
 
-def cost(flops, nbytes):
-    return pl.CostEstimate(flops=int(flops), bytes_accessed=int(nbytes), transcendentals=0)
+def lasting(microseconds):
+    return pl.CostEstimate(
+        flops=0, bytes_accessed=int(microseconds * 3690000), transcendentals=0
+    )
 
 
 def swap(value, axis, bit):
@@ -291,7 +293,7 @@
         out_specs=col(rows),
         out_shape=jax.ShapeDtypeStruct((rows, width), BF),
         compiler_params=params(),
-        cost_estimate=cost(8 * rows * count * width, 4 * count * width),
+        cost_estimate=lasting(5.5),
         name="attention",
     )(query, keys, values, *marks)
 
@@ -311,7 +313,7 @@
             jax.ShapeDtypeStruct((count, width), BF),
         ],
         compiler_params=params(),
-        cost_estimate=cost(20 * rows * count * width, 8 * count * width),
+        cost_estimate=lasting(7),
         name="attention_grad",
     )(query, keys, values, grads, *marks)
 
@@ -342,7 +344,7 @@
             jax.ShapeDtypeStruct((2, rows, count), BF),
         ],
         compiler_params=params(),
-        cost_estimate=cost(1, 1),
+        cost_estimate=lasting(4.5),
         name="units",
     )(x, wgate, wup)
 
@@ -400,7 +402,7 @@
             jax.ShapeDtypeStruct((rows, depth), F32),
         ],
         compiler_params=params(),
-        cost_estimate=cost(1, 1),
+        cost_estimate=lasting(6),
         name="hidden_units",
     )(*args)
 
@@ -517,7 +519,7 @@
         ],
         input_output_aliases=aliases,
         compiler_params=params(),
-        cost_estimate=cost(2 * tok * height * width // parts, 14 * height * width // parts),
+        cost_estimate=lasting(9),
         name="weight_grad",
     )(*args)
 
@@ -565,7 +567,7 @@
         out_specs=[tall] * 9 + [wide] * 3 + [gram],
         out_shape=shapes + [gram_shape],
         compiler_params=params(),
-        cost_estimate=cost(8 * len(ones) * ones[0].shape[0] * share * width, 56 * share * width),
+        cost_estimate=lasting(18),
         name="attention_weights",
     )(place, *ones, *grads, *attns, *mids, *moms)
     return out[:3], out[3:6], out[6:9], out[9:12], out[12]
@@ -622,7 +624,6 @@
     aliases = {len(args) + k: k for k in range(9)}
     in_specs += [pl.BlockSpec(memory_space=pl.ANY)] * 9 + [gram] * 3
     args += [v for out in into for v in out[:3]] + [out[3] for out in into]
-    tok = sum(v.shape[0] for v in twos)
     out = pl.pallas_call(
         functools.partial(mlp_weights_kernel, len(twos), part * blocks, True),
         grid=(blocks, share // tile),
@@ -631,7 +632,7 @@
         out_shape=shapes + [gram_shape] * 3,
         input_output_aliases=aliases,
         compiler_params=params(),
-        cost_estimate=cost(6 * tok * share * width // parts, 42 * share * width // parts),
+        cost_estimate=lasting(24),
         name="mlp_weights",
     )(*args)
     return [(*out[3 * k : 3 * k + 3], out[9 + k]) for k in range(3)]
@@ -705,7 +706,7 @@
         out_shape=jax.ShapeDtypeStruct((3 * half + 16, half), BF),
         scratch_shapes=[pltpu.VMEM((size, size), F32)],
         compiler_params=params(),
-        cost_estimate=cost(34 * size**3, 10 * size * size),
+        cost_estimate=lasting(10),
         name="polynomial",
     )(a, b)
 
@@ -772,7 +773,7 @@
         ),
         out_shape=jax.ShapeDtypeStruct(weight.shape, F32),
         compiler_params=params(),
-        cost_estimate=cost(2 * size * height * width, 8 * height * width),
+        cost_estimate=lasting(9),
         name="update",
     )(me, factors, look, weight)
 
@@ -819,7 +820,7 @@
         ),
         out_shape=[jax.ShapeDtypeStruct(w.shape, F32) for w in weights],
         compiler_params=params(),
-        cost_estimate=cost(8 * size * share * width, 32 * share * width),
+        cost_estimate=lasting(9),
         name="attention_update",
     )(me, factors, factors, factors, factors, *looks, *weights)
 
@@ -926,8 +927,8 @@
 
     trio_twos = [ctx_two(trio) for trio in trios]
     grad_two = z_reduce_slow(dx_two)
-    trio_alls = [ctx_four(later(trio_twos[0], dx_two)), ctx_four(later(trio_twos[1], grad_two))]
-    two_all, dy_all = ctx_four(later(two_two, dx_two)), ctx_four(later(dy_two, dx_two))
+    trio_alls = [ctx_four(later(two, grad_two)) for two in trio_twos]
+    two_all, dy_all = ctx_four(later(two_two, grad_two)), ctx_four(later(dy_two, grad_two))
     scaled_two = middle * inv_two
     weighted = grad_two * gain_two
     mean = f_all(jnp.sum(weighted * scaled_two, axis=1, keepdims=True)) * (1.0 / depth)
@@ -939,7 +940,11 @@
         span=span,
     )
     mid_spread = z_gather_groups_slow(own_mid, gate_out)
-    grad_attn = f_reduce_rows(dot(mid_spread, w_out, 1, 1)).astype(BF)
+    out_part = sum(
+        dot(trio[0], w_down[p * count : (p + 1) * count]) for p, trio in enumerate(trios)
+    ).astype(BF)
+    out_sum = z_reduce(out_part)
+    grad_attn = later(f_reduce_rows(dot(mid_spread, w_out, 1, 1)).astype(BF), out_part)
 
     dquery, dkeys, dvalues = attention_grad(query, keys, values, grad_attn, marks)
     dkv = jnp.concatenate([dkeys, dvalues], axis=1)
@@ -958,58 +963,59 @@
         ],
         axis=1,
     ).astype(BF)
-    dqkv_rows = f_gather_rows(dqkv)
-
-    one_all = ctx_four(one_two)
+    mid_two = ctx_two(mid_spread)
     down_out = weight_grad(
         later(place, dqkv), trio_alls[0], dy_all, mom_down, width, False, (512, 1024), (0, None),
         span=span,
     )
-    gate_out, up_out, down_out = mlp_weights(
-        later(place, dqkv_rows), two_all, trio_alls[1], dy_all, (mom_gate, mom_up, mom_down),
-        width, (1, halves), (gate_out, up_out, down_out),
-    )
-    g_gate, m_gate, l_gate, gram_gate = gate_out
-    g_up, m_up, l_up, gram_up = up_out
-    g_down, m_down, l_down, gram_down = down_out
-
-    mid_all, attn_all = ctx_parts(mid_spread), ctx_four(attn_two)
-    dqkv_all = ctx_parts(dqkv_rows)
-    query_out, key_out, value_out, out_out, gram_attn = attention_weights(
-        later(place, g_down), one_all, dqkv_all, attn_all, mid_all,
-        (mom_query, mom_key, mom_value, mom_out),
-    )
-    g_query, m_query, l_query = query_out
-    g_key, m_key, l_key = key_out
-    g_value, m_value, l_value = value_out
-    g_out, m_out, l_out = out_out
-
-    trios, dqkv_rows = later((trios, dqkv_rows), down_out[3])
-    out_part = sum(
-        dot(trio[0], w_down[p * count : (p + 1) * count]) for p, trio in enumerate(trios)
-    )
-    result = f_gather_cols((middle + z_reduce(out_part)).astype(BF))
-    result = z_gather_slow(result)
-
+    dqkv_rows = later(f_gather_rows(dqkv), mid_two[1], down_out)
+    dqkv_two = ctx_two(dqkv_rows)
     dx_one = (
         dot(dqkv_rows[:, :width], w_query, 1, 1)
         + dot(dqkv_rows[:, width : 2 * width], w_key, 1, 1)
         + dot(dqkv_rows[:, 2 * width :], w_value, 1, 1)
     )
-    grad_one = z_reduce(dx_one)
-    scaled_one = own_in * own_inv
-    weighted = grad_one * gain_one
-    mean = f_all(jnp.sum(weighted * scaled_one, axis=1, keepdims=True)) * (1.0 / depth)
-    input_grad = grad_middle + own_inv * (weighted - scaled_one * mean)
-    input_grad = z_gather_slow(f_gather_cols(input_grad.astype(BF))).astype(F32)
-
     gain_parts = jnp.stack(
         [
             jnp.sum(dx_one * one_spread.astype(F32), axis=0),
             jnp.sum(dx_two * two_spread.astype(F32), axis=0),
         ]
     )
-    gain_sums = all_sum(gain_parts, ("ctx", "tp"))
+    grad_one = z_reduce(dx_one)
+
+    one_all = ctx_four(one_two)
+    gate_out, up_out, down_out = mlp_weights(
+        later(place, dqkv_rows, out_sum, gain_parts), two_all, trio_alls[1], dy_all, (mom_gate, mom_up, mom_down),
+        width, (1, halves), (gate_out, up_out, down_out),
+    )
+    g_gate, m_gate, l_gate, gram_gate = gate_out
+    g_up, m_up, l_up, gram_up = up_out
+    g_down, m_down, l_down, gram_down = down_out
+
+    mid_all, attn_all = ctx_four(later(mid_two, dqkv_rows)), ctx_four(attn_two)
+    dqkv_all = ctx_four(later(dqkv_two, g_down))
+    gain_sums = all_sum(gain_parts, ("ctx",))
+    query_out, key_out, value_out, out_out, gram_attn = attention_weights(
+        later(place, g_down, grad_one, gain_sums), one_all, dqkv_all, attn_all, mid_all,
+        (mom_query, mom_key, mom_value, mom_out),
+    )
+    g_query, m_query, l_query = query_out
+    g_key, m_key, l_key = key_out
+    g_value, m_value, l_value = value_out
+    g_out, m_out, l_out = out_out
+
+    out_sum, grad_one, gain_sums = later((out_sum, grad_one, gain_sums), g_value)
+    result = f_gather_cols((middle + out_sum).astype(BF))
+    scaled_one = own_in * own_inv
+    weighted = grad_one * gain_one
+    mean = f_all(jnp.sum(weighted * scaled_one, axis=1, keepdims=True)) * (1.0 / depth)
+    input_grad = grad_middle + own_inv * (weighted - scaled_one * mean)
+    input_grad = f_gather_cols(input_grad.astype(BF))
+    result_cols, input_cols = result, input_grad
+    result = z_gather_slow(result)
+    input_grad = z_gather_slow(input_grad).astype(F32)
+
+    gain_sums = all_sum(gain_sums, ("tp",))
     grad_gain_one = gain_sums[0] / gain_one
     grad_gain_two = gain_sums[1] / gain_two
 
@@ -1017,16 +1023,16 @@
         even = lax.axis_index("fsdp") == 0
         kept = jnp.where(even, gram_down, gram_gate)
         sent = jnp.where(even, gram_gate, gram_down)
-        both = later((kept, swap(sent, "fsdp", 1)), g_value, result, input_grad)
+        both = later((kept, swap(sent, "fsdp", 1)), g_value)
         q_own = polynomial(*both)
         got_attn = swap(gram_attn, "fsdp", 1)
-        both = later((gram_up, swap(gram_up, "fsdp", 1)), q_own, gain_sums)
+        both = later((gram_up, swap(gram_up, "fsdp", 1)), q_own)
         q_up = polynomial(*both)
         q_other = swap(q_own, "fsdp", 1)
         q_down = ctx_two(jnp.where(even, q_own, q_other))
         q_gate = ctx_two(jnp.where(even, q_other, q_own))
         q_up = ctx_two(q_up)
-        both = later((gram_attn, got_attn), q_up[0])
+        both = later((gram_attn, got_attn), q_up[0], mean, result_cols)
         q_attn = ctx_two(polynomial(*both))
     else:
         grams = lax.psum(jnp.stack([gram_down, gram_gate, gram_up, gram_attn]), "fsdp")
@@ -1037,12 +1043,13 @@
         jnp.stack(ctx_four(q)) for q in (q_down, q_gate, q_up, q_attn)
     )
     ctx_place = place[:1]
-    new_down = update(q_down, l_down, w_down, False, ctx_place)
-    new_gate = update(q_gate, l_gate, w_gate, True, ctx_place)
-    new_up = update(q_up, l_up, w_up, True, ctx_place)
+    new_down = update(q_down, l_down, w_down, False, later(ctx_place, input_cols))
+    new_gate = update(q_gate, l_gate, w_gate, True, later(ctx_place, new_down, result))
+    turn = later(ctx_place, new_gate, input_grad, gain_sums)
+    new_up = update(q_up, l_up, w_up, True, turn)
 
     new_query, new_key, new_value, new_out = attention_update(
-        q_attn, (l_query, l_key, l_value, l_out), (w_query, w_key, w_value, w_out), ctx_place
+        q_attn, (l_query, l_key, l_value, l_out), (w_query, w_key, w_value, w_out), later(ctx_place, new_up)
     )
 
     return (

time: 509 us -> 484 us (0.951)
  the two profiles are of different devices: /device:TPU:21 before, /device:TPU:0 now
where the time goes in v3:
time: 484 us; the launch traced here: 475 us
  Pallas kernels  168 us (35%)
  waiting for transfers between devices  135 us (28%)
  starting transfers between devices  83.2 us (17%)
  local copies, waits for them, and re-layouts  28.4 us (6%)
  other arithmetic  28.1 us (6%)
  blocking collectives  16.2 us (3%)
  matrix products  14 us (3%)
    ppermute x62, waiting for transfers between devices, swap(): return lax.ppermute(value, axis, [(i, i ^ bit) for i in range(size)])  99.8 us
    ppermute x62, starting transfers between devices, swap(): return lax.ppermute(value, axis, [(i, i ^ bit) for i in range(size)])  46.5 us
    pallas_call x3, Pallas kernels, polynomial(): pl.pallas_call(polynomial_kernel, in_specs=[pl.BlockSpec(memory_space=plt...  30 us
    pallas_call x3, Pallas kernels, weight_grad(): pl.pallas_call(functools.partial(weight_grad_kernel, len(lefts), len(righ...  26.6 us
    pallas_call x3, Pallas kernels, update(): pl.pallas_call(functools.partial(update_kernel, by_columns), grid_spec=pl...  26.2 us
    pallas_call x1, Pallas kernels, mlp_weights(): pl.pallas_call(functools.partial(mlp_weights_kernel, len(twos), part * bl...  24.2 us
    ppermute x15, waiting for transfers between devices, z_shift(): return lax.ppermute(value, 'tp', [(i, (i + k) % size) for i in range(size)])  22.7 us
    ppermute x15, starting transfers between devices, z_shift(): return lax.ppermute(value, 'tp', [(i, (i + k) % size) for i in range(size)])  21.4 us
  transfers between devices with their start and end apart: 80, of which 28 were waited for; matrix products, arithmetic and copies ran while one was open for 11% of the time, Pallas kernels for 28%

profile of v3, /device:TPU:0, one launch (start us, length us, event | category | flops | bytes accessed | tf_op | source)
XLA Modules:
  0.0 474.8 jit_solution(13479769116287448378)
XLA Ops:
  1.9 3.0 collective-permute-start
  6.3 1.8 dynamic-slice_bitcast_fusion.1
  8.0 1.9 collective-permute-start.3
  10.0 1.9 collective-permute-done
  15.1 1.9 collective-permute-start.1
  21.3 3.9 collective-permute-done.1
  26.7 1.8 collective-permute-start.5
  29.2 4.0 collective-permute-done.5
  36.3 6.0 %attention.1 = bf16[128,512]{1,0:T(8,128)(2,1)} custom-call(bf16[128,512]{1,0:T(8,128)(2,1)} %get-tuple-element.122.q_ref, bf16[512,512]{1,0:T(8,128)(2,1)} %get-tuple-element.235.k_ref, bf16[512,512]{1,0:T(8,128)(2,1)} %get-tuple-element.234.v_ref, s32[128,1]{1,0:T(8,128)} %iota_add_fusion.qi_ref, s32[128,1]{1,0:T(8,128)} %copy.66.qs_ref, ...), custom_call_target="tpu_custom_call" | custom-call | bytes 20295000 | tf_op jit(solution)/shard_map/attention/pallas_call | solution.py:289
  42.4 1.8 collective-permute-start.7
  44.2 2.9 fusion.79
  49.9 5.2 %all-to-all-start = ((bf16[4,64,1024]{2,1,0:T(8,128)(2,1)}), bf16[4,64,1024]{2,1,0:T(8,128)(2,1)S(1)}, u32[]{:S(2)}, u32[]{:S(2)}) async-start(bf16[4,64,1024]{2,1,0:T(8,128)(2,1)} %bitcast.20), calls=%async_computation | async-start | bytes 1048576 | tf_op jit(solution)/shard_map/all_to_all | solution.py:148
  57.3 12.2 %all-to-all-done = bf16[4,64,1024]{2,1,0:T(8,128)(2,1)S(1)} async-done(((bf16[4,64,1024]{2,1,0:T(8,128)(2,1)}), bf16[4,64,1024]{2,1,0:T(8,128)(2,1)S(1)}, u32[]{:S(2)}, u32[]{:S(2)}) %all-to-all-start) | async-done | bytes 524320 | tf_op jit(solution)/shard_map/all_to_all | solution.py:148
  70.1 4.0 collective-permute-done.9.refs_10_
  75.8 2.1 collective-permute-done.10
  79.7 16.2 %all-gather = bf16[256,1024]{1,0:T(8,128)(2,1)S(1)} all-gather(bf16[64,1024]{1,0:T(8,128)(2,1)S(1)} %multiply_convert_fusion), channel_id=2, replica_groups=mesh['ctx'=4,'tp'=4,'fsdp'=2] {'tp'}, dimensions={0}, use_global_device_ids=true | all-gather | bytes 655360 | tf_op jit(solution)/shard_map/all_gather | solution.py:154
  96.7 4.2 collective-permute-done.11.dgot_ref
  100.9 5.0 %units.2 = (f32[2,256,1024]{2,1,0:T(8,128)}, bf16[2,256,1024]{2,1,0:T(8,128)(2,1)}) custom-call(bf16[256,1024]{1,0:T(8,128)(2,1)} %bitcast.153, bf16[1024,2048]{1,0:T(8,128)(2,1)} %w_ref.4, bf16[1024,2048]{1,0:T(8,128)(2,1)} %w_ref.5), custom_call_target="tpu_custom_call" | custom-call | bytes 16605000 | tf_op jit(solution)/shard_map/units/pallas_call | solution.py:337
  109.7 4.3 units.3
  114.0 8.7 %collective-permute-done.13.refs_2_ = bf16[256,1024]{1,0:T(8,128)(2,1)} collective-permute-done((bf16[256,1024]{1,0:T(8,128)(2,1)S(1)}, bf16[256,1024]{1,0:T(8,128)(2,1)}, u32[]{:S(2)}, u32[]{:S(2)}) %collective-permute-start.13) | collective-permute-done | bytes 524320 | tf_op jit(solution)/shard_map/ppermute | solution.py:43
  122.6 6.2 %collective-permute-done.12.refs_2_ = bf16[256,1024]{1,0:T(8,128)(2,1)S(1)} collective-permute-done((bf16[256,1024]{1,0:T(8,128)(2,1)S(1)}, bf16[256,1024]{1,0:T(8,128)(2,1)S(1)}, u32[]{:S(2)}, u32[]{:S(2)}) %collective-permute-start.12) | collective-permute-done | bytes 524320 | tf_op jit(solution)/shard_map/ppermute | solution.py:43
  129.9 5.7 %hidden_units.2 = (bf16[3,256,1024]{2,1,0:T(8,128)(2,1)}, f32[256,1024]{1,0:T(8,128)}) custom-call(f32[2,256,1024]{2,1,0:T(8,128)} %get-tuple-element.129.own_ref, bf16[2,256,1024]{2,1,0:T(8,128)(2,1)} %copy-done.37, f32[256,2048]{1,0:T(8,128)} %get-tuple-element.295.dh_ref, bf16[256,2048]{1,0:T(8,128)(2,1)} %copy-done.22, bf16[1024,2048]{1,0:T(8,128)(2,1)} %w_ref.4, ...), custom_call_target="tpu_custom_call" | custom-call | bytes 22140000 | tf_op jit(solution)/shard_map/hidden_units/pallas_call | solution.py:395
  137.8 19.5 %collective-permute-done.15.got_ref = bf16[2,256,1024]{2,1,0:T(8,128)(2,1)S(1)} collective-permute-done((bf16[2,256,1024]{2,1,0:T(8,128)(2,1)S(1)}, bf16[2,256,1024]{2,1,0:T(8,128)(2,1)S(1)}, u32[]{:S(2)}, u32[]{:S(2)}) %collective-permute-start.15) | collective-permute-done | bytes 1048608 | tf_op jit(solution)/shard_map/ppermute | solution.py:43
  158.3 6.0 %hidden_units.3 = (bf16[3,256,1024]{2,1,0:T(8,128)(2,1)}, f32[256,1024]{1,0:T(8,128)}) custom-call(f32[2,256,1024]{2,1,0:T(8,128)} %get-tuple-element.128.own_ref, bf16[2,256,1024]{2,1,0:T(8,128)(2,1)} %copy-done.39, f32[256,2048]{1,0:T(8,128)} %get-tuple-element.295.dh_ref, bf16[256,2048]{1,0:T(8,128)(2,1)} %copy-done.22, bf16[1024,2048]{1,0:T(8,128)(2,1)} %w_ref.4, ...), custom_call_target="tpu_custom_call" | custom-call | bytes 22140000 | tf_op jit(solution)/shard_map/hidden_units/pallas_call | solution.py:395
  165.9 2.8 collective-permute-start.18
  171.3 4.2 collective-permute-done.17
  175.5 1.8 collective-permute-done.16
  181.1 1.8 collective-permute-done.19
  184.2 17.1 %collective-permute-done.21.refs_6_.refs_10_.refs_14_ = bf16[3,256,1024]{2,1,0:T(8,128)(2,1)} collective-permute-done((bf16[3,256,1024]{2,1,0:T(8,128)(2,1)}, bf16[3,256,1024]{2,1,0:T(8,128)(2,1)}, u32[]{:S(2)}, u32[]{:S(2)}) %collective-permute-start.21) | collective-permute-done | bytes 1572896 | tf_op jit(solution)/shard_map/ppermute | solution.py:43
  201.2 2.7 collective-permute-start.22
  205.3 2.5 fusion
  207.8 8.9 %weight_grad.3 = (f32[1024,2048]{1,0:T(8,128)}, f32[1024,2048]{1,0:T(8,128)}, bf16[1024,2048]{1,0:T(8,128)(2,1)}, f32[3,256,256]{2,1,0:T(8,128)}) custom-call(s32[2]{0:T(128)} %pad_add_fusion.2.place_ref, bf16[256,1024]{1,0:T(8,128)(2,1)} %bitcast.155, bf16[256,1024]{1,0:T(8,128)(2,1)} %copy-done.12, bf16[256,1024]{1,0:T(8,128)(2,1)} %copy-done.11, ...), custom_call_target="tpu_custom_call" | custom-call | bytes 33210000 | tf_op jit(solution)/shard_map/weight_grad/pallas_call | solution.py:507
  217.7 2.1 fusion.80
  220.5 2.6 fusion.7
  223.1 1.7 collective-permute-done.29
  225.5 7.0 %attention_grad.1 = (f32[128,512]{1,0:T(8,128)}, bf16[512,512]{1,0:T(8,128)(2,1)}, bf16[512,512]{1,0:T(8,128)(2,1)}) custom-call(bf16[128,512]{1,0:T(8,128)(2,1)} %get-tuple-element.122.q_ref, bf16[512,512]{1,0:T(8,128)(2,1)} %get-tuple-element.235.k_ref, bf16[512,512]{1,0:T(8,128)(2,1)} %get-tuple-element.234.v_ref, bf16[128,512]{1,0:T(8,128)(2,1)} %fusion.31.g_ref, ...), custom_call_target="tpu_custom_call" | custom-call | bytes 25830000 | tf_op jit(solution)/shard_map/attention_grad/pallas_call | solution.py:305
  235.9 8.8 %weight_grad.4 = (f32[1024,2048]{1,0:T(8,128)}, f32[1024,2048]{1,0:T(8,128)}, bf16[1024,2048]{1,0:T(8,128)(2,1)}, f32[3,256,256]{2,1,0:T(8,128)}) custom-call(s32[2]{0:T(128)} %pad_add_fusion.2.place_ref, bf16[256,1024]{1,0:T(8,128)(2,1)} %bitcast.156, bf16[256,1024]{1,0:T(8,128)(2,1)} %copy-done.12, bf16[256,1024]{1,0:T(8,128)(2,1)} %copy-done.11, ...), custom_call_target="tpu_custom_call" | custom-call | bytes 33210000 | tf_op jit(solution)/shard_map/weight_grad/pallas_call | solution.py:507
  251.0 1.9 copy.69
  252.9 4.5 all-to-all-start.1
  258.9 8.9 %weight_grad.5 = (f32[2048,1024]{1,0:T(8,128)}, f32[2048,1024]{1,0:T(8,128)}, bf16[2048,1024]{1,0:T(8,128)(2,1)}, f32[3,256,256]{2,1,0:T(8,128)}) custom-call(s32[2]{0:T(128)} %pad_add_fusion.2.place_ref, bf16[3,256,1024]{2,1,0:T(8,128)(2,1)} %get-tuple-element.140.refs_4_.refs_0_, bf16[3,256,1024]{2,1,0:T(8,128)(2,1)} %collective-permute-done.25.refs_5_.refs_1_, ...), custom_call_target="tpu_custom_call" | custom-call | bytes 33210000 | tf_op jit(solution)/shard_map/weight_grad/pallas_call | solution.py:507
  274.5 1.9 copy.78
  276.3 5.5 %all-to-all-start.2 = ((bf16[4,64,1024]{2,1,0:T(8,128)(2,1)}), bf16[4,64,1024]{2,1,0:T(8,128)(2,1)S(1)}, u32[]{:S(2)}, u32[]{:S(2)}) async-start(bf16[4,64,1024]{2,1,0:T(8,128)(2,1)} %bitcast.54), calls=%async_computation.2 | async-start | bytes 1048576 | tf_op jit(solution)/shard_map/all_to_all | solution.py:148
  281.9 24.2 %mlp_weights.1 = (f32[1024,2048]{1,0:T(8,128)}, f32[1024,2048]{1,0:T(8,128)}, bf16[1024,2048]{1,0:T(8,128)(2,1)}, f32[1024,2048]{1,0:T(8,128)}, f32[1024,2048]{1...) custom-call(s32[2]{0:T(128)} %pad_add_fusion.2.place_ref, ...), custom_call_target="tpu_custom_call", output_to_operand_aliasing={{0}: (24, {}), {1}: (25, {}), {2}: (26, {}), {3}: (27, {}),... | custom-call | bytes 88560000 | tf_op jit(solution)/shard_map/mlp_weights/pallas_call | solution.py:627
  306.8 2.9 collective-permute-start.37
  310.2 2.7 broadcast_select_fusion.2
  315.3 1.9 collective-permute-done.48.refs_15_
  319.0 17.7 %attention_weights.1 = (f32[1024,512]{1,0:T(8,128)}, f32[1024,512]{1,0:T(8,128)}, bf16[1024,512]{1,0:T(8,128)(2,1)}, f32[1024,512]{1,0:T(8,128)}, f32[1024,512]{...) custom-call(s32[2]{0:T(128)} %pad_add_fusion.2.place_ref, ...), custom_call_target="tpu_custom_call" | custom-call | bytes 66420000 | tf_op jit(solution)/shard_map/attention_weights/pallas_call | solution.py:558
  336.7 3.6 collective-permute-start.60
  343.2 9.9 %polynomial.3 = bf16[784,256]{1,0:T(8,128)(2,1)} custom-call(f32[3,256,256]{2,1,0:T(8,128)} %get-tuple-element.195.a_ref, f32[3,256,256]{2,1,0:T(8,128)} %collective-permute-done.61.b_ref), custom_call_target="tpu_custom_call" | custom-call | bytes 36900000 | tf_op jit(solution)/shard_map/polynomial/pallas_call | solution.py:702
  353.8 10.1 %polynomial.4 = bf16[784,256]{1,0:T(8,128)(2,1)} custom-call(f32[3,256,256]{2,1,0:T(8,128)} %get-tuple-element.202.a_ref, f32[3,256,256]{2,1,0:T(8,128)} %collective-permute-done.69.b_ref), custom_call_target="tpu_custom_call" | custom-call | bytes 36900000 | tf_op jit(solution)/shard_map/polynomial/pallas_call | solution.py:702
  369.9 2.8 collective-permute-start.50
  373.8 6.6 %collective-permute-done.50 = bf16[32,2048]{1,0:T(8,128)(2,1)S(1)} collective-permute-done((bf16[32,2048]{1,0:T(8,128)(2,1)S(1)}, bf16[32,2048]{1,0:T(8,128)(2,1)S(1)}, u32[]{:S(2)}, u32[]{:S(2)}) %collective-permute-start.50) | collective-permute-done | bytes 131104 | tf_op jit(solution)/shard_map/ppermute | solution.py:126
  380.9 4.5 collective-permute-start.56
  385.4 5.1 %collective-permute-done.52 = bf16[32,2048]{1,0:T(8,128)(2,1)S(1)} collective-permute-done((bf16[32,2048]{1,0:T(8,128)(2,1)S(1)}, bf16[32,2048]{1,0:T(8,128)(2,1)S(1)}, u32[]{:S(2)}, u32[]{:S(2)}) %collective-permute-start.52) | collective-permute-done | bytes 131104 | tf_op jit(solution)/shard_map/ppermute | solution.py:126
  391.6 2.0 collective-permute-start.73
  393.6 2.7 collective-permute-done.57
  396.7 2.0 collective-permute-start.64
  398.9 12.9 %collective-permute-done.73.b_ref = f32[3,256,256]{2,1,0:T(8,128)S(1)} collective-permute-done((f32[3,256,256]{2,1,0:T(8,128)S(1)}, f32[3,256,256]{2,1,0:T(8,128)S(1)}, u32[]{:S(2)}, u32[]{:S(2)}) %collective-permute-start.73) | collective-permute-done | bytes 786464 | tf_op jit(solution)/shard_map/ppermute | solution.py:43
  412.7 9.9 %polynomial.5 = bf16[784,256]{1,0:T(8,128)(2,1)} custom-call(f32[3,256,256]{2,1,0:T(8,128)} %get-tuple-element.207.a_ref, f32[3,256,256]{2,1,0:T(8,128)} %copy-done.43), custom_call_target="tpu_custom_call" | custom-call | bytes 36900000 | tf_op jit(solution)/shard_map/polynomial/pallas_call | solution.py:702
  427.2 6.6 %collective-permute-done.75 = bf16[784,256]{1,0:T(8,128)(2,1)S(1)} collective-permute-done((bf16[784,256]{1,0:T(8,128)(2,1)}, bf16[784,256]{1,0:T(8,128)(2,1)S(1)}, u32[]{:S(2)}, u32[]{:S(2)}) %collective-permute-start.75) | collective-permute-done | bytes 401440 | tf_op jit(solution)/shard_map/ppermute | solution.py:43
  436.5 8.9 %update.3 = f32[2048,1024]{1,0:T(8,128)} custom-call(s32[1]{0:T(128)} %bitcast.47.me_ref, bf16[4,784,256]{2,1,0:T(8,128)(2,1)} %pad_maximum_fusion.q_ref, bf16[2048,1024]{1,0:T(8,128)(2,1)} %get-tuple-element.197.l_ref, bf16[2048,1024]{1,0:T(8,128)(2,1)} %w_ref.3), custom_call_target="tpu_custom_call" | custom-call | bytes 33210000 | tf_op jit(solution)/shard_map/update/pallas_call | solution.py:758
  446.8 8.6 %update.4 = f32[1024,2048]{1,0:T(8,128)} custom-call(s32[1]{0:T(128)} %bitcast.47.me_ref, bf16[4,784,256]{2,1,0:T(8,128)(2,1)} %pad_maximum_fusion.1.q_ref, bf16[1024,2048]{1,0:T(8,128)(2,1)} %get-tuple-element.199.l_ref, bf16[1024,2048]{1,0:T(8,128)(2,1)} %w_ref.4), custom_call_target="tpu_custom_call" | custom-call | bytes 33210000 | tf_op jit(solution)/shard_map/update/pallas_call | solution.py:758
  455.4 8.6 %update.5 = f32[1024,2048]{1,0:T(8,128)} custom-call(s32[1]{0:T(128)} %bitcast.47.me_ref, bf16[4,784,256]{2,1,0:T(8,128)(2,1)} %pad_maximum_fusion.2.q_ref, bf16[1024,2048]{1,0:T(8,128)(2,1)} %get-tuple-element.204.l_ref, bf16[1024,2048]{1,0:T(8,128)(2,1)} %w_ref.5), custom_call_target="tpu_custom_call" | custom-call | bytes 33210000 | tf_op jit(solution)/shard_map/update/pallas_call | solution.py:758
  465.4 9.0 %attention_update.1 = (f32[1024,512]{1,0:T(8,128)}, f32[1024,512]{1,0:T(8,128)}, f32[1024,512]{1,0:T(8,128)}, f32[512,1024]{1,0:T(8,128)}) custom-call(s32[1]{0:T(128)} %bitcast.47.me_ref, bf16[4,784,256]{2,1,0:T(8,128)(2,1)} %pad_maximum_fusion.3.refs_0_.refs_1_.refs_2_.refs_3_, bf16[4,784,256]{2,1,0:T(8,128)(2,1)} %pad_maximum_fusion.3.refs_0_.refs_1_.refs_2_.refs_3_, ...), custom_call_target="tpu_custom_call" | custom-call | bytes 33210000 | tf_op jit(solution)/shard_map/attention_update/pallas_call | solution.py:808
  (362 shorter events, 92.1 us)
Async XLA Ops:
  1.9 10.0 %collective-permute-start = (bf16[128,1024]{1,0:T(8,128)(2,1)S(1)}, bf16[128,1024]{1,0:T(8,128)(2,1)S(1)}, u32[]{:S(2)}, u32[]{:S(2)}) collective-permute-start(bf16[128,1024]{1,0:T(8,128)(2,1)S(1)} %get-tuple-element.259), channel_id=1, source_target_pairs={{0,1},{1,0},{2,3},{3,2},{4,5},{5,4},{6,7},{7,6},{8,9},{9,8},{10,11... | collective-permute-start | bytes 786440 | tf_op jit(solution)/shard_map/ppermute | solution.py:43
  6.1 11.4 %collective-permute-start.2 = (f32[128,1]{0,1:T(1,128)S(1)}, f32[128,1]{0,1:T(1,128)S(1)}, u32[]{:S(2)}, u32[]{:S(2)}) collective-permute-start(f32[128,1]{0,1:T(1,128)S(1)} %get-tuple-element.292), channel_id=1, source_target_pairs={{0,1},{1,0},{2,3},{3,2},{4,5},{5,4},{6,7},{7,6},{8,9},{9,8},{10,11... | collective-permute-start | bytes 1544 | tf_op jit(solution)/shard_map/ppermute | solution.py:43
  8.0 27.1 %collective-permute-start.3 = (bf16[128,1024]{1,0:T(8,128)(2,1)}, bf16[128,1024]{1,0:T(8,128)(2,1)S(1)}, u32[]{:S(2)}, u32[]{:S(2)}) collective-permute-start(bf16[128,1024]{1,0:T(8,128)(2,1)} %get-tuple-element.257), channel_id=1, source_target_pairs={{0,1},{1,0},{2,3},{3,2},{4,5},{5,4},{6,7},{7,6},{8,9},{9,8},{10,11... | collective-permute-start | bytes 786440 | tf_op jit(solution)/shard_map/ppermute | solution.py:43
  15.1 10.1 %collective-permute-start.1 = (bf16[128,1536]{1,0:T(8,128)(2,1)S(1)}, bf16[128,1536]{1,0:T(8,128)(2,1)S(1)}, u32[]{:S(2)}, u32[]{:S(2)}) collective-permute-start(bf16[128,1536]{1,0:T(8,128)(2,1)S(1)} %pad_maximum_fusion.10), channel_id=1, source_target_pairs={{0,1},{1,0},{2,3},{3,2},{4,5},{5,4},{6,7},{7,6},{8,9},{9,8},{10,11... | collective-permute-start | bytes 1179656 | tf_op jit(solution)/shard_map/ppermute | solution.py:43
  49.9 19.6 %all-to-all-start = ((bf16[4,64,1024]{2,1,0:T(8,128)(2,1)}), bf16[4,64,1024]{2,1,0:T(8,128)(2,1)S(1)}, u32[]{:S(2)}, u32[]{:S(2)}) async-start(bf16[4,64,1024]{2,1,0:T(8,128)(2,1)} %bitcast.20), calls=%async_computation | async-start | bytes 1048576 | tf_op jit(solution)/shard_map/all_to_all | solution.py:148
  55.2 15.0 %collective-permute-start.8 = (bf16[256,1024]{1,0:T(8,128)(2,1)S(1)}, bf16[256,1024]{1,0:T(8,128)(2,1)}, u32[]{:S(2)}, u32[]{:S(2)}) collective-permute-start(bf16[256,1024]{1,0:T(8,128)(2,1)S(1)} %pad_maximum_fusion.7.refs_4_.refs_16_), channel_id=1, source_target_pairs={{0,16},{8,24},{16,0},{24,8},{1,17},{9,25},{17,1},{25,9},{2,18},{10... | collective-permute-start | bytes 1572872 | tf_op jit(solution)/shard_map/ppermute | solution.py:43
  56.7 17.5 %collective-permute-start.9 = (bf16[256,512]{1,0:T(8,128)(2,1)S(1)}, bf16[256,512]{1,0:T(8,128)(2,1)}, u32[]{:S(2)}, u32[]{:S(2)}) collective-permute-start(bf16[256,512]{1,0:T(8,128)(2,1)S(1)} %pad_maximum_fusion.13.refs_8_), channel_id=1, source_target_pairs={{0,16},{8,24},{16,0},{24,8},{1,17},{9,25},{17,1},{25,9},{2,18},{10... | collective-permute-start | bytes 786440 | tf_op jit(solution)/shard_map/ppermute | solution.py:43
  78.2 22.7 %collective-permute-start.11 = (bf16[256,2048]{1,0:T(8,128)(2,1)}, bf16[256,2048]{1,0:T(8,128)(2,1)S(1)}, u32[]{:S(2)}, u32[]{:S(2)}) collective-permute-start(bf16[256,2048]{1,0:T(8,128)(2,1)} %get-tuple-element.125), channel_id=1, source_target_pairs={{0,1},{1,0},{2,3},{3,2},{4,5},{5,4},{6,7},{7,6},{8,9},{9,8},{10,11... | collective-permute-start | bytes 3145736 | tf_op jit(solution)/shard_map/ppermute | solution.py:43
  105.9 23.0 %collective-permute-start.14 = (bf16[2,256,1024]{2,1,0:T(8,128)(2,1)}, bf16[2,256,1024]{2,1,0:T(8,128)(2,1)S(1)}, u32[]{:S(2)}, u32[]{:S(2)}) collective-permute-start(bf16[2,256,1024]{2,1,0:T(8,128)(2,1)} %get-tuple-element.130), channel_id=1, source_target_pairs={{0,1},{1,0},{2,3},{3,2},{4,5},{5,4},{6,7},{7,6},{8,9},{9,8},{10,11... | collective-permute-start | bytes 3145736 | tf_op jit(solution)/shard_map/ppermute | solution.py:43
  107.6 15.0 %collective-permute-start.13 = (bf16[256,1024]{1,0:T(8,128)(2,1)S(1)}, bf16[256,1024]{1,0:T(8,128)(2,1)}, u32[]{:S(2)}, u32[]{:S(2)}) collective-permute-start(bf16[256,1024]{1,0:T(8,128)(2,1)S(1)} %fusion.12.refs_0_), channel_id=1, source_target_pairs={{0,16},{8,24},{16,0},{24,8},{1,17},{9,25},{17,1},{25,9},{2,18},{10... | collective-permute-start | bytes 1572872 | tf_op jit(solution)/shard_map/ppermute | solution.py:43
  109.2 19.6 %collective-permute-start.12 = (bf16[256,1024]{1,0:T(8,128)(2,1)S(1)}, bf16[256,1024]{1,0:T(8,128)(2,1)S(1)}, u32[]{:S(2)}, u32[]{:S(2)}) collective-permute-start(bf16[256,1024]{1,0:T(8,128)(2,1)S(1)} %bitcast.158), channel_id=1, source_target_pairs={{0,16},{8,24},{16,0},{24,8},{1,17},{9,25},{17,1},{25,9},{2,18},{10... | collective-permute-start | bytes 1572872 | tf_op jit(solution)/shard_map/ppermute | solution.py:43
  135.6 42.6 %collective-permute-start.20 = (bf16[3,256,1024]{2,1,0:T(8,128)(2,1)}, bf16[3,256,1024]{2,1,0:T(8,128)(2,1)}, u32[]{:S(2)}, u32[]{:S(2)}) collective-permute-start(bf16[3,256,1024]{2,1,0:T(8,128)(2,1)} %get-tuple-element.140.refs_4_.refs_0_), channel_id=1, source_target_pairs={{0,16},{8,24},{16,0},{24,8},{1,17},{9,25},{17,1},{25,9},{2,18},{10... | collective-permute-start | bytes 4718600 | tf_op jit(solution)/shard_map/ppermute | solution.py:43
  137.3 20.0 %collective-permute-start.15 = (bf16[2,256,1024]{2,1,0:T(8,128)(2,1)S(1)}, bf16[2,256,1024]{2,1,0:T(8,128)(2,1)S(1)}, u32[]{:S(2)}, u32[]{:S(2)}) collective-permute-start(bf16[2,256,1024]{2,1,0:T(8,128)(2,1)S(1)} %copy-done.59), channel_id=1, source_target_pairs={{0,1},{1,0},{2,3},{3,2},{4,5},{5,4},{6,7},{7,6},{8,9},{9,8},{10,11... | collective-permute-start | bytes 3145736 | tf_op jit(solution)/shard_map/ppermute | solution.py:43
  168.6 8.7 %collective-permute-start.16 = (bf16[64,1024]{1,0:T(8,128)(2,1)S(1)}, bf16[64,1024]{1,0:T(8,128)(2,1)S(1)}, u32[]{:S(2)}, u32[]{:S(2)}) collective-permute-start(bf16[64,1024]{1,0:T(8,128)(2,1)S(1)} %get-tuple-element.231), channel_id=1, source_target_pairs={{0,4},{2,6},{4,0},{6,2},{1,5},{3,7},{5,1},{7,3},{8,12},{10,14},{12... | collective-permute-start | bytes 393224 | tf_op jit(solution)/shard_map/ppermute | solution.py:126
  169.8 31.5 %collective-permute-start.21 = (bf16[3,256,1024]{2,1,0:T(8,128)(2,1)}, bf16[3,256,1024]{2,1,0:T(8,128)(2,1)}, u32[]{:S(2)}, u32[]{:S(2)}) collective-permute-start(bf16[3,256,1024]{2,1,0:T(8,128)(2,1)} %get-tuple-element.168.refs_4_.refs_8_.refs_12_), channel_id=1, source_target_pairs={{0,16},{8,24},{16,0},{24,8},{1,17},{9,25},{17,1},{25,9},{2,18},{10... | collective-permute-start | bytes 4718600 | tf_op jit(solution)/shard_map/ppermute | solution.py:43
  178.2 29.6 %collective-permute-start.25 = (bf16[3,256,1024]{2,1,0:T(8,128)(2,1)S(1)}, bf16[3,256,1024]{2,1,0:T(8,128)(2,1)}, u32[]{:S(2)}, u32[]{:S(2)}) collective-permute-start(bf16[3,256,1024]{2,1,0:T(8,128)(2,1)S(1)} %copy-done.5), channel_id=1, source_target_pairs={{0,8},{8,0},{16,24},{24,16},{1,9},{9,1},{17,25},{25,17},{2,10},{10... | collective-permute-start | bytes 4718600 | tf_op jit(solution)/shard_map/ppermute | solution.py:43
  178.3 29.5 %collective-permute-start.26 = (bf16[3,256,1024]{2,1,0:T(8,128)(2,1)}, bf16[3,256,1024]{2,1,0:T(8,128)(2,1)}, u32[]{:S(2)}, u32[]{:S(2)}) collective-permute-start(bf16[3,256,1024]{2,1,0:T(8,128)(2,1)} %collective-permute-done.20.refs_6_.refs_2_), channel_id=1, source_target_pairs={{0,8},{8,0},{16,24},{24,16},{1,9},{9,1},{17,25},{25,17},{2,10},{10... | collective-permute-start | bytes 4718600 | tf_op jit(solution)/shard_map/ppermute | solution.py:43
  181.1 22.9 %collective-permute-start.23 = (bf16[256,1024]{1,0:T(8,128)(2,1)S(1)}, bf16[256,1024]{1,0:T(8,128)(2,1)S(1)}, u32[]{:S(2)}, u32[]{:S(2)}) collective-permute-start(bf16[256,1024]{1,0:T(8,128)(2,1)S(1)} %bitcast.159), channel_id=1, source_target_pairs={{0,8},{8,0},{16,24},{24,16},{1,9},{9,1},{17,25},{25,17},{2,10},{10... | collective-permute-start | bytes 1572872 | tf_op jit(solution)/shard_map/ppermute | solution.py:43
  182.9 21.2 %collective-permute-start.24 = (bf16[256,1024]{1,0:T(8,128)(2,1)}, bf16[256,1024]{1,0:T(8,128)(2,1)S(1)}, u32[]{:S(2)}, u32[]{:S(2)}) collective-permute-start(bf16[256,1024]{1,0:T(8,128)(2,1)} %copy-done.11), channel_id=1, source_target_pairs={{0,8},{8,0},{16,24},{24,16},{1,9},{9,1},{17,25},{25,17},{2,10},{10... | collective-permute-start | bytes 1572872 | tf_op jit(solution)/shard_map/ppermute | solution.py:43
  201.2 15.4 %collective-permute-start.22 = (bf16[64,1024]{1,0:T(8,128)(2,1)S(1)}, bf16[64,1024]{1,0:T(8,128)(2,1)S(1)}, u32[]{:S(2)}, u32[]{:S(2)}) collective-permute-start(bf16[64,1024]{1,0:T(8,128)(2,1)S(1)} %fusion.64), channel_id=1, source_target_pairs={{0,6},{2,0},{4,2},{6,4},{1,7},{3,1},{5,3},{7,5},{8,14},{10,8},{12,... | collective-permute-start | bytes 393224 | tf_op jit(solution)/shard_map/ppermute | solution.py:126
  203.9 12.7 %collective-permute-start.27 = (bf16[64,1024]{1,0:T(8,128)(2,1)S(1)}, bf16[64,1024]{1,0:T(8,128)(2,1)S(1)}, u32[]{:S(2)}, u32[]{:S(2)}) collective-permute-start(bf16[64,1024]{1,0:T(8,128)(2,1)S(1)} %fusion.64), channel_id=1, source_target_pairs={{0,2},{2,4},{4,6},{6,0},{1,3},{3,5},{5,7},{7,1},{8,10},{10,12},{12... | collective-permute-start | bytes 393224 | tf_op jit(solution)/shard_map/ppermute | solution.py:126
  204.2 12.5 %collective-permute-start.28 = (bf16[64,1024]{1,0:T(8,128)(2,1)S(1)}, bf16[64,1024]{1,0:T(8,128)(2,1)S(1)}, u32[]{:S(2)}, u32[]{:S(2)}) collective-permute-start(bf16[64,1024]{1,0:T(8,128)(2,1)S(1)} %fusion.64), channel_id=1, source_target_pairs={{0,4},{2,6},{4,0},{6,2},{1,5},{3,7},{5,1},{7,3},{8,12},{10,14},{12... | collective-permute-start | bytes 393224 | tf_op jit(solution)/shard_map/ppermute | solution.py:126
  234.8 9.9 %collective-permute-start.30 = (bf16[256,1024]{1,0:T(8,128)(2,1)S(1)}, bf16[256,1024]{1,0:T(8,128)(2,1)S(1)}, u32[]{:S(2)}, u32[]{:S(2)}) collective-permute-start(bf16[256,1024]{1,0:T(8,128)(2,1)S(1)} %slice.251), channel_id=1, source_target_pairs={{0,16},{8,24},{16,0},{24,8},{1,17},{9,25},{17,1},{25,9},{2,18},{10... | collective-permute-start | bytes 1572872 | tf_op jit(solution)/shard_map/ppermute | solution.py:43
  245.7 13.0 %collective-permute-start.35 = (bf16[256,1024]{1,0:T(8,128)(2,1)}, bf16[256,1024]{1,0:T(8,128)(2,1)}, u32[]{:S(2)}, u32[]{:S(2)}) collective-permute-start(bf16[256,1024]{1,0:T(8,128)(2,1)} %collective-permute-done.8.refs_6_.refs_18_), channel_id=1, source_target_pairs={{0,8},{8,0},{16,24},{24,16},{1,9},{9,1},{17,25},{25,17},{2,10},{10... | collective-permute-start | bytes 1572872 | tf_op jit(solution)/shard_map/ppermute | solution.py:43
  248.6 19.1 %collective-permute-start.32 = (bf16[128,1536]{1,0:T(8,128)(2,1)}, bf16[128,1536]{1,0:T(8,128)(2,1)}, u32[]{:S(2)}, u32[]{:S(2)}) collective-permute-start(bf16[128,1536]{1,0:T(8,128)(2,1)} %pad_maximum_fusion.11), channel_id=1, source_target_pairs={{0,1},{1,0},{2,3},{3,2},{4,5},{5,4},{6,7},{7,6},{8,9},{9,8},{10,11... | collective-permute-start | bytes 1179656 | tf_op jit(solution)/shard_map/ppermute | solution.py:43
  249.2 23.5 %collective-permute-start.38 = (bf16[3,256,1024]{2,1,0:T(8,128)(2,1)S(1)}, bf16[3,256,1024]{2,1,0:T(8,128)(2,1)}, u32[]{:S(2)}, u32[]{:S(2)}) collective-permute-start(bf16[3,256,1024]{2,1,0:T(8,128)(2,1)S(1)} %copy-done.6), channel_id=1, source_target_pairs={{0,8},{8,0},{16,24},{24,16},{1,9},{9,1},{17,25},{25,17},{2,10},{10... | collective-permute-start | bytes 4718600 | tf_op jit(solution)/shard_map/ppermute | solution.py:43
  249.2 23.6 %collective-permute-start.39 = (bf16[3,256,1024]{2,1,0:T(8,128)(2,1)}, bf16[3,256,1024]{2,1,0:T(8,128)(2,1)}, u32[]{:S(2)}, u32[]{:S(2)}) collective-permute-start(bf16[3,256,1024]{2,1,0:T(8,128)(2,1)} %collective-permute-done.21.refs_6_.refs_10_.refs_14_), channel_id=1, source_target_pairs={{0,8},{8,0},{16,24},{24,16},{1,9},{9,1},{17,25},{25,17},{2,10},{10... | collective-permute-start | bytes 4718600 | tf_op jit(solution)/shard_map/ppermute | solution.py:43
  250.5 18.8 %collective-permute-start.33 = (bf16[256,1024]{1,0:T(8,128)(2,1)}, bf16[256,1024]{1,0:T(8,128)(2,1)}, u32[]{:S(2)}, u32[]{:S(2)}) collective-permute-start(bf16[256,1024]{1,0:T(8,128)(2,1)} %bitcast.50.refs_12_), channel_id=1, source_target_pairs={{0,16},{8,24},{16,0},{24,8},{1,17},{9,25},{17,1},{25,9},{2,18},{10... | collective-permute-start | bytes 1572872 | tf_op jit(solution)/shard_map/ppermute | solution.py:43
  252.9 20.4 %all-to-all-start.1 = ((bf16[4,64,1024]{2,1,0:T(8,128)(2,1)}), bf16[4,64,1024]{2,1,0:T(8,128)(2,1)}, u32[]{:S(2)}, u32[]{:S(2)}) async-start(bf16[4,64,1024]{2,1,0:T(8,128)(2,1)} %bitcast.167), calls=%async_computation.1 | async-start | bytes 1048576 | tf_op jit(solution)/shard_map/all_to_all | solution.py:148
  258.8 48.0 %collective-permute-start.40 = (bf16[256,1024]{1,0:T(8,128)(2,1)S(1)}, bf16[256,1024]{1,0:T(8,128)(2,1)}, u32[]{:S(2)}, u32[]{:S(2)}) collective-permute-start(bf16[256,1024]{1,0:T(8,128)(2,1)S(1)} %copy-done.15), channel_id=1, source_target_pairs={{0,8},{8,0},{16,24},{24,16},{1,9},{9,1},{17,25},{25,17},{2,10},{10... | collective-permute-start | bytes 1572872 | tf_op jit(solution)/shard_map/ppermute | solution.py:43
  267.8 41.9 %collective-permute-start.41 = (bf16[256,1024]{1,0:T(8,128)(2,1)}, bf16[256,1024]{1,0:T(8,128)(2,1)}, u32[]{:S(2)}, u32[]{:S(2)}) collective-permute-start(bf16[256,1024]{1,0:T(8,128)(2,1)} %collective-permute-done.13.refs_2_), channel_id=1, source_target_pairs={{0,8},{8,0},{16,24},{24,16},{1,9},{9,1},{17,25},{25,17},{2,10},{10... | collective-permute-start | bytes 1572872 | tf_op jit(solution)/shard_map/ppermute | solution.py:43
  269.8 36.4 %collective-permute-start.42 = (bf16[256,1536]{1,0:T(8,128)(2,1)S(1)}, bf16[256,1536]{1,0:T(8,128)(2,1)}, u32[]{:S(2)}, u32[]{:S(2)}) collective-permute-start(bf16[256,1536]{1,0:T(8,128)(2,1)S(1)} %pad_maximum_fusion.5.refs_4_), channel_id=1, source_target_pairs={{0,16},{8,24},{16,0},{24,8},{1,17},{9,25},{17,1},{25,9},{2,18},{10... | collective-permute-start | bytes 2359304 | tf_op jit(solution)/shard_map/ppermute | solution.py:43
  272.7 37.1 %collective-permute-start.45 = (bf16[256,512]{1,0:T(8,128)(2,1)S(1)}, bf16[256,512]{1,0:T(8,128)(2,1)}, u32[]{:S(2)}, u32[]{:S(2)}) collective-permute-start(bf16[256,512]{1,0:T(8,128)(2,1)S(1)} %copy-done.24), channel_id=1, source_target_pairs={{0,8},{8,0},{16,24},{24,16},{1,9},{9,1},{17,25},{25,17},{2,10},{10... | collective-permute-start | bytes 786440 | tf_op jit(solution)/shard_map/ppermute | solution.py:43
  272.8 33.3 %collective-permute-start.36 = (f32[2,1024]{1,0:T(2,128)S(1)}, f32[2,1024]{1,0:T(2,128)S(1)}, u32[]{:S(2)}, u32[]{:S(2)}) collective-permute-start(f32[2,1024]{1,0:T(2,128)S(1)} %pad_maximum_fusion.16), channel_id=1, source_target_pairs={{0,8},{8,0},{16,24},{24,16},{1,9},{9,1},{17,25},{25,17},{2,10},{10... | collective-permute-start | bytes 24584 | tf_op jit(solution)/shard_map/ppermute | solution.py:43
  276.3 38.8 %all-to-all-start.2 = ((bf16[4,64,1024]{2,1,0:T(8,128)(2,1)}), bf16[4,64,1024]{2,1,0:T(8,128)(2,1)S(1)}, u32[]{:S(2)}, u32[]{:S(2)}) async-start(bf16[4,64,1024]{2,1,0:T(8,128)(2,1)} %bitcast.54), calls=%async_computation.2 | async-start | bytes 1048576 | tf_op jit(solution)/shard_map/all_to_all | solution.py:148
  306.1 8.9 %collective-permute-start.47 = (bf16[256,1024]{1,0:T(8,128)(2,1)}, bf16[256,1024]{1,0:T(8,128)(2,1)}, u32[]{:S(2)}, u32[]{:S(2)}) collective-permute-start(bf16[256,1024]{1,0:T(8,128)(2,1)} %bitcast.50.refs_12_), channel_id=1, source_target_pairs={{0,8},{8,0},{16,24},{24,16},{1,9},{9,1},{17,25},{25,17},{2,10},{10... | collective-permute-start | bytes 1572872 | tf_op jit(solution)/shard_map/ppermute | solution.py:43
  306.8 7.6 %collective-permute-start.37 = (f32[2,1024]{1,0:T(2,128)S(1)}, f32[2,1024]{1,0:T(2,128)S(1)}, u32[]{:S(2)}, u32[]{:S(2)}) collective-permute-start(f32[2,1024]{1,0:T(2,128)S(1)} %fusion.63), channel_id=1, source_target_pairs={{0,16},{8,24},{16,0},{24,8},{1,17},{9,25},{17,1},{25,9},{2,18},{10... | collective-permute-start | bytes 24584 | tf_op jit(solution)/shard_map/ppermute | solution.py:43
  309.7 7.5 %collective-permute-start.43 = (bf16[256,1536]{1,0:T(8,128)(2,1)S(1)}, bf16[256,1536]{1,0:T(8,128)(2,1)S(1)}, u32[]{:S(2)}, u32[]{:S(2)}) collective-permute-start(bf16[256,1536]{1,0:T(8,128)(2,1)S(1)} %pad_maximum_fusion.5.refs_4_), channel_id=1, source_target_pairs={{0,8},{8,0},{16,24},{24,16},{1,9},{9,1},{17,25},{25,17},{2,10},{10... | collective-permute-start | bytes 2359304 | tf_op jit(solution)/shard_map/ppermute | solution.py:43
  309.9 7.4 %collective-permute-start.44 = (bf16[256,1536]{1,0:T(8,128)(2,1)}, bf16[256,1536]{1,0:T(8,128)(2,1)S(1)}, u32[]{:S(2)}, u32[]{:S(2)}) collective-permute-start(bf16[256,1536]{1,0:T(8,128)(2,1)} %collective-permute-done.42.refs_6_), channel_id=1, source_target_pairs={{0,8},{8,0},{16,24},{24,16},{1,9},{9,1},{17,25},{25,17},{2,10},{10... | collective-permute-start | bytes 2359304 | tf_op jit(solution)/shard_map/ppermute | solution.py:43
  312.9 28.8 %collective-permute-start.61 = (f32[3,256,256]{2,1,0:T(8,128)}, f32[3,256,256]{2,1,0:T(8,128)}, u32[]{:S(2)}, u32[]{:S(2)}) collective-permute-start(f32[3,256,256]{2,1,0:T(8,128)} %get-tuple-element.225), channel_id=1, source_target_pairs={{0,1},{1,0},{2,3},{3,2},{4,5},{5,4},{6,7},{7,6},{8,9},{9,8},{10,11... | collective-permute-start | bytes 2359304 | tf_op jit(solution)/shard_map/ppermute | solution.py:43
  314.3 38.8 %collective-permute-start.69 = (f32[3,256,256]{2,1,0:T(8,128)}, f32[3,256,256]{2,1,0:T(8,128)}, u32[]{:S(2)}, u32[]{:S(2)}) collective-permute-start(f32[3,256,256]{2,1,0:T(8,128)} %get-tuple-element.202.a_ref), channel_id=1, source_target_pairs={{0,1},{1,0},{2,3},{3,2},{4,5},{5,4},{6,7},{7,6},{8,9},{9,8},{10,11... | collective-permute-start | bytes 2359304 | tf_op jit(solution)/shard_map/ppermute | solution.py:43
  336.7 28.8 %collective-permute-start.60 = (f32[2,1024]{1,0:T(2,128)S(1)}, f32[2,1024]{1,0:T(2,128)S(1)}, u32[]{:S(2)}, u32[]{:S(2)}) collective-permute-start(f32[2,1024]{1,0:T(2,128)S(1)} %fusion.92), channel_id=1, source_target_pairs={{0,6},{2,0},{4,2},{6,4},{1,7},{3,1},{5,3},{7,5},{8,14},{10,8},{12,... | collective-permute-start | bytes 24584 | tf_op jit(solution)/shard_map/ppermute | solution.py:126
  340.3 26.7 %collective-permute-start.58 = (f32[2,1024]{1,0:T(2,128)S(1)}, f32[2,1024]{1,0:T(2,128)S(1)}, u32[]{:S(2)}, u32[]{:S(2)}) collective-permute-start(f32[2,1024]{1,0:T(2,128)S(1)} %fusion.92), channel_id=1, source_target_pairs={{0,4},{2,6},{4,0},{6,2},{1,5},{3,7},{5,1},{7,3},{8,12},{10,14},{12... | collective-permute-start | bytes 24584 | tf_op jit(solution)/shard_map/ppermute | solution.py:126
  340.3 27.3 %collective-permute-start.59 = (f32[2,1024]{1,0:T(2,128)S(1)}, f32[2,1024]{1,0:T(2,128)S(1)}, u32[]{:S(2)}, u32[]{:S(2)}) collective-permute-start(f32[2,1024]{1,0:T(2,128)S(1)} %fusion.92), channel_id=1, source_target_pairs={{0,2},{2,4},{4,6},{6,0},{1,3},{3,5},{5,7},{7,1},{8,10},{10,12},{12... | collective-permute-start | bytes 24584 | tf_op jit(solution)/shard_map/ppermute | solution.py:126
  341.8 22.2 %collective-permute-start.53 = (f32[64,1]{0,1:T(1,128)S(1)}, f32[64,1]{0,1:T(1,128)S(1)}, u32[]{:S(2)}, u32[]{:S(2)}) collective-permute-start(f32[64,1]{0,1:T(1,128)S(1)} %bitcast.210), channel_id=1, source_target_pairs={{0,1},{1,0},{2,3},{3,2},{4,5},{5,4},{6,7},{7,6},{8,9},{9,8},{10,11... | collective-permute-start | bytes 776 | tf_op jit(solution)/shard_map/ppermute | solution.py:43
  353.1 43.5 %collective-permute-start.62 = (bf16[784,256]{1,0:T(8,128)(2,1)}, bf16[784,256]{1,0:T(8,128)(2,1)S(1)}, u32[]{:S(2)}, u32[]{:S(2)}) collective-permute-start(bf16[784,256]{1,0:T(8,128)(2,1)} %polynomial.3), channel_id=1, source_target_pairs={{0,1},{1,0},{2,3},{3,2},{4,5},{5,4},{6,7},{7,6},{8,9},{9,8},{10,11... | collective-permute-start | bytes 1204232 | tf_op jit(solution)/shard_map/ppermute | solution.py:43
  364.0 34.7 %collective-permute-start.71 = (bf16[784,256]{1,0:T(8,128)(2,1)}, bf16[784,256]{1,0:T(8,128)(2,1)S(1)}, u32[]{:S(2)}, u32[]{:S(2)}) collective-permute-start(bf16[784,256]{1,0:T(8,128)(2,1)} %polynomial.4), channel_id=1, source_target_pairs={{0,16},{8,24},{16,0},{24,8},{1,17},{9,25},{17,1},{25,9},{2,18},{10... | collective-permute-start | bytes 1204232 | tf_op jit(solution)/shard_map/ppermute | solution.py:43
  369.9 10.5 %collective-permute-start.50 = (bf16[32,2048]{1,0:T(8,128)(2,1)S(1)}, bf16[32,2048]{1,0:T(8,128)(2,1)S(1)}, u32[]{:S(2)}, u32[]{:S(2)}) collective-permute-start(bf16[32,2048]{1,0:T(8,128)(2,1)S(1)} %pad_maximum_fusion.14), channel_id=1, source_target_pairs={{0,6},{2,0},{4,2},{6,4},{1,7},{3,1},{5,3},{7,5},{8,14},{10,8},{12,... | collective-permute-start | bytes 393224 | tf_op jit(solution)/shard_map/ppermute | solution.py:126
  372.6 8.2 %collective-permute-start.51 = (bf16[32,2048]{1,0:T(8,128)(2,1)S(1)}, bf16[32,2048]{1,0:T(8,128)(2,1)S(1)}, u32[]{:S(2)}, u32[]{:S(2)}) collective-permute-start(bf16[32,2048]{1,0:T(8,128)(2,1)S(1)} %pad_maximum_fusion.14), channel_id=1, source_target_pairs={{0,2},{2,4},{4,6},{6,0},{1,3},{3,5},{5,7},{7,1},{8,10},{10,12},{12... | collective-permute-start | bytes 393224 | tf_op jit(solution)/shard_map/ppermute | solution.py:126
  372.6 17.9 %collective-permute-start.52 = (bf16[32,2048]{1,0:T(8,128)(2,1)S(1)}, bf16[32,2048]{1,0:T(8,128)(2,1)S(1)}, u32[]{:S(2)}, u32[]{:S(2)}) collective-permute-start(bf16[32,2048]{1,0:T(8,128)(2,1)S(1)} %pad_maximum_fusion.14), channel_id=1, source_target_pairs={{0,4},{2,6},{4,0},{6,2},{1,5},{3,7},{5,1},{7,3},{8,12},{10,14},{12... | collective-permute-start | bytes 393224 | tf_op jit(solution)/shard_map/ppermute | solution.py:126
  380.4 11.1 %collective-permute-start.55 = (bf16[32,2048]{1,0:T(8,128)(2,1)S(1)}, bf16[32,2048]{1,0:T(8,128)(2,1)S(1)}, u32[]{:S(2)}, u32[]{:S(2)}) collective-permute-start(bf16[32,2048]{1,0:T(8,128)(2,1)S(1)} %pad_maximum_fusion.15), channel_id=1, source_target_pairs={{0,6},{2,0},{4,2},{6,4},{1,7},{3,1},{5,3},{7,5},{8,14},{10,8},{12,... | collective-permute-start | bytes 393224 | tf_op jit(solution)/shard_map/ppermute | solution.py:126
  380.9 10.7 %collective-permute-start.56 = (bf16[32,2048]{1,0:T(8,128)(2,1)S(1)}, bf16[32,2048]{1,0:T(8,128)(2,1)S(1)}, u32[]{:S(2)}, u32[]{:S(2)}) collective-permute-start(bf16[32,2048]{1,0:T(8,128)(2,1)S(1)} %pad_maximum_fusion.15), channel_id=1, source_target_pairs={{0,2},{2,4},{4,6},{6,0},{1,3},{3,5},{5,7},{7,1},{8,10},{10,12},{12... | collective-permute-start | bytes 393224 | tf_op jit(solution)/shard_map/ppermute | solution.py:126
  391.6 31.0 %collective-permute-start.70 = (bf16[784,256]{1,0:T(8,128)(2,1)S(1)}, bf16[784,256]{1,0:T(8,128)(2,1)S(1)}, u32[]{:S(2)}, u32[]{:S(2)}) collective-permute-start(bf16[784,256]{1,0:T(8,128)(2,1)S(1)} %copy-done.33), channel_id=1, source_target_pairs={{0,8},{8,0},{16,24},{24,16},{1,9},{9,1},{17,25},{25,17},{2,10},{10... | collective-permute-start | bytes 1204232 | tf_op jit(solution)/shard_map/ppermute | solution.py:43
  391.6 20.2 %collective-permute-start.73 = (f32[3,256,256]{2,1,0:T(8,128)S(1)}, f32[3,256,256]{2,1,0:T(8,128)S(1)}, u32[]{:S(2)}, u32[]{:S(2)}) collective-permute-start(f32[3,256,256]{2,1,0:T(8,128)S(1)} %copy-done.42), channel_id=1, source_target_pairs={{0,1},{1,0},{2,3},{3,2},{4,5},{5,4},{6,7},{7,6},{8,9},{9,8},{10,11... | collective-permute-start | bytes 2359304 | tf_op jit(solution)/shard_map/ppermute | solution.py:43
  396.7 27.6 %collective-permute-start.64 = (bf16[784,256]{1,0:T(8,128)(2,1)S(1)}, bf16[784,256]{1,0:T(8,128)(2,1)S(1)}, u32[]{:S(2)}, u32[]{:S(2)}) collective-permute-start(bf16[784,256]{1,0:T(8,128)(2,1)S(1)} %get-tuple-element.237), channel_id=1, source_target_pairs={{0,16},{8,24},{16,0},{24,8},{1,17},{9,25},{17,1},{25,9},{2,18},{10... | collective-permute-start | bytes 1204232 | tf_op jit(solution)/shard_map/ppermute | solution.py:43
  398.7 26.7 %collective-permute-start.63 = (bf16[784,256]{1,0:T(8,128)(2,1)S(1)}, bf16[784,256]{1,0:T(8,128)(2,1)S(1)}, u32[]{:S(2)}, u32[]{:S(2)}) collective-permute-start(bf16[784,256]{1,0:T(8,128)(2,1)S(1)} %get-tuple-element.237), channel_id=1, source_target_pairs={{0,8},{8,0},{16,24},{24,16},{1,9},{9,1},{17,25},{25,17},{2,10},{10... | collective-permute-start | bytes 1204232 | tf_op jit(solution)/shard_map/ppermute | solution.py:43
  398.7 27.2 %collective-permute-start.67 = (bf16[784,256]{1,0:T(8,128)(2,1)S(1)}, bf16[784,256]{1,0:T(8,128)(2,1)S(1)}, u32[]{:S(2)}, u32[]{:S(2)}) collective-permute-start(bf16[784,256]{1,0:T(8,128)(2,1)S(1)} %get-tuple-element.236), channel_id=1, source_target_pairs={{0,16},{8,24},{16,0},{24,8},{1,17},{9,25},{17,1},{25,9},{2,18},{10... | collective-permute-start | bytes 1204232 | tf_op jit(solution)/shard_map/ppermute | solution.py:43
  411.8 15.0 %collective-permute-start.72 = (bf16[784,256]{1,0:T(8,128)(2,1)S(1)}, bf16[784,256]{1,0:T(8,128)(2,1)S(1)}, u32[]{:S(2)}, u32[]{:S(2)}) collective-permute-start(bf16[784,256]{1,0:T(8,128)(2,1)S(1)} %collective-permute-done.71), channel_id=1, source_target_pairs={{0,8},{8,0},{16,24},{24,16},{1,9},{9,1},{17,25},{25,17},{2,10},{10... | collective-permute-start | bytes 1204232 | tf_op jit(solution)/shard_map/ppermute | solution.py:43
  422.6 11.2 %collective-permute-start.75 = (bf16[784,256]{1,0:T(8,128)(2,1)}, bf16[784,256]{1,0:T(8,128)(2,1)S(1)}, u32[]{:S(2)}, u32[]{:S(2)}) collective-permute-start(bf16[784,256]{1,0:T(8,128)(2,1)} %polynomial.5), channel_id=1, source_target_pairs={{0,16},{8,24},{16,0},{24,8},{1,17},{9,25},{17,1},{25,9},{2,18},{10... | collective-permute-start | bytes 1204232 | tf_op jit(solution)/shard_map/ppermute | solution.py:43
  424.3 10.9 %collective-permute-start.65 = (bf16[784,256]{1,0:T(8,128)(2,1)S(1)}, bf16[784,256]{1,0:T(8,128)(2,1)S(1)}, u32[]{:S(2)}, u32[]{:S(2)}) collective-permute-start(bf16[784,256]{1,0:T(8,128)(2,1)S(1)} %collective-permute-done.64), channel_id=1, source_target_pairs={{0,8},{8,0},{16,24},{24,16},{1,9},{9,1},{17,25},{25,17},{2,10},{10... | collective-permute-start | bytes 1204232 | tf_op jit(solution)/shard_map/ppermute | solution.py:43
  425.4 20.1 %collective-permute-start.66 = (bf16[784,256]{1,0:T(8,128)(2,1)S(1)}, bf16[784,256]{1,0:T(8,128)(2,1)S(1)}, u32[]{:S(2)}, u32[]{:S(2)}) collective-permute-start(bf16[784,256]{1,0:T(8,128)(2,1)S(1)} %get-tuple-element.236), channel_id=1, source_target_pairs={{0,8},{8,0},{16,24},{24,16},{1,9},{9,1},{17,25},{25,17},{2,10},{10... | collective-permute-start | bytes 1204232 | tf_op jit(solution)/shard_map/ppermute | solution.py:43
  425.9 19.6 %collective-permute-start.68 = (bf16[784,256]{1,0:T(8,128)(2,1)S(1)}, bf16[784,256]{1,0:T(8,128)(2,1)S(1)}, u32[]{:S(2)}, u32[]{:S(2)}) collective-permute-start(bf16[784,256]{1,0:T(8,128)(2,1)S(1)} %collective-permute-done.67), channel_id=1, source_target_pairs={{0,8},{8,0},{16,24},{24,16},{1,9},{9,1},{17,25},{25,17},{2,10},{10... | collective-permute-start | bytes 1204232 | tf_op jit(solution)/shard_map/ppermute | solution.py:43
  426.8 37.3 %collective-permute-start.74 = (bf16[784,256]{1,0:T(8,128)(2,1)S(1)}, bf16[784,256]{1,0:T(8,128)(2,1)S(1)}, u32[]{:S(2)}, u32[]{:S(2)}) collective-permute-start(bf16[784,256]{1,0:T(8,128)(2,1)S(1)} %copy-done.34), channel_id=1, source_target_pairs={{0,8},{8,0},{16,24},{24,16},{1,9},{9,1},{17,25},{25,17},{2,10},{10... | collective-permute-start | bytes 1204232 | tf_op jit(solution)/shard_map/ppermute | solution.py:43
  433.8 30.2 %collective-permute-start.76 = (bf16[784,256]{1,0:T(8,128)(2,1)S(1)}, bf16[784,256]{1,0:T(8,128)(2,1)S(1)}, u32[]{:S(2)}, u32[]{:S(2)}) collective-permute-start(bf16[784,256]{1,0:T(8,128)(2,1)S(1)} %collective-permute-done.75), channel_id=1, source_target_pairs={{0,8},{8,0},{16,24},{24,16},{1,9},{9,1},{17,25},{25,17},{2,10},{10... | collective-permute-start | bytes 1204232 | tf_op jit(solution)/shard_map/ppermute | solution.py:43
  (76 other events, 697.7 us)
